TPU v7x, 32 devices: a whole 2x2x4 slice. The times are simulated.
32 devices in a mesh: section: 2 (over y), dp: 16 (over z, x, core).
Axes of the slice: x: 2, y: 2, z: 4, core: 2. Of those that a mesh axis runs over, the one named last changes fastest.
Arguments:
- tokens: bfloat16 [2, 16, 512, 384], P(None, 'dp'), may hold values from -6 to 6
- cotangent: bfloat16 [2, 16, 512, 384], P(None, 'dp'), may hold values from -6 to 6
- views: int32 [2, 16], P(None, 'dp'), may hold values from 2 to 8, as said below
- attn_gain: bfloat16 [2, 384], P('section'), may hold values from 0.099609375 to 1.8984375
- attn_shift: bfloat16 [2, 384], P('section'), may hold values from -1.75 to 1.75
- qkv_weight: bfloat16 [2, 384, 1152], P('section'), may hold values from -0.3125 to 0.3125
- query_bias: bfloat16 [2, 384], P('section'), may hold values from -3 to 3
- value_bias: bfloat16 [2, 384], P('section'), may hold values from -3 to 3
- out_weight: bfloat16 [2, 384, 384], P('section'), may hold values from -1.25 to 1.25
- out_bias: bfloat16 [2, 384], P('section'), may hold values from -1.75 to 1.75
- mlp_gain: bfloat16 [2, 384], P('section'), may hold values from 0.099609375 to 1.8984375
- mlp_shift: bfloat16 [2, 384], P('section'), may hold values from -1.75 to 1.75
- up_weight: bfloat16 [2, 384, 1536], P('section'), may hold values from -0.3125 to 0.3125
- up_bias: bfloat16 [2, 1536], P('section'), may hold values from -3 to 3
- down_weight: bfloat16 [2, 1536, 384], P('section'), may hold values from -0.15625 to 0.15625
- down_bias: bfloat16 [2, 384], P('section'), may hold values from -1.75 to 1.75
Outputs:
- layer_out: bfloat16 [2, 2, 16, 512, 384], P('section', None, 'dp')
- input_grads: bfloat16 [2, 2, 16, 512, 384], P('section', None, 'dp')
- grad_attn_gain: float32 [2, 384], P('section')
- grad_attn_shift: float32 [2, 384], P('section')
- grad_qkv_weight: float32 [2, 384, 1152], P('section')
- grad_query_bias: float32 [2, 384], P('section')
- grad_value_bias: float32 [2, 384], P('section')
- grad_out_weight: float32 [2, 384, 384], P('section')
- grad_out_bias: float32 [2, 384], P('section')
- grad_mlp_gain: float32 [2, 384], P('section')
- grad_mlp_shift: float32 [2, 384], P('section')
- grad_up_weight: float32 [2, 384, 1536], P('section')
- grad_up_bias: float32 [2, 1536], P('section')
- grad_down_weight: float32 [2, 1536, 384], P('section')
- grad_down_bias: float32 [2, 384], P('section')
Inputs may be any that keep to these rules, and one draw needn't show every extreme that they name: In every micro-batch some scene has 8 views.
All inputs are finite; a program needn't handle non-finite values.
Results may differ from a plain program's by a relative error of at most 0.014.
Values may be sent and summed in bfloat16 or wider, within the bound.
No kernel may reach another device: no remote copies, remote signals or barrier semaphores. Data moves between devices by JAX's collectives and lax.ppermute only.
A program may use at most 192 MiB of HBM per device.

v0:
```python
import jax
import jax.numpy as jnp
from jax import lax
from jax.experimental import pallas as pl
from jax.experimental.pallas import tpu as pltpu
from jax.sharding import PartitionSpec as P

HEADS = 6
HEAD = 64
PATCHES = 64
EPSILON = 1e-06
MASKED = -1e30
LANES = 128
CUTS = 16
F32 = jnp.float32
BF16 = jnp.bfloat16
VMEM_LIMIT = 28 * 2**20


def dot(a, b):
    return lax.dot_general(a, b, (((1,), (0,)), ((), ())), preferred_element_type=F32)


def dot_nt(a, b):
    return lax.dot_general(a, b, (((1,), (1,)), ((), ())), preferred_element_type=F32)


def unit_rows(values):
    center = values - jnp.mean(values, -1, keepdims=True)
    spread = jnp.mean(center * center, -1, keepdims=True)
    scale = lax.rsqrt(spread + EPSILON)
    return center * scale, scale


def row(vec, name):
    return vec[name][...].astype(F32)


LINES = ("ag", "as", "qb", "vb", "ob", "mg", "ms", "db", "ub")
CHUNK = 256


def padded(rows, odd):
    zero = jnp.zeros_like(rows)
    return jnp.concatenate([zero, rows] if odd else [rows, zero], 0)


def forward(x_ref, y_ref, count, vec, w, r, wait, done):
    slots, width = x_ref.shape
    ub = row(vec, "ub")
    ff = ub.shape[1]

    unit, _ = unit_rows(x_ref[...].astype(F32))
    a = (unit * row(vec, "ag") + row(vec, "as")).astype(BF16)
    r["a"][...] = a
    wait("qkv")
    q = dot(a, w["qkv"][:, :width]) + row(vec, "qb")
    r["qt"][...] = (q * HEAD**-0.5).astype(BF16).T.reshape(HEADS, HEAD, slots)
    k = dot(a, w["qkv"][:, width : 2 * width]).astype(BF16)
    r["kt"][...] = k.T.reshape(HEADS, HEAD, slots)
    v = (dot(a, w["qkv"][:, 2 * width :]) + row(vec, "vb")).astype(BF16)
    r["vt"][...] = v.T.reshape(HEADS, HEAD, slots)
    for p in range(HEADS // 2):
        r["k"][p] = k[:, p * 2 * HEAD : (p + 1) * 2 * HEAD]
        r["v"][p] = v[:, p * 2 * HEAD : (p + 1) * 2 * HEAD]
    for n in ("a", "qt", "k", "kt", "v"):
        done(n)
    groups = slots // PATCHES
    shift = [jnp.where(g < count, 0.0, MASKED).astype(F32) for g in range(groups)]

    last = HEADS - 1

    def scores(h, odd):
        r["s"][odd] = dot(r["k"][h // 2], padded(r["qt"][h], odd))

    def soften(h, odd):
        s_ref = r["s"].at[odd]
        for c in range(slots // LANES):
            cols = slice(c * LANES, (c + 1) * LANES)
            peak = s_ref[0:PATCHES, cols]
            for g in range(1, groups):
                block = s_ref[g * PATCHES : (g + 1) * PATCHES, cols]
                peak = jnp.maximum(peak, block if g < 2 else block + shift[g])
            peak = jnp.max(peak, 0, keepdims=True)
            acc = jnp.zeros((PATCHES, LANES), F32)
            for g in range(groups):
                block = s_ref[g * PATCHES : (g + 1) * PATCHES, cols]
                e = jnp.exp(block - (peak - shift[g]))
                acc = acc + e
                r["e"][h, g * PATCHES : (g + 1) * PATCHES, cols] = e.astype(BF16)
            r["inv"][h, :, cols] = 1.0 / jnp.sum(acc, 0, keepdims=True)

    def mix(h):
        r["ot"][h] = dot(r["vt"][h], r["e"][h]) * r["inv"][h]

    def pair(i):
        h = 2 * i
        scores(h + 1, 1)
        soften(h, 0)
        if h:
            mix(h - 1)
        if h + 2 < HEADS:
            scores(h + 2, 0)
        soften(h + 1, 1)
        mix(h)

    scores(0, 0)
    for i in range(HEADS // 2):
        pair(i)
    mix(last)
    for n in ("e", "inv", "ot"):
        done(n)
    wait("out")
    o = r["ot"][...].reshape(width, slots).astype(BF16).T
    hidden = x_ref[...].astype(F32) + dot(o, w["out"][...]) + row(vec, "ob")
    r["h"][...] = hidden
    done("h")
    unit, _ = unit_rows(hidden)
    c = (unit * row(vec, "mg") + row(vec, "ms")).astype(BF16)
    r["c"][...] = c
    done("c")
    wait("up")
    for f in range(0, ff, CHUNK):
        cols = slice(f, f + CHUNK)
        u = dot(c, w["up"][:, cols]) + ub[:, cols]
        phi = 0.5 + 0.5 * lax.erf(u * 0.5**0.5)
        density = jnp.exp(-0.5 * u * u) * 0.3989422804014327
        r["z"][:, cols] = (u * phi).astype(BF16)
        r["gp"][:, cols] = (phi + u * density).astype(BF16)
    done("z")
    done("gp")
    wait("down")
    y_ref[...] = (r["h"][...] + dot(r["z"][...], w["down"][...]) + row(vec, "db")).astype(BF16)


def nothing(name):
    pass


def sizes(slots, width, ff):
    turned = ((HEADS, HEAD, slots), BF16)
    pairs = ((HEADS // 2, slots, 2 * HEAD), BF16)
    return dict(
        a=((slots, width), BF16),
        qt=turned,
        k=pairs,
        kt=turned,
        v=pairs,
        vt=turned,
        s=((2, slots, slots), F32),
        e=((HEADS, slots, slots), BF16),
        inv=((HEADS, 1, slots), F32),
        ot=((HEADS, HEAD, slots), F32),
        h=((slots, width), F32),
        c=((slots, width), BF16),
        z=((slots, ff), BF16),
        gp=((slots, ff), BF16),
    )


def norm_back(grad, gain, unit, scale):
    t = grad * gain
    inner = jnp.mean(t, -1, keepdims=True)
    along = jnp.mean(t * unit, -1, keepdims=True)
    return scale * (t - inner - unit * along)


M_GAIN_G, M_SHIFT_G, A_GAIN_G, A_SHIFT_G = range(4)


def backward_mlp(grad_ref, vec, w, r, wait, done):
    slots, width = grad_ref.shape
    ff = r["du"].shape[1]
    wait("down")
    wait("gp")
    low = grad_ref[...]
    for f in range(0, ff, CHUNK):
        cols = slice(f, f + CHUNK)
        dz = dot_nt(low, w["down"][cols, :])
        r["du"][:, cols] = (dz * r["gp"][:, cols].astype(F32)).astype(BF16)
    done("du")
    wait("up")
    dc = dot_nt(r["du"][...], w["up"][...])
    wait("h")
    unit, scale = unit_rows(r["h"][...])
    r["small"][M_GAIN_G : M_GAIN_G + 1, :] = jnp.sum(dc * unit, 0, keepdims=True)
    r["small"][M_SHIFT_G : M_SHIFT_G + 1, :] = jnp.sum(dc, 0, keepdims=True)
    dh = low.astype(F32) + norm_back(dc, row(vec, "mg"), unit, scale)
    r["dh"][...] = dh
    r["dp"][...] = dh.astype(BF16)
    done("dp")


def backward_attention(x_ref, g_ref, vec, w, r, wait, done):
    slots, width = x_ref.shape
    wait("out")
    dot_t = dot_nt(w["out"][...], r["dp"][...])
    r["dot"][...] = dot_t.reshape(HEADS, HEAD, slots)

    last = HEADS - 1
    for n in ("inv", "ot", "v", "e", "kt", "qt"):
        wait(n)

    def spread(h, odd):
        g = (r["dot"][h] * r["inv"][h]).astype(BF16)
        r["g"][odd] = g
        r["center"][odd] = jnp.sum(g.astype(F32) * r["ot"][h], 0, keepdims=True)
        r["s"][odd] = dot(r["v"][h // 2], padded(g, odd))

    def weigh(h, odd):
        s_ref = r["s"].at[odd]
        for c in range(slots // LANES):
            cols = slice(c * LANES, (c + 1) * LANES)
            center = r["center"][odd, :, cols]
            for b in range(0, slots, PATCHES):
                block = s_ref[b : b + PATCHES, cols] - center
                r["ds"][odd, b : b + PATCHES, cols] = (
                    block * r["e"][h, b : b + PATCHES, cols].astype(F32)
                ).astype(BF16)

    def gather(h, odd):
        ds = r["ds"][odd]
        r["dqkv"][0, h] = (dot(r["kt"][h], ds) * HEAD**-0.5).astype(BF16)
        r["dqkv"][1, h] = dot_nt(r["qt"][h], ds).astype(BF16)

    def gather_v(h, odd):
        r["dqkv"][2, h] = dot_nt(r["g"][odd], r["e"][h]).astype(BF16)

    def pair(i):
        h = 2 * i
        gather_v(h, 0)
        spread(h + 1, 1)
        weigh(h, 0)
        if h:
            gather(h - 1, 1)
        gather_v(h + 1, 1)
        if h + 2 < HEADS:
            spread(h + 2, 0)
        weigh(h + 1, 1)
        gather(h, 0)

    spread(0, 0)
    for i in range(HEADS // 2):
        pair(i)
    gather(last, 1)
    done("dqkv")

    wait("qkv")
    da = dot(w["qkv"][...], r["dqkv"][...].reshape(3 * width, slots)).T
    unit, scale = unit_rows(x_ref[...].astype(F32))
    r["small"][A_GAIN_G : A_GAIN_G + 1, :] = jnp.sum(da * unit, 0, keepdims=True)
    r["small"][A_SHIFT_G : A_SHIFT_G + 1, :] = jnp.sum(da, 0, keepdims=True)
    done("small")
    g_ref[...] = (r["dh"][...] + norm_back(da, row(vec, "ag"), unit, scale)).astype(BF16)


def back_sizes(slots, width, ff):
    return dict(
        du=((slots, ff), BF16),
        dh=((slots, width), F32),
        dp=((slots, width), BF16),
        dot=((HEADS, HEAD, slots), F32),
        ds=((2, slots, slots), BF16),
        g=((2, HEAD, slots), BF16),
        center=((2, 1, slots), F32),
        dqkv=((3, HEADS, HEAD, slots), BF16),
        small=((8, width), F32),
    )


WEIGHTS = ("qkv", "out", "up", "down")
SAVED = ("a", "qt", "kt", "v", "e", "inv", "ot", "h", "c", "z", "gp")
TERMS = ("du", "dp", "dqkv", "small", "dm")
STEPS = 3


def run(body, ins, outs, scratch, aliases=None, us=1):
    space = {"s": pltpu.SMEM, "v": pltpu.VMEM, "a": pl.ANY}
    return pl.pallas_call(
        body,
        out_shape=[jax.ShapeDtypeStruct(s, t) for s, t, _ in outs],
        in_specs=[pl.BlockSpec(memory_space=space[k]) for _, k in ins],
        out_specs=[pl.BlockSpec(memory_space=space[k]) for _, _, k in outs],
        scratch_shapes=scratch,
        input_output_aliases=aliases or {},
        compiler_params=pltpu.CompilerParams(vmem_limit_bytes=VMEM_LIMIT),
        cost_estimate=pl.CostEstimate(
            flops=us * 10**9, bytes_accessed=us * 2 * 10**6, transcendentals=0
        ),
    )(*[x for x, _ in ins])


def weight_sizes(width, ff):
    return dict(qkv=(width, 3 * width), out=(width, width), up=(width, ff), down=(ff, width))


def all_sizes(dims):
    slots, width, ff = dims
    return {**sizes(*dims), **back_sizes(*dims), "dm": ((slots, width), BF16)}


class Moves:
    def __init__(self, sem):
        self.sem = sem
        self.used = 0
        self.made = {}

    def make(self, name, src, dst):
        self.made[name] = pltpu.make_async_copy(src, dst, self.sem.at[self.used])
        self.used += 1
        return self.made[name]

    def start(self, name, src, dst):
        self.make(name, src, dst).start()

    def wait(self, name):
        if name in self.made:
            self.made.pop(name).wait()

    def finish(self):
        for name in list(self.made):
            self.wait(name)


def blank(dims):
    slots, width, _ = dims
    shapes = all_sizes(dims)
    outs = [((slots, width), BF16, "a")] + [((2, slots, width), BF16, "a")] * 2
    outs += [((2, *shapes[n][0]), shapes[n][1], "a") for n in SAVED + TERMS]

    def body(*refs):
        pass

    got = run(body, [], outs, [])
    return got[0], tuple(got[1:])


def cell(step, views, lines, tokens, cotangent, recv, weights, bufs, dims):
    slots, width, ff = dims
    shapes = all_sizes(dims)
    wshapes = weight_sizes(width, ff)
    names = [n for n in shapes if n != "dm"]
    n_in = 2 + len(lines) + 3 + 4
    loads = ("gp", "h", "inv", "ot", "v", "e", "kt", "qt")

    def body(*refs):
        step_ref, views_ref = refs[:2]
        vec = dict(zip(LINES, refs[2 : 2 + len(lines)]))
        tokens_hbm, cot_hbm, recv_hbm = refs[2 + len(lines) : 5 + len(lines)]
        w_hbm = dict(zip(WEIGHTS, refs[5 + len(lines) : n_in]))
        rest = refs[n_in + len(bufs) :]
        send_hbm, outs_hbm, grads_hbm = rest[:3]
        kept = dict(zip(SAVED + TERMS, rest[3:]))
        rest = rest[3 + len(SAVED + TERMS) :]
        w = dict(zip(WEIGHTS, rest[:4]))
        r = dict(zip(names, rest[4 : 4 + len(names)]))
        x, dm, y, sem = rest[4 + len(names) :]
        moves = Moves(sem)
        t = step_ref[0]
        lead = lax.axis_index("section") == 0
        run_f = jnp.where(lead, t < 2, t > 0)
        run_b = jnp.where(lead, t == 2, t > 0)
        slot = jnp.where(lead, t % 2, jnp.maximum(t - 1, 0))
        only_b = jnp.logical_and(lead, run_b)
        not_lead = jnp.logical_not(lead)
        token_copy = moves.make("x", tokens_hbm.at[slot, 0], x)
        recv_copy = pltpu.make_async_copy(recv_hbm, x, token_copy_sem(moves, "x"))
        cot_copy = moves.make("dm", cot_hbm.at[slot, 0], dm)
        grad_copy = pltpu.make_async_copy(recv_hbm, dm, token_copy_sem(moves, "dm"))
        w_copy = {n: moves.make("w " + n, w_hbm[n].at[0], w[n]) for n in WEIGHTS}
        l_copy = {n: moves.make("l " + n, kept[n].at[slot], r[n]) for n in loads}
        s_copy = {n: moves.make("s " + n, r[n], kept[n].at[slot]) for n in SAVED}
        b_copy = {n: moves.make("b " + n, r[n], kept[n].at[slot]) for n in TERMS[:4]}
        b_copy["dm"] = moves.make("b dm", dm, kept["dm"].at[slot])
        y_copy = moves.make("y", y, outs_hbm.at[slot])
        g_copy = moves.make("g", x, grads_hbm.at[slot])
        y_send = moves.make("ys", y, send_hbm)
        g_send = moves.make("gs", x, send_hbm)

        @pl.when(run_f)
        def _():
            @pl.when(lead)
            def _():
                token_copy.start()

            @pl.when(not_lead)
            def _():
                recv_copy.start()

            for n in WEIGHTS:
                w_copy[n].start()

            @pl.when(not_lead)
            def _():
                cot_copy.start()

            token_copy.wait()
            forward(
                x, y, views_ref[slot, 0], vec, w, r,
                lambda n: w_copy[n].wait(), lambda n: s_copy[n].start() if n in s_copy else None,
            )
            y_copy.start()

            @pl.when(lead)
            def _():
                y_send.start()

            @pl.when(not_lead)
            def _():
                cot_copy.wait()

        @pl.when(only_b)
        def _():
            grad_copy.start()
            for n in ("down", "gp", "up", "h", "out", "inv", "ot", "v", "e", "kt", "qt", "qkv"):
                (w_copy if n in w_copy else l_copy)[n].start()
            token_copy.start()
            grad_copy.wait()
            for n in ("down", "gp", "up", "h"):
                (w_copy if n in w_copy else l_copy)[n].wait()

        @pl.when(run_b)
        def _():
            b_copy["dm"].start()
            backward_mlp(dm, vec, w, r, nothing, lambda n: b_copy[n].start())

            @pl.when(only_b)
            def _():
                for n in ("out", "inv", "ot", "v", "e", "kt", "qt", "qkv"):
                    (w_copy if n in w_copy else l_copy)[n].wait()
                token_copy.wait()

            backward_attention(x, x, vec, w, r, nothing, lambda n: b_copy[n].start())
            g_copy.start()

            @pl.when(not_lead)
            def _():
                g_send.start()

        @pl.when(run_f)
        def _():
            for n in SAVED:
                s_copy[n].wait()
            y_copy.wait()

            @pl.when(lead)
            def _():
                y_send.wait()

        @pl.when(run_b)
        def _():
            for n in TERMS:
                b_copy[n].wait()
            g_copy.wait()

            @pl.when(not_lead)
            def _():
                g_send.wait()

    ins = [(step, "s"), (views, "s")] + [(v, "v") for v in lines]
    ins += [(x, "a") for x in (tokens, cotangent, recv, *weights, *bufs)]
    outs = [((slots, width), BF16, "a")] + [(b.shape, b.dtype, "a") for b in bufs]
    scratch = [pltpu.VMEM(wshapes[n], BF16) for n in WEIGHTS]
    scratch += [pltpu.VMEM(*shapes[n]) for n in names]
    scratch += [pltpu.VMEM((slots, width), BF16)] * 3 + [pltpu.SemaphoreType.DMA((40,))]
    got = run(body, ins, outs, scratch, {n_in + i: 1 + i for i in range(len(bufs))})
    return got[0], tuple(got[1:])


def token_copy_sem(moves, name):
    return moves.sem.at[list(moves.made).index(name)]


def scatter_blocks(sem, me, blocks, keep_hbm, send_hbm):
    for p in range(CUTS):
        place = jnp.bitwise_xor(p, me)

        @pl.when(jnp.bitwise_and(place, 1) == 0)
        def _():
            pltpu.make_async_copy(blocks.at[p], keep_hbm.at[place // 2], sem.at[p]).start()

        @pl.when(jnp.bitwise_and(place, 1) == 1)
        def _():
            pltpu.make_async_copy(blocks.at[p], send_hbm.at[place // 2], sem.at[p]).start()

    for p in range(CUTS):
        pltpu.make_async_copy(blocks.at[p], keep_hbm.at[0], sem.at[p]).wait()


def own_place():
    return lax.axis_index("dp") if lax.axis_size("dp") == CUTS else 0


def down_grads(z, dm, recv, dims):
    slots, width, ff = dims
    deep = width // 4

    def body(z_hbm, dm_hbm, recv_hbm, keep, send, sums, z_ref, m, blocks, sem, sem2):
        moves = Moves(sem)
        lead = lax.axis_index("section") == 0
        moves.start("m0", dm_hbm.at[0], m.at[0])
        first = moves.make("m1", dm_hbm.at[1], m.at[1])
        second = pltpu.make_async_copy(recv_hbm, m.at[1], sem.at[1])

        @pl.when(lead)
        def _():
            second.start()

        @pl.when(jnp.logical_not(lead))
        def _():
            first.start()

        for i in (0, 1):
            moves.start("z%d" % i, z_hbm.at[i], z_ref.at[i])
        moves.wait("m0")
        moves.wait("m1")
        ones = jnp.ones((16, slots), BF16)
        sums[...] = (dot(ones, m[0]) + dot(ones, m[1]))[:8]
        turned = [m[i].T for i in (0, 1)]
        moves.finish()
        for j in range(4):
            cols = slice(j * width, (j + 1) * width)
            part = dot(turned[0], z_ref[0, :, cols]) + dot(turned[1], z_ref[1, :, cols])
            blocks[4 * j : 4 * j + 4] = part.astype(BF16).reshape(4, deep, width)
        scatter_blocks(sem2, own_place(), blocks, keep, send)

    half = ((CUTS // 2, deep, width), BF16, "a")
    scratch = [
        pltpu.VMEM((2, slots, ff), BF16),
        pltpu.VMEM((2, slots, width), BF16),
        pltpu.VMEM((CUTS, deep, width), BF16),
        pltpu.SemaphoreType.DMA((4,)),
        pltpu.SemaphoreType.DMA((CUTS,)),
    ]
    ins = [(z, "a"), (dm, "a"), (recv, "a")]
    return run(body, ins, [half, half, ((8, width), F32, "v")], scratch, us=4)


def up_grads(lines, recv, weights, kept, dims):
    slots, width, ff = dims
    deep = width // 4
    shapes = all_sizes(dims)
    halves = (slice(0, slots), slice(slots, 2 * slots))
    names = ("gp", "h", "du", "dp", "dh", "small", "dm")
    given = ("gp", "h", "c", "du", "dp", "small")
    n_in = len(lines) + 3 + len(given)

    def body(*refs):
        vec = dict(zip(LINES, refs[: len(lines)]))
        recv_hbm, up_hbm, down_hbm = refs[len(lines) : len(lines) + 3]
        hbm = dict(zip(given, refs[len(lines) + 3 : n_in]))
        keep, send, sums, dp_hbm, small_hbm, dh_hbm = refs[n_in : n_in + 6]
        rest = refs[n_in + 6 :]
        w = {"up": rest[0], "down": rest[1]}
        r = dict(zip(names, rest[2 : 2 + len(names)]))
        c, d, blocks, sem, sem2 = rest[2 + len(names) :]
        moves = Moves(sem)
        lead = lax.axis_index("section") == 0
        for i, h in enumerate(halves):
            moves.start("c%d" % i, hbm["c"].at[i], c.at[h])
        moves.start("d0", hbm["du"].at[0], d.at[0])
        own = moves.make("d1", hbm["du"].at[1], d.at[1])

        @pl.when(jnp.logical_not(lead))
        def _():
            own.start()
            own.wait()

        @pl.when(lead)
        def _():
            inner = Moves(sem.at[pl.ds(4, 12)])
            inner.start("dm", recv_hbm, r["dm"])
            inner.start("down", down_hbm.at[0], w["down"])
            inner.start("gp", hbm["gp"].at[1], r["gp"])
            inner.start("up", up_hbm.at[0], w["up"])
            inner.start("h", hbm["h"].at[1], r["h"])
            inner.wait("dm")
            out = {"dp": dp_hbm.at[1]}

            def done(n):
                if n in out:
                    inner.start("save " + n, r[n], out[n])

            r["du"] = d.at[1]
            backward_mlp(r["dm"], vec, w, r, inner.wait, done)
            inner.start("save small", r["small"], small_hbm.at[1])
            inner.start("save dh", r["dh"], dh_hbm)
            inner.finish()

        for n in ("c0", "c1", "d0"):
            moves.wait(n)
        ones = jnp.ones((16, slots), BF16)
        turned = [c[h, :].T for h in halves]
        for j in range(4):
            cols = slice(j * width, (j + 1) * width)
            parts = [d[i, :, cols] for i in (0, 1)]
            sums[j] = (dot(ones, parts[0]) + dot(ones, parts[1]))[:8]
            part = (dot(turned[0], parts[0]) + dot(turned[1], parts[1])).astype(BF16)
            blocks[4 * j : 4 * j + 4] = part.reshape(4, deep, width)
        scatter_blocks(sem2, own_place(), blocks, keep, send)

    half = ((CUTS // 2, deep, width), BF16, "a")
    ins = [(v, "v") for v in lines] + [(recv, "a"), (weights[2], "a"), (weights[3], "a")]
    ins += [(kept[n], "a") for n in given]
    outs = [half, half, ((4, 8, width), F32, "v")]
    outs += [(kept[n].shape, kept[n].dtype, "a") for n in ("dp", "small")]
    outs += [((slots, width), F32, "a")]
    wshapes = weight_sizes(width, ff)
    scratch = [pltpu.VMEM(wshapes["up"], BF16), pltpu.VMEM(wshapes["down"], BF16)]
    scratch += [pltpu.VMEM(*shapes[n]) for n in names]
    scratch += [
        pltpu.VMEM((2 * slots, width), BF16),
        pltpu.VMEM((2, slots, ff), BF16),
        pltpu.VMEM((CUTS, deep, width), BF16),
        pltpu.SemaphoreType.DMA((16,)),
        pltpu.SemaphoreType.DMA((CUTS,)),
    ]
    return run(body, ins, outs, scratch, {n_in - 2: 3, n_in - 1: 4}, us=6)


def attention_grads(lines, tokens, weights, kept, dh, grads, down_sums, up_sums, dims):
    slots, width, ff = dims
    deep = width // 4
    tall = deep + 16
    shapes = all_sizes(dims)
    names = (
        "dp", "dh", "inv", "ot", "v", "e", "kt", "qt", "s", "ds", "g", "center", "dot", "dqkv",
        "small",
    )
    loads = ("inv", "v", "e", "kt", "qt")
    given = ("a", "ot", "dp", "dqkv", "small") + loads
    n_in = len(lines) + 7 + len(given)

    def body(*refs):
        vec = dict(zip(LINES, refs[: len(lines)]))
        tokens_hbm, out_hbm, qkv_hbm, dh_hbm, grads_in, down_ref, up_ref = refs[
            len(lines) : len(lines) + 7
        ]
        hbm = dict(zip(given, refs[len(lines) + 7 : n_in]))
        keep, send, grads_hbm = refs[n_in : n_in + 3]
        rest = refs[n_in + 3 :]
        w = {"out": rest[0], "qkv": rest[1]}
        r = dict(zip(names, rest[2 : 2 + len(names)]))
        x, a, d, o, p, s, blocks, sem, sem2 = rest[2 + len(names) :]
        moves = Moves(sem)
        lead = lax.axis_index("section") == 0
        moves.start("p1", hbm["dp"].at[1], p.at[1])
        moves.start("o1", hbm["ot"].at[1], o.at[1])
        moves.start("s1", hbm["small"].at[1], s.at[1])
        own = moves.make("d1", hbm["dqkv"].at[1], d.at[1])

        @pl.when(jnp.logical_not(lead))
        def _():
            own.start()

        @pl.when(lead)
        def _():
            inner = Moves(sem.at[pl.ds(12, 12)])
            inner.start("out", out_hbm.at[0], w["out"])
            for n in loads:
                inner.start(n, hbm[n].at[1], r[n])
            inner.start("qkv", qkv_hbm.at[0], w["qkv"])
            inner.start("x", tokens_hbm.at[1, 0], x)
            inner.start("dh", dh_hbm, r["dh"])
            for n in ("p1", "o1", "s1"):
                moves.made[n].wait()
            r.update(dp=p.at[1], ot=o.at[1], dqkv=d.at[1], small=s.at[1])

            def wait(n):
                if n == "qkv":
                    inner.wait("x")
                    inner.wait("dh")
                inner.wait(n)

            backward_attention(x, x, vec, w, r, wait, nothing)
            inner.start("g", x, grads_hbm.at[1])
            inner.finish()

        @pl.when(jnp.logical_not(lead))
        def _():
            for n in ("p1", "o1", "s1", "d1"):
                moves.made[n].wait()

        for n in ("p1", "o1", "s1", "d1"):
            moves.made.pop(n)
        moves.start("p0", hbm["dp"].at[0], p.at[0])
        moves.start("o0", hbm["ot"].at[0], o.at[0])
        moves.start("s0", hbm["small"].at[0], s.at[0])
        moves.start("d0", hbm["dqkv"].at[0], d.at[0])
        moves.start("a0", hbm["a"].at[0], a.at[0])
        moves.start("a1", hbm["a"].at[1], a.at[1])
        moves.finish()
        ones = jnp.ones((16, slots), BF16)
        turned = [a[i].T for i in (0, 1)]
        both = s[0] + s[1]
        rows = [
            both[A_GAIN_G : A_GAIN_G + 1], both[A_SHIFT_G : A_SHIFT_G + 1], None, None,
            (dot(ones, p[0]) + dot(ones, p[1]))[:1],
            both[M_GAIN_G : M_GAIN_G + 1], both[M_SHIFT_G : M_SHIFT_G + 1],
            down_ref[:1], up_ref[0, :1], up_ref[1, :1], up_ref[2, :1], up_ref[3, :1],
        ]
        for j in range(3):
            parts = [d[i, j].reshape(width, slots) for i in (0, 1)]
            if j != 1:
                rows[2 + j // 2] = (dot_nt(ones, parts[0]) + dot_nt(ones, parts[1]))[:1]
            part = (dot_nt(turned[0], parts[0]) + dot_nt(turned[1], parts[1])).astype(BF16)
            blocks[4 * j : 4 * j + 4, :deep] = part.reshape(4, deep, width)
        mixed = [o[i].reshape(width, slots).astype(BF16) for i in (0, 1)]
        part = dot(mixed[0], p[0]) + dot(mixed[1], p[1])
        blocks[12:16, :deep] = part.astype(BF16).reshape(4, deep, width)
        for i in range(CUTS):
            line = rows[i] if i < 12 else jnp.zeros((1, width), F32)
            blocks[i, deep:] = jnp.broadcast_to(line, (16, width)).astype(BF16)
        scatter_blocks(sem2, own_place(), blocks, keep, send)

    ins = [(v, "v") for v in lines] + [(tokens, "a"), (weights[1], "a"), (weights[0], "a")]
    ins += [(dh, "a"), (grads, "a"), (down_sums, "v"), (up_sums, "v")]
    ins += [(kept[n], "a") for n in given]
    half = ((CUTS // 2, tall, width), BF16, "a")
    outs = [half, half, (grads.shape, grads.dtype, "a")]
    wshapes = weight_sizes(width, ff)
    scratch = [pltpu.VMEM(wshapes["out"], BF16), pltpu.VMEM(wshapes["qkv"], BF16)]
    scratch += [pltpu.VMEM(*shapes[n]) for n in names]
    scratch += [pltpu.VMEM((slots, width), BF16)]
    scratch += [pltpu.VMEM((2, *shapes[n][0]), shapes[n][1]) for n in ("a", "dqkv", "ot", "dp", "small")]
    scratch += [
        pltpu.VMEM((CUTS, tall, width), BF16),
        pltpu.SemaphoreType.DMA((24,)),
        pltpu.SemaphoreType.DMA((CUTS,)),
    ]
    return run(body, ins, outs, scratch, {len(lines) + 4: 2}, us=12)


def block(own, other, p):
    place = jnp.bitwise_xor(p, own_place())
    mine = own[place // 2]
    theirs = other[place // 2]
    odd = jnp.bitwise_and(place, 1)
    return jnp.where(odd == 1, theirs, mine).astype(F32)


def down_out(own, other, dims):
    slots, width, ff = dims

    def body(own_ref, other_ref, out):
        for j in range(4):
            part = [block(own_ref, other_ref, 4 * j + i) for i in range(4)]
            out[0, j * width : (j + 1) * width, :] = jnp.concatenate(part, 0).T

    return run(body, [(own, "v"), (other, "v")], [((1, ff, width), F32, "v")], [], us=3)[0]


def up_out(own, other, dims):
    slots, width, ff = dims
    deep = width // 4

    def body(own_ref, other_ref, out):
        for p in range(CUTS):
            j, i = p // 4, p % 4
            out[0, i * deep : (i + 1) * deep, j * width : (j + 1) * width] = block(
                own_ref, other_ref, p
            )

    return run(body, [(own, "v"), (other, "v")], [((1, width, ff), F32, "v")], [], us=3)[0]


def attention_out(own, other, dims):
    slots, width, ff = dims
    deep = width // 4

    def body(own_ref, other_ref, qkv, out, *lines):
        for p in range(CUTS):
            j, i = p // 4, p % 4
            got = block(own_ref, other_ref, p)
            if j < 3:
                qkv[0, i * deep : (i + 1) * deep, j * width : (j + 1) * width] = got[:deep]
            else:
                out[0, i * deep : (i + 1) * deep, :] = got[:deep]
            if p < 8:
                lines[p][...] = got[deep : deep + 1]
            elif p < 12:
                lines[8][:, (p - 8) * width : (p - 7) * width] = got[deep : deep + 1]

    outs = [((1, width, 3 * width), F32, "v"), ((1, width, width), F32, "v")]
    outs += [((1, width), F32, "v")] * 8 + [((1, ff), F32, "v")]
    return run(body, [(own, "v"), (other, "v")], outs, [], us=3)


def swapped(x, bits):
    return lax.ppermute(x, "dp", [(i, i ^ bits) for i in range(CUTS)])


def added(*parts):
    total = parts[0].astype(F32)
    for x in parts[1:]:
        total = total + x.astype(F32)
    return total.astype(BF16)


def all_reduced(keep, send):
    if lax.axis_size("dp") != CUTS:
        return lax.psum(keep, "dp"), lax.psum(send, "dp")
    u = added(keep, swapped(send, 1))
    u = u.reshape(4, 2, *u.shape[1:])
    u = added(u[:, 0], swapped(u[:, 1], 2))
    u = added(u[0], *[swapped(u[j], 4 * j) for j in (1, 2, 3)])
    u = jnp.stack([u] + [swapped(u, 4 * j) for j in (1, 2, 3)])
    u = jnp.stack([u, swapped(u, 2)], 1)
    u = u.reshape(8, *u.shape[2:])
    return u, swapped(u, 1)


def shards(
    tokens, cotangent, views, attn_gain, attn_shift, qkv_weight, query_bias, value_bias,
    out_weight, out_bias, mlp_gain, mlp_shift, up_weight, up_bias, down_weight, down_bias,
):
    dims = (tokens.shape[2], tokens.shape[3], up_bias.shape[1])
    weights = (qkv_weight, out_weight, up_weight, down_weight)
    lines = (
        attn_gain, attn_shift, query_bias, value_bias, out_bias, mlp_gain, mlp_shift, down_bias,
        up_bias,
    )

    def advance(t, carry):
        recv, bufs = carry
        step = jnp.reshape(t, (1,))
        send, bufs = cell(step, views, lines, tokens, cotangent, recv, weights, bufs, dims)
        return lax.ppermute(send, "section", [(0, 1), (1, 0)]), bufs

    recv, bufs = lax.fori_loop(0, STEPS, advance, blank(dims))
    outs, grads = bufs[:2]
    kept = dict(zip(SAVED + TERMS, bufs[2:]))
    keep, send, down_sums = down_grads(kept["z"], kept["dm"], recv, dims)
    down_sum = all_reduced(keep, send)
    keep, send, up_sums, kept["dp"], kept["small"], dh = up_grads(lines, recv, weights, kept, dims)
    up_sum = all_reduced(keep, send)
    keep, send, grads = attention_grads(
        lines, tokens, weights, kept, dh, grads, down_sums, up_sums, dims
    )
    attention_sum = all_reduced(keep, send)
    g_down = down_out(*down_sum, dims)
    g_up = up_out(*up_sum, dims)
    g_qkv, g_out, *rows = attention_out(*attention_sum, dims)
    g_ag, g_as, g_qb, g_vb, g_ob, g_mg, g_ms, g_db, g_ub = rows
    return (
        outs[None, :, None], grads[None, :, None], g_ag, g_as, g_qkv, g_qb, g_vb, g_out, g_ob,
        g_mg, g_ms, g_up, g_ub, g_down, g_db,
    )


def solution(mesh):
    scene = P(None, "dp", None, None)
    line = P("section", None)
    table = P("section", None, None)
    kept = P("section", None, "dp", None, None)
    kinds = (line, line, table, line, line, table, line, line, line, table, line, table, line)
    return jax.shard_map(
        shards,
        mesh=mesh,
        in_specs=(scene, scene, P(None, "dp")) + kinds,
        out_specs=(kept, kept) + kinds,
        check_vma=False,
    )
```

profile of v0, /device:TPU:0, one launch (start us, length us, event | category | flops | bytes accessed | tf_op | source)
XLA Modules:
  0.0 178.7 jit_solution(11372999386562909244)
XLA Ops:
  2.0 75.0 %while.49 = (s32[]{:T(128)}, bf16[512,384]{1,0:T(8,128)(2,1)}, bf16[2,512,384]{2,1,0:T(8,128)(2,1)}, bf16[2,512,384]{2,1,0:T(8,128)(2,1)}, bf16[2,512,384]{2,1,0...) while((s32[]{:T(128)}, bf16[512,384]{1,0:T(8,128)(2,1)}, ...), condition=%wide.region_1.0_spmd, body=%wide.region_0.0_spmd.sunk | while | flops 1000000000 | bytes 3573221 | solution.py:830
  2.0 10.1 %eval_jaxpr.5 = (bf16[512,384]{1,0:T(8,128)(2,1)S(1)}, bf16[2,512,384]{2,1,0:T(8,128)(2,1)}, bf16[2,512,384]{2,1,0:T(8,128)(2,1)}, bf16[2,512,384]{2,1,0:T(8,128...) custom-call(s32[1]{0:T(128)} %bitcast.105.refs_0_, ...), custom_call_target="tpu_custom_call", output_to_operand_aliasing={{1}: (18, {}), {2}: (19, {}), {3}: (20, {}), {4}: (21, {}),... | custom-call | flops 1000000000 | bytes 2000000 | tf_op jit(solution)/shard_map/while/body/eval_jaxpr/pallas_call | solution.py:279
  12.2 11.6 %collective-permute-done = bf16[512,384]{1,0:T(8,128)(2,1)} collective-permute-done((bf16[512,384]{1,0:T(8,128)(2,1)S(1)}, bf16[512,384]{1,0:T(8,128)(2,1)}, u32[]{:S(2)}, u32[]{:S(2)}) %collective-permute-start) | collective-permute-done | bytes 393248 | tf_op jit(solution)/shard_map/while/body/eval_jaxpr/ppermute | solution.py:828
  23.7 10.0 %eval_jaxpr.5 = (bf16[512,384]{1,0:T(8,128)(2,1)S(1)}, bf16[2,512,384]{2,1,0:T(8,128)(2,1)}, bf16[2,512,384]{2,1,0:T(8,128)(2,1)}, bf16[2,512,384]{2,1,0:T(8,128...) custom-call(s32[1]{0:T(128)} %bitcast.105.refs_0_, ...), custom_call_target="tpu_custom_call", output_to_operand_aliasing={{1}: (18, {}), {2}: (19, {}), {3}: (20, {}), {4}: (21, {}),... | custom-call | flops 1000000000 | bytes 2000000 | tf_op jit(solution)/shard_map/while/body/eval_jaxpr/pallas_call | solution.py:279
  33.8 7.0 %collective-permute-start = (bf16[512,384]{1,0:T(8,128)(2,1)S(1)}, bf16[512,384]{1,0:T(8,128)(2,1)}, u32[]{:S(2)}, u32[]{:S(2)}) collective-permute-start(bf16[512,384]{1,0:T(8,128)(2,1)S(1)} %get-tuple-element.1035), channel_id=1, source_target_pairs={{0,16},{16,0},{1,17},{17,1},{2,18},{18,2},{3,19},{19,3},{4,20},{20... | collective-permute-start | bytes 1179656 | tf_op jit(solution)/shard_map/while/body/eval_jaxpr/ppermute | solution.py:828
  40.8 9.3 %collective-permute-done = bf16[512,384]{1,0:T(8,128)(2,1)} collective-permute-done((bf16[512,384]{1,0:T(8,128)(2,1)S(1)}, bf16[512,384]{1,0:T(8,128)(2,1)}, u32[]{:S(2)}, u32[]{:S(2)}) %collective-permute-start) | collective-permute-done | bytes 393248 | tf_op jit(solution)/shard_map/while/body/eval_jaxpr/ppermute | solution.py:828
  50.1 11.3 %eval_jaxpr.5 = (bf16[512,384]{1,0:T(8,128)(2,1)S(1)}, bf16[2,512,384]{2,1,0:T(8,128)(2,1)}, bf16[2,512,384]{2,1,0:T(8,128)(2,1)}, bf16[2,512,384]{2,1,0:T(8,128...) custom-call(s32[1]{0:T(128)} %bitcast.105.refs_0_, ...), custom_call_target="tpu_custom_call", output_to_operand_aliasing={{1}: (18, {}), {2}: (19, {}), {3}: (20, {}), {4}: (21, {}),... | custom-call | flops 1000000000 | bytes 2000000 | tf_op jit(solution)/shard_map/while/body/eval_jaxpr/pallas_call | solution.py:279
  61.4 7.2 %collective-permute-start = (bf16[512,384]{1,0:T(8,128)(2,1)S(1)}, bf16[512,384]{1,0:T(8,128)(2,1)}, u32[]{:S(2)}, u32[]{:S(2)}) collective-permute-start(bf16[512,384]{1,0:T(8,128)(2,1)S(1)} %get-tuple-element.1035), channel_id=1, source_target_pairs={{0,16},{16,0},{1,17},{17,1},{2,18},{18,2},{3,19},{19,3},{4,20},{20... | collective-permute-start | bytes 1179656 | tf_op jit(solution)/shard_map/while/body/eval_jaxpr/ppermute | solution.py:828
  68.6 8.4 %collective-permute-done = bf16[512,384]{1,0:T(8,128)(2,1)} collective-permute-done((bf16[512,384]{1,0:T(8,128)(2,1)S(1)}, bf16[512,384]{1,0:T(8,128)(2,1)}, u32[]{:S(2)}, u32[]{:S(2)}) %collective-permute-start) | collective-permute-done | bytes 393248 | tf_op jit(solution)/shard_map/while/body/eval_jaxpr/ppermute | solution.py:828
  77.1 5.3 %shard_map.273 = (bf16[8,96,384]{2,1,0:T(8,128)(2,1)S(1)}, bf16[8,96,384]{2,1,0:T(8,128)(2,1)S(1)}, f32[8,384]{1,0:T(8,128)S(1)}) custom-call(bf16[2,512,1536]{2,1,0:T(8,128)(2,1)S(1)} %get-tuple-element.629.z_hbm, bf16[2,512,384]{2,1,0:T(8,128)(2,1)} %get-tuple-element.630.dm_hbm, bf16[512,384]{1,0:T(8,128)(2,1)} %get-tuple-element.620.refs_9_.recv_hbm), custom_call_target="tpu_custom_call" | custom-call | flops 4000000000 | bytes 8000000 | tf_op jit(solution)/shard_map/pallas_call | solution.py:279
  82.7 9.1 %shard_map.272 = (bf16[8,96,384]{2,1,0:T(8,128)(2,1)S(1)}, bf16[8,96,384]{2,1,0:T(8,128)(2,1)S(1)}, f32[4,8,384]{2,1,0:T(8,128)S(1)}, bf16[2,512,384]{2,1,0:T(8,...) custom-call(bf16[1,384]{1,0:T(2,128)(2,1)S(1)} %get-tuple-element.123, ...), custom_call_target="tpu_custom_call", output_to_operand_aliasing={{3}: (16, {}), {4}: (17, {})} | custom-call | flops 6000000000 | bytes 12000000 | tf_op jit(solution)/shard_map/pallas_call | solution.py:279
  92.4 12.4 %shard_map.274 = (bf16[8,112,384]{2,1,0:T(8,128)(2,1)S(1)}, bf16[8,112,384]{2,1,0:T(8,128)(2,1)S(1)}, bf16[2,512,384]{2,1,0:T(8,128)(2,1)S(1)}) custom-call(bf16[1,384]{1,0:T(2,128)(2,1)S(1)} %get-tuple-element.1232, bf16[1,384]{1,0:T(2,128)(2,1)S(1)} %get-tuple-element.1233, bf16[1,384]{1,0:T(2,128)(2,1)S(1)} %copy-done.21, ...), custom_call_target="tpu_custom_call", output_to_operand_aliasing={{2}: (13, {})} | custom-call | flops 12000000000 | bytes 24000000 | tf_op jit(solution)/shard_map/pallas_call | solution.py:279
  108.9 6.2 %collective-permute-done.22 = bf16[4,96,384]{2,1,0:T(8,128)(2,1)S(1)} collective-permute-done((bf16[4,96,384]{2,1,0:T(8,128)(2,1)S(1)}, bf16[4,96,384]{2,1,0:T(8,128)(2,1)S(1)}, u32[]{:S(2)}, u32[]{:S(2)}) %collective-permute-start.22) | collective-permute-done | bytes 294944 | tf_op jit(solution)/shard_map/ppermute | solution.py:790
  116.4 2.5 %collective-permute-start.25 = (bf16[96,384]{1,0:T(8,128)(2,1)S(1)}, bf16[96,384]{1,0:T(8,128)(2,1)S(1)}, u32[]{:S(2)}, u32[]{:S(2)}) collective-permute-start(bf16[96,384]{1,0:T(8,128)(2,1)S(1)} %get-tuple-element.792), channel_id=1, source_target_pairs={{0,12},{1,13},{2,14},{3,15},{4,8},{5,9},{6,10},{7,11},{8,4},{9,5},... | collective-permute-start | bytes 221192 | tf_op jit(solution)/shard_map/ppermute | solution.py:790
  119.0 2.4 %collective-permute-done.12 = bf16[4,96,384]{2,1,0:T(8,128)(2,1)S(1)} collective-permute-done((bf16[4,96,384]{2,1,0:T(8,128)(2,1)S(1)}, bf16[4,96,384]{2,1,0:T(8,128)(2,1)S(1)}, u32[]{:S(2)}, u32[]{:S(2)}) %collective-permute-start.12) | collective-permute-done | bytes 294944 | tf_op jit(solution)/shard_map/ppermute | solution.py:790
  122.7 2.5 %collective-permute-start.15 = (bf16[96,384]{1,0:T(8,128)(2,1)S(1)}, bf16[96,384]{1,0:T(8,128)(2,1)S(1)}, u32[]{:S(2)}, u32[]{:S(2)}) collective-permute-start(bf16[96,384]{1,0:T(8,128)(2,1)S(1)} %get-tuple-element.797), channel_id=1, source_target_pairs={{0,12},{1,13},{2,14},{3,15},{4,8},{5,9},{6,10},{7,11},{8,4},{9,5},... | collective-permute-start | bytes 221192 | tf_op jit(solution)/shard_map/ppermute | solution.py:790
  126.2 2.2 %collective-permute-start.28 = (bf16[96,384]{1,0:T(8,128)(2,1)S(1)}, bf16[96,384]{1,0:T(8,128)(2,1)S(1)}, u32[]{:S(2)}, u32[]{:S(2)}) collective-permute-start(bf16[96,384]{1,0:T(8,128)(2,1)S(1)} %fusion.8), channel_id=1, source_target_pairs={{0,12},{1,13},{2,14},{3,15},{4,8},{5,9},{6,10},{7,11},{8,4},{9,5},... | collective-permute-start | bytes 221192 | tf_op jit(solution)/shard_map/ppermute | solution.py:790
  129.2 6.0 %collective-permute-done.14 = bf16[96,384]{1,0:T(8,128)(2,1)S(1)} collective-permute-done((bf16[96,384]{1,0:T(8,128)(2,1)S(1)}, bf16[96,384]{1,0:T(8,128)(2,1)S(1)}, u32[]{:S(2)}, u32[]{:S(2)}) %collective-permute-start.14) | collective-permute-done | bytes 73760 | tf_op jit(solution)/shard_map/ppermute | solution.py:790
  135.3 3.1 %collective-permute-start.18 = (bf16[96,384]{1,0:T(8,128)(2,1)S(1)}, bf16[96,384]{1,0:T(8,128)(2,1)S(1)}, u32[]{:S(2)}, u32[]{:S(2)}) collective-permute-start(bf16[96,384]{1,0:T(8,128)(2,1)S(1)} %fusion.11), channel_id=1, source_target_pairs={{0,12},{1,13},{2,14},{3,15},{4,8},{5,9},{6,10},{7,11},{8,4},{9,5},... | collective-permute-start | bytes 221192 | tf_op jit(solution)/shard_map/ppermute | solution.py:790
  139.9 2.4 %collective-permute-done.18 = bf16[96,384]{1,0:T(8,128)(2,1)S(1)} collective-permute-done((bf16[96,384]{1,0:T(8,128)(2,1)S(1)}, bf16[96,384]{1,0:T(8,128)(2,1)S(1)}, u32[]{:S(2)}, u32[]{:S(2)}) %collective-permute-start.18) | collective-permute-done | bytes 73760 | tf_op jit(solution)/shard_map/ppermute | solution.py:790
  144.4 2.4 %collective-permute-start.5 = (bf16[112,384]{1,0:T(8,128)(2,1)S(1)}, bf16[112,384]{1,0:T(8,128)(2,1)S(1)}, u32[]{:S(2)}, u32[]{:S(2)}) collective-permute-start(bf16[112,384]{1,0:T(8,128)(2,1)S(1)} %get-tuple-element.787), channel_id=1, source_target_pairs={{0,12},{1,13},{2,14},{3,15},{4,8},{5,9},{6,10},{7,11},{8,4},{9,5},... | collective-permute-start | bytes 258056 | tf_op jit(solution)/shard_map/ppermute | solution.py:790
  147.0 2.0 %collective-permute-start.26 = (bf16[96,384]{1,0:T(8,128)(2,1)S(1)}, bf16[96,384]{1,0:T(8,128)(2,1)S(1)}, u32[]{:S(2)}, u32[]{:S(2)}) collective-permute-start(bf16[96,384]{1,0:T(8,128)(2,1)S(1)} %fusion.8), channel_id=1, source_target_pairs={{0,4},{1,5},{2,6},{3,7},{4,0},{5,1},{6,2},{7,3},{8,12},{9,13},{10,... | collective-permute-start | bytes 221192 | tf_op jit(solution)/shard_map/ppermute | solution.py:790
  149.0 2.8 %collective-permute-done.5 = bf16[112,384]{1,0:T(8,128)(2,1)S(1)} collective-permute-done((bf16[112,384]{1,0:T(8,128)(2,1)S(1)}, bf16[112,384]{1,0:T(8,128)(2,1)S(1)}, u32[]{:S(2)}, u32[]{:S(2)}) %collective-permute-start.5) | collective-permute-done | bytes 86048 | tf_op jit(solution)/shard_map/ppermute | solution.py:790
  151.8 1.5 collective-permute-start.19
  153.9 2.3 %collective-permute-start.8 = (bf16[112,384]{1,0:T(8,128)(2,1)S(1)}, bf16[112,384]{1,0:T(8,128)(2,1)S(1)}, u32[]{:S(2)}, u32[]{:S(2)}) collective-permute-start(bf16[112,384]{1,0:T(8,128)(2,1)S(1)} %fusion.5), channel_id=1, source_target_pairs={{0,12},{1,13},{2,14},{3,15},{4,8},{5,9},{6,10},{7,11},{8,4},{9,5},... | collective-permute-start | bytes 258056 | tf_op jit(solution)/shard_map/ppermute | solution.py:790
  156.2 2.1 %collective-permute-start.6 = (bf16[112,384]{1,0:T(8,128)(2,1)S(1)}, bf16[112,384]{1,0:T(8,128)(2,1)S(1)}, u32[]{:S(2)}, u32[]{:S(2)}) collective-permute-start(bf16[112,384]{1,0:T(8,128)(2,1)S(1)} %fusion.5), channel_id=1, source_target_pairs={{0,4},{1,5},{2,6},{3,7},{4,0},{5,1},{6,2},{7,3},{8,12},{9,13},{10,... | collective-permute-start | bytes 258056 | tf_op jit(solution)/shard_map/ppermute | solution.py:790
  158.4 1.4 collective-permute-start.29
  161.1 2.4 %collective-permute-done.7 = bf16[112,384]{1,0:T(8,128)(2,1)S(1)} collective-permute-done((bf16[112,384]{1,0:T(8,128)(2,1)S(1)}, bf16[112,384]{1,0:T(8,128)(2,1)S(1)}, u32[]{:S(2)}, u32[]{:S(2)}) %collective-permute-start.7) | collective-permute-done | bytes 86048 | tf_op jit(solution)/shard_map/ppermute | solution.py:790
  166.3 7.2 %collective-permute-done.9 = bf16[4,112,384]{2,1,0:T(8,128)(2,1)S(1)} collective-permute-done((bf16[4,112,384]{2,1,0:T(8,128)(2,1)S(1)}, bf16[4,112,384]{2,1,0:T(8,128)(2,1)S(1)}, u32[]{:S(2)}, u32[]{:S(2)}) %collective-permute-start.9) | collective-permute-done | bytes 344096 | tf_op jit(solution)/shard_map/ppermute | solution.py:790
  173.7 1.6 shard_map.276
  175.3 1.8 %shard_map.277 = f32[1,1536,384]{2,1,0:T(8,128)} custom-call(bf16[8,96,384]{2,1,0:T(8,128)(2,1)S(1)} %bitcast.111, bf16[8,96,384]{2,1,0:T(8,128)(2,1)S(1)} %collective-permute-done.30.other_ref), custom_call_target="tpu_custom_call" | custom-call | flops 3000000000 | bytes 6000000 | tf_op jit(solution)/shard_map/pallas_call | solution.py:279
  177.1 1.6 shard_map.275
  (128 shorter events, 19.3 us)
Async XLA Ops:
  12.1 11.6 %collective-permute-start = (bf16[512,384]{1,0:T(8,128)(2,1)S(1)}, bf16[512,384]{1,0:T(8,128)(2,1)}, u32[]{:S(2)}, u32[]{:S(2)}) collective-permute-start(bf16[512,384]{1,0:T(8,128)(2,1)S(1)} %get-tuple-element.1035), channel_id=1, source_target_pairs={{0,16},{16,0},{1,17},{17,1},{2,18},{18,2},{3,19},{19,3},{4,20},{20... | collective-permute-start | bytes 1179656 | tf_op jit(solution)/shard_map/while/body/eval_jaxpr/ppermute | solution.py:828
  33.8 16.3 %collective-permute-start = (bf16[512,384]{1,0:T(8,128)(2,1)S(1)}, bf16[512,384]{1,0:T(8,128)(2,1)}, u32[]{:S(2)}, u32[]{:S(2)}) collective-permute-start(bf16[512,384]{1,0:T(8,128)(2,1)S(1)} %get-tuple-element.1035), channel_id=1, source_target_pairs={{0,16},{16,0},{1,17},{17,1},{2,18},{18,2},{3,19},{19,3},{4,20},{20... | collective-permute-start | bytes 1179656 | tf_op jit(solution)/shard_map/while/body/eval_jaxpr/ppermute | solution.py:828
  61.4 15.6 %collective-permute-start = (bf16[512,384]{1,0:T(8,128)(2,1)S(1)}, bf16[512,384]{1,0:T(8,128)(2,1)}, u32[]{:S(2)}, u32[]{:S(2)}) collective-permute-start(bf16[512,384]{1,0:T(8,128)(2,1)S(1)} %get-tuple-element.1035), channel_id=1, source_target_pairs={{0,16},{16,0},{1,17},{17,1},{2,18},{18,2},{3,19},{19,3},{4,20},{20... | collective-permute-start | bytes 1179656 | tf_op jit(solution)/shard_map/while/body/eval_jaxpr/ppermute | solution.py:828
  82.4 22.6 %collective-permute-start.21 = (bf16[8,96,384]{2,1,0:T(8,128)(2,1)S(1)}, bf16[8,96,384]{2,1,0:T(8,128)(2,1)S(1)}, u32[]{:S(2)}, u32[]{:S(2)}) collective-permute-start(bf16[8,96,384]{2,1,0:T(8,128)(2,1)S(1)} %get-tuple-element.659), channel_id=1, source_target_pairs={{0,1},{1,0},{2,3},{3,2},{4,5},{5,4},{6,7},{7,6},{8,9},{9,8},{10,11... | collective-permute-start | bytes 1769480 | tf_op jit(solution)/shard_map/ppermute | solution.py:790
  91.8 14.5 %collective-permute-start.11 = (bf16[8,96,384]{2,1,0:T(8,128)(2,1)S(1)}, bf16[8,96,384]{2,1,0:T(8,128)(2,1)S(1)}, u32[]{:S(2)}, u32[]{:S(2)}) collective-permute-start(bf16[8,96,384]{2,1,0:T(8,128)(2,1)S(1)} %get-tuple-element.656), channel_id=1, source_target_pairs={{0,1},{1,0},{2,3},{3,2},{4,5},{5,4},{6,7},{7,6},{8,9},{9,8},{10,11... | collective-permute-start | bytes 1769480 | tf_op jit(solution)/shard_map/ppermute | solution.py:790
  105.2 9.9 %collective-permute-start.22 = (bf16[4,96,384]{2,1,0:T(8,128)(2,1)S(1)}, bf16[4,96,384]{2,1,0:T(8,128)(2,1)S(1)}, u32[]{:S(2)}, u32[]{:S(2)}) collective-permute-start(bf16[4,96,384]{2,1,0:T(8,128)(2,1)S(1)} %slice_bitcast_fusion.2), channel_id=1, source_target_pairs={{0,2},{1,3},{2,0},{3,1},{4,6},{5,7},{6,4},{7,5},{8,10},{9,11},{10,... | collective-permute-start | bytes 884744 | tf_op jit(solution)/shard_map/ppermute | solution.py:790
  106.5 14.9 %collective-permute-start.12 = (bf16[4,96,384]{2,1,0:T(8,128)(2,1)S(1)}, bf16[4,96,384]{2,1,0:T(8,128)(2,1)S(1)}, u32[]{:S(2)}, u32[]{:S(2)}) collective-permute-start(bf16[4,96,384]{2,1,0:T(8,128)(2,1)S(1)} %slice_bitcast_fusion.4), channel_id=1, source_target_pairs={{0,2},{1,3},{2,0},{3,1},{4,6},{5,7},{6,4},{7,5},{8,10},{9,11},{10,... | collective-permute-start | bytes 884744 | tf_op jit(solution)/shard_map/ppermute | solution.py:790
  107.8 30.7 %collective-permute-start.2 = (bf16[4,112,384]{2,1,0:T(8,128)(2,1)S(1)}, bf16[4,112,384]{2,1,0:T(8,128)(2,1)S(1)}, u32[]{:S(2)}, u32[]{:S(2)}) collective-permute-start(bf16[4,112,384]{2,1,0:T(8,128)(2,1)S(1)} %slice_bitcast_fusion), channel_id=1, source_target_pairs={{0,2},{1,3},{2,0},{3,1},{4,6},{5,7},{6,4},{7,5},{8,10},{9,11},{10,... | collective-permute-start | bytes 1032200 | tf_op jit(solution)/shard_map/ppermute | solution.py:790
  115.2 7.5 %collective-permute-start.23 = (bf16[96,384]{1,0:T(8,128)(2,1)S(1)}, bf16[96,384]{1,0:T(8,128)(2,1)S(1)}, u32[]{:S(2)}, u32[]{:S(2)}) collective-permute-start(bf16[96,384]{1,0:T(8,128)(2,1)S(1)} %get-tuple-element.791), channel_id=1, source_target_pairs={{0,4},{1,5},{2,6},{3,7},{4,0},{5,1},{6,2},{7,3},{8,12},{9,13},{10,... | collective-permute-start | bytes 221192 | tf_op jit(solution)/shard_map/ppermute | solution.py:790
  116.4 8.8 %collective-permute-start.25 = (bf16[96,384]{1,0:T(8,128)(2,1)S(1)}, bf16[96,384]{1,0:T(8,128)(2,1)S(1)}, u32[]{:S(2)}, u32[]{:S(2)}) collective-permute-start(bf16[96,384]{1,0:T(8,128)(2,1)S(1)} %get-tuple-element.792), channel_id=1, source_target_pairs={{0,12},{1,13},{2,14},{3,15},{4,8},{5,9},{6,10},{7,11},{8,4},{9,5},... | collective-permute-start | bytes 221192 | tf_op jit(solution)/shard_map/ppermute | solution.py:790
  118.9 7.2 %collective-permute-start.24 = (bf16[96,384]{1,0:T(8,128)(2,1)S(1)}, bf16[96,384]{1,0:T(8,128)(2,1)S(1)}, u32[]{:S(2)}, u32[]{:S(2)}) collective-permute-start(bf16[96,384]{1,0:T(8,128)(2,1)S(1)} %get-tuple-element.793), channel_id=1, source_target_pairs={{0,8},{1,9},{2,10},{3,11},{4,12},{5,13},{6,14},{7,15},{8,0},{9,1},... | collective-permute-start | bytes 221192 | tf_op jit(solution)/shard_map/ppermute | solution.py:790
  121.5 6.9 %collective-permute-start.13 = (bf16[96,384]{1,0:T(8,128)(2,1)S(1)}, bf16[96,384]{1,0:T(8,128)(2,1)S(1)}, u32[]{:S(2)}, u32[]{:S(2)}) collective-permute-start(bf16[96,384]{1,0:T(8,128)(2,1)S(1)} %get-tuple-element.796), channel_id=1, source_target_pairs={{0,4},{1,5},{2,6},{3,7},{4,0},{5,1},{6,2},{7,3},{8,12},{9,13},{10,... | collective-permute-start | bytes 221192 | tf_op jit(solution)/shard_map/ppermute | solution.py:790
  122.7 6.5 %collective-permute-start.15 = (bf16[96,384]{1,0:T(8,128)(2,1)S(1)}, bf16[96,384]{1,0:T(8,128)(2,1)S(1)}, u32[]{:S(2)}, u32[]{:S(2)}) collective-permute-start(bf16[96,384]{1,0:T(8,128)(2,1)S(1)} %get-tuple-element.797), channel_id=1, source_target_pairs={{0,12},{1,13},{2,14},{3,15},{4,8},{5,9},{6,10},{7,11},{8,4},{9,5},... | collective-permute-start | bytes 221192 | tf_op jit(solution)/shard_map/ppermute | solution.py:790
  125.2 10.1 %collective-permute-start.14 = (bf16[96,384]{1,0:T(8,128)(2,1)S(1)}, bf16[96,384]{1,0:T(8,128)(2,1)S(1)}, u32[]{:S(2)}, u32[]{:S(2)}) collective-permute-start(bf16[96,384]{1,0:T(8,128)(2,1)S(1)} %get-tuple-element.798), channel_id=1, source_target_pairs={{0,8},{1,9},{2,10},{3,11},{4,12},{5,13},{6,14},{7,15},{8,0},{9,1},... | collective-permute-start | bytes 221192 | tf_op jit(solution)/shard_map/ppermute | solution.py:790
  126.2 30.0 %collective-permute-start.28 = (bf16[96,384]{1,0:T(8,128)(2,1)S(1)}, bf16[96,384]{1,0:T(8,128)(2,1)S(1)}, u32[]{:S(2)}, u32[]{:S(2)}) collective-permute-start(bf16[96,384]{1,0:T(8,128)(2,1)S(1)} %fusion.8), channel_id=1, source_target_pairs={{0,12},{1,13},{2,14},{3,15},{4,8},{5,9},{6,10},{7,11},{8,4},{9,5},... | collective-permute-start | bytes 221192 | tf_op jit(solution)/shard_map/ppermute | solution.py:790
  128.4 27.8 %collective-permute-start.27 = (bf16[96,384]{1,0:T(8,128)(2,1)S(1)}, bf16[96,384]{1,0:T(8,128)(2,1)S(1)}, u32[]{:S(2)}, u32[]{:S(2)}) collective-permute-start(bf16[96,384]{1,0:T(8,128)(2,1)S(1)} %fusion.8), channel_id=1, source_target_pairs={{0,8},{1,9},{2,10},{3,11},{4,12},{5,13},{6,14},{7,15},{8,0},{9,1},... | collective-permute-start | bytes 221192 | tf_op jit(solution)/shard_map/ppermute | solution.py:790
  135.3 7.0 %collective-permute-start.18 = (bf16[96,384]{1,0:T(8,128)(2,1)S(1)}, bf16[96,384]{1,0:T(8,128)(2,1)S(1)}, u32[]{:S(2)}, u32[]{:S(2)}) collective-permute-start(bf16[96,384]{1,0:T(8,128)(2,1)S(1)} %fusion.11), channel_id=1, source_target_pairs={{0,12},{1,13},{2,14},{3,15},{4,8},{5,9},{6,10},{7,11},{8,4},{9,5},... | collective-permute-start | bytes 221192 | tf_op jit(solution)/shard_map/ppermute | solution.py:790
  138.5 6.0 %collective-permute-start.17 = (bf16[96,384]{1,0:T(8,128)(2,1)S(1)}, bf16[96,384]{1,0:T(8,128)(2,1)S(1)}, u32[]{:S(2)}, u32[]{:S(2)}) collective-permute-start(bf16[96,384]{1,0:T(8,128)(2,1)S(1)} %fusion.11), channel_id=1, source_target_pairs={{0,8},{1,9},{2,10},{3,11},{4,12},{5,13},{6,14},{7,15},{8,0},{9,1},... | collective-permute-start | bytes 221192 | tf_op jit(solution)/shard_map/ppermute | solution.py:790
  138.5 8.4 %collective-permute-start.16 = (bf16[96,384]{1,0:T(8,128)(2,1)S(1)}, bf16[96,384]{1,0:T(8,128)(2,1)S(1)}, u32[]{:S(2)}, u32[]{:S(2)}) collective-permute-start(bf16[96,384]{1,0:T(8,128)(2,1)S(1)} %fusion.11), channel_id=1, source_target_pairs={{0,4},{1,5},{2,6},{3,7},{4,0},{5,1},{6,2},{7,3},{8,12},{9,13},{10,... | collective-permute-start | bytes 221192 | tf_op jit(solution)/shard_map/ppermute | solution.py:790
  142.3 4.6 %collective-permute-start.3 = (bf16[112,384]{1,0:T(8,128)(2,1)S(1)}, bf16[112,384]{1,0:T(8,128)(2,1)S(1)}, u32[]{:S(2)}, u32[]{:S(2)}) collective-permute-start(bf16[112,384]{1,0:T(8,128)(2,1)S(1)} %get-tuple-element.786), channel_id=1, source_target_pairs={{0,4},{1,5},{2,6},{3,7},{4,0},{5,1},{6,2},{7,3},{8,12},{9,13},{10,... | collective-permute-start | bytes 258056 | tf_op jit(solution)/shard_map/ppermute | solution.py:790
  144.4 7.3 %collective-permute-start.5 = (bf16[112,384]{1,0:T(8,128)(2,1)S(1)}, bf16[112,384]{1,0:T(8,128)(2,1)S(1)}, u32[]{:S(2)}, u32[]{:S(2)}) collective-permute-start(bf16[112,384]{1,0:T(8,128)(2,1)S(1)} %get-tuple-element.787), channel_id=1, source_target_pairs={{0,12},{1,13},{2,14},{3,15},{4,8},{5,9},{6,10},{7,11},{8,4},{9,5},... | collective-permute-start | bytes 258056 | tf_op jit(solution)/shard_map/ppermute | solution.py:790
  146.9 6.9 %collective-permute-start.4 = (bf16[112,384]{1,0:T(8,128)(2,1)S(1)}, bf16[112,384]{1,0:T(8,128)(2,1)S(1)}, u32[]{:S(2)}, u32[]{:S(2)}) collective-permute-start(bf16[112,384]{1,0:T(8,128)(2,1)S(1)} %get-tuple-element.788), channel_id=1, source_target_pairs={{0,8},{1,9},{2,10},{3,11},{4,12},{5,13},{6,14},{7,15},{8,0},{9,1},... | collective-permute-start | bytes 258056 | tf_op jit(solution)/shard_map/ppermute | solution.py:790
  147.0 11.4 %collective-permute-start.26 = (bf16[96,384]{1,0:T(8,128)(2,1)S(1)}, bf16[96,384]{1,0:T(8,128)(2,1)S(1)}, u32[]{:S(2)}, u32[]{:S(2)}) collective-permute-start(bf16[96,384]{1,0:T(8,128)(2,1)S(1)} %fusion.8), channel_id=1, source_target_pairs={{0,4},{1,5},{2,6},{3,7},{4,0},{5,1},{6,2},{7,3},{8,12},{9,13},{10,... | collective-permute-start | bytes 221192 | tf_op jit(solution)/shard_map/ppermute | solution.py:790
  151.8 13.1 %collective-permute-start.19 = (bf16[4,96,384]{2,1,0:T(8,128)(2,1)S(1)}, bf16[4,96,384]{2,1,0:T(8,128)(2,1)S(1)}, u32[]{:S(2)}, u32[]{:S(2)}) collective-permute-start(bf16[4,96,384]{2,1,0:T(8,128)(2,1)S(1)} %get-tuple-element.795), channel_id=1, source_target_pairs={{0,2},{1,3},{2,0},{3,1},{4,6},{5,7},{6,4},{7,5},{8,10},{9,11},{10,... | collective-permute-start | bytes 884744 | tf_op jit(solution)/shard_map/ppermute | solution.py:790
  153.9 7.2 %collective-permute-start.8 = (bf16[112,384]{1,0:T(8,128)(2,1)S(1)}, bf16[112,384]{1,0:T(8,128)(2,1)S(1)}, u32[]{:S(2)}, u32[]{:S(2)}) collective-permute-start(bf16[112,384]{1,0:T(8,128)(2,1)S(1)} %fusion.5), channel_id=1, source_target_pairs={{0,12},{1,13},{2,14},{3,15},{4,8},{5,9},{6,10},{7,11},{8,4},{9,5},... | collective-permute-start | bytes 258056 | tf_op jit(solution)/shard_map/ppermute | solution.py:790
  156.2 7.3 %collective-permute-start.7 = (bf16[112,384]{1,0:T(8,128)(2,1)S(1)}, bf16[112,384]{1,0:T(8,128)(2,1)S(1)}, u32[]{:S(2)}, u32[]{:S(2)}) collective-permute-start(bf16[112,384]{1,0:T(8,128)(2,1)S(1)} %fusion.5), channel_id=1, source_target_pairs={{0,8},{1,9},{2,10},{3,11},{4,12},{5,13},{6,14},{7,15},{8,0},{9,1},... | collective-permute-start | bytes 258056 | tf_op jit(solution)/shard_map/ppermute | solution.py:790
  156.2 7.3 %collective-permute-start.6 = (bf16[112,384]{1,0:T(8,128)(2,1)S(1)}, bf16[112,384]{1,0:T(8,128)(2,1)S(1)}, u32[]{:S(2)}, u32[]{:S(2)}) collective-permute-start(bf16[112,384]{1,0:T(8,128)(2,1)S(1)} %fusion.5), channel_id=1, source_target_pairs={{0,4},{1,5},{2,6},{3,7},{4,0},{5,1},{6,2},{7,3},{8,12},{9,13},{10,... | collective-permute-start | bytes 258056 | tf_op jit(solution)/shard_map/ppermute | solution.py:790
  158.4 7.7 %collective-permute-start.29 = (bf16[4,96,384]{2,1,0:T(8,128)(2,1)S(1)}, bf16[4,96,384]{2,1,0:T(8,128)(2,1)S(1)}, u32[]{:S(2)}, u32[]{:S(2)}) collective-permute-start(bf16[4,96,384]{2,1,0:T(8,128)(2,1)S(1)} %get-tuple-element.790), channel_id=1, source_target_pairs={{0,2},{1,3},{2,0},{3,1},{4,6},{5,7},{6,4},{7,5},{8,10},{9,11},{10,... | collective-permute-start | bytes 884744 | tf_op jit(solution)/shard_map/ppermute | solution.py:790
  163.5 10.0 %collective-permute-start.9 = (bf16[4,112,384]{2,1,0:T(8,128)(2,1)S(1)}, bf16[4,112,384]{2,1,0:T(8,128)(2,1)S(1)}, u32[]{:S(2)}, u32[]{:S(2)}) collective-permute-start(bf16[4,112,384]{2,1,0:T(8,128)(2,1)S(1)} %get-tuple-element.785), channel_id=1, source_target_pairs={{0,2},{1,3},{2,0},{3,1},{4,6},{5,7},{6,4},{7,5},{8,10},{9,11},{10,... | collective-permute-start | bytes 1032200 | tf_op jit(solution)/shard_map/ppermute | solution.py:790
  164.9 8.7 %collective-permute-start.20 = (bf16[8,96,384]{2,1,0:T(8,128)(2,1)S(1)}, bf16[8,96,384]{2,1,0:T(8,128)(2,1)S(1)}, u32[]{:S(2)}, u32[]{:S(2)}) collective-permute-start(bf16[8,96,384]{2,1,0:T(8,128)(2,1)S(1)} %bitcast.108), channel_id=1, source_target_pairs={{0,1},{1,0},{2,3},{3,2},{4,5},{5,4},{6,7},{7,6},{8,9},{9,8},{10,11... | collective-permute-start | bytes 1769480 | tf_op jit(solution)/shard_map/ppermute | solution.py:790
  166.2 9.1 %collective-permute-start.30 = (bf16[8,96,384]{2,1,0:T(8,128)(2,1)S(1)}, bf16[8,96,384]{2,1,0:T(8,128)(2,1)S(1)}, u32[]{:S(2)}, u32[]{:S(2)}) collective-permute-start(bf16[8,96,384]{2,1,0:T(8,128)(2,1)S(1)} %bitcast.110), channel_id=1, source_target_pairs={{0,1},{1,0},{2,3},{3,2},{4,5},{5,4},{6,7},{7,6},{8,9},{9,8},{10,11... | collective-permute-start | bytes 1769480 | tf_op jit(solution)/shard_map/ppermute | solution.py:790
  173.6 3.5 %collective-permute-start.10 = (bf16[8,112,384]{2,1,0:T(8,128)(2,1)S(1)}, bf16[8,112,384]{2,1,0:T(8,128)(2,1)S(1)}, u32[]{:S(2)}, u32[]{:S(2)}) collective-permute-start(bf16[8,112,384]{2,1,0:T(8,128)(2,1)S(1)} %bitcast.106), channel_id=1, source_target_pairs={{0,1},{1,0},{2,3},{3,2},{4,5},{5,4},{6,7},{7,6},{8,9},{9,8},{10,11... | collective-permute-start | bytes 2064392 | tf_op jit(solution)/shard_map/ppermute | solution.py:790
  (31 other events, 207.0 us)
where the time goes:
time: 179 us
  Pallas kernels  63.3 us (35%)
  waiting for transfers between devices  62.8 us (35%)
  starting transfers between devices  48.5 us (27%)
    pallas_call x10, Pallas kernels, run(): pl.pallas_call(body, out_shape=[jax.ShapeDtypeStruct(s, t) for s, t, _ in...  63.3 us
    ppermute x30, starting transfers between devices, swapped(): return lax.ppermute(x, 'dp', [(i, i ^ bits) for i in range(CUTS)])  34.2 us
    ppermute x30, waiting for transfers between devices, swapped(): return lax.ppermute(x, 'dp', [(i, i ^ bits) for i in range(CUTS)])  33.5 us
    ppermute x3, waiting for transfers between devices, advance(): return (lax.ppermute(send, 'section', [(0, 1), (1, 0)]), bufs)  29.2 us
    ppermute x3, starting transfers between devices, advance(): return (lax.ppermute(send, 'section', [(0, 1), (1, 0)]), bufs)  14.3 us
  transfers between devices with their start and end apart: 33, of which 15 were waited for; matrix products, arithmetic and copies ran while one was open for 1% of the time, Pallas kernels for 14%

commit v1 on v0

--- a/solution.py
+++ b/solution.py
@@ -14,7 +14,8 @@
 CUTS = 16
 F32 = jnp.float32
 BF16 = jnp.bfloat16
-VMEM_LIMIT = 28 * 2**20
+VMEM_LIMIT = 16 * 2**20
+BIG = 55 * 2**20
 
 
 def dot(a, b):
@@ -274,7 +275,7 @@
 STEPS = 3
 
 
-def run(body, ins, outs, scratch, aliases=None, us=1):
+def run(body, ins, outs, scratch, aliases=None, us=1, limit=VMEM_LIMIT):
     space = {"s": pltpu.SMEM, "v": pltpu.VMEM, "a": pl.ANY}
     return pl.pallas_call(
         body,
@@ -283,7 +284,7 @@
         out_specs=[pl.BlockSpec(memory_space=space[k]) for _, _, k in outs],
         scratch_shapes=scratch,
         input_output_aliases=aliases or {},
-        compiler_params=pltpu.CompilerParams(vmem_limit_bytes=VMEM_LIMIT),
+        compiler_params=pltpu.CompilerParams(vmem_limit_bytes=limit),
         cost_estimate=pl.CostEstimate(
             flops=us * 10**9, bytes_accessed=us * 2 * 10**6, transcendentals=0
         ),
@@ -300,9 +301,9 @@
 
 
 class Moves:
-    def __init__(self, sem):
+    def __init__(self, sem, used=0):
         self.sem = sem
-        self.used = 0
+        self.used = used
         self.made = {}
 
     def make(self, name, src, dst):
@@ -463,7 +464,7 @@
     scratch = [pltpu.VMEM(wshapes[n], BF16) for n in WEIGHTS]
     scratch += [pltpu.VMEM(*shapes[n]) for n in names]
     scratch += [pltpu.VMEM((slots, width), BF16)] * 3 + [pltpu.SemaphoreType.DMA((40,))]
-    got = run(body, ins, outs, scratch, {n_in + i: 1 + i for i in range(len(bufs))})
+    got = run(body, ins, outs, scratch, {n_in + i: 1 + i for i in range(len(bufs))}, us=15, limit=BIG)
     return got[0], tuple(got[1:])
 
 
@@ -471,78 +472,42 @@
     return moves.sem.at[list(moves.made).index(name)]
 
 
-def scatter_blocks(sem, me, blocks, keep_hbm, send_hbm):
-    for p in range(CUTS):
-        place = jnp.bitwise_xor(p, me)
-
-        @pl.when(jnp.bitwise_and(place, 1) == 0)
-        def _():
-            pltpu.make_async_copy(blocks.at[p], keep_hbm.at[place // 2], sem.at[p]).start()
-
-        @pl.when(jnp.bitwise_and(place, 1) == 1)
-        def _():
-            pltpu.make_async_copy(blocks.at[p], send_hbm.at[place // 2], sem.at[p]).start()
-
-    for p in range(CUTS):
-        pltpu.make_async_copy(blocks.at[p], keep_hbm.at[0], sem.at[p]).wait()
+class Scatter:
+    def __init__(self, sem, blocks, keep_hbm, send_hbm):
+        self.sem = sem
+        self.blocks = blocks
+        self.hbm = (keep_hbm, send_hbm)
+
+    def start(self, p, rows, base=0):
+        place = jnp.bitwise_xor(p, own_place())
+        sem = self.sem.at[base + p]
+        src = self.blocks.at[p, rows]
+        for side in (0, 1):
+
+            @pl.when(jnp.bitwise_and(place, 1) == side)
+            def _():
+                pltpu.make_async_copy(src, self.hbm[side].at[place // 2, rows], sem).start()
+
+    def finish(self, rows, base=0):
+        for p in range(CUTS):
+            src = self.blocks.at[p, rows]
+            pltpu.make_async_copy(src, self.hbm[0].at[0, rows], self.sem.at[base + p]).wait()
+
+
+def with_ones(rows):
+    return jnp.concatenate([rows, jnp.ones((16, rows.shape[1]), BF16)], 0)
 
 
 def own_place():
     return lax.axis_index("dp") if lax.axis_size("dp") == CUTS else 0
 
 
-def down_grads(z, dm, recv, dims):
-    slots, width, ff = dims
-    deep = width // 4
-
-    def body(z_hbm, dm_hbm, recv_hbm, keep, send, sums, z_ref, m, blocks, sem, sem2):
-        moves = Moves(sem)
-        lead = lax.axis_index("section") == 0
-        moves.start("m0", dm_hbm.at[0], m.at[0])
-        first = moves.make("m1", dm_hbm.at[1], m.at[1])
-        second = pltpu.make_async_copy(recv_hbm, m.at[1], sem.at[1])
-
-        @pl.when(lead)
-        def _():
-            second.start()
-
-        @pl.when(jnp.logical_not(lead))
-        def _():
-            first.start()
-
-        for i in (0, 1):
-            moves.start("z%d" % i, z_hbm.at[i], z_ref.at[i])
-        moves.wait("m0")
-        moves.wait("m1")
-        ones = jnp.ones((16, slots), BF16)
-        sums[...] = (dot(ones, m[0]) + dot(ones, m[1]))[:8]
-        turned = [m[i].T for i in (0, 1)]
-        moves.finish()
-        for j in range(4):
-            cols = slice(j * width, (j + 1) * width)
-            part = dot(turned[0], z_ref[0, :, cols]) + dot(turned[1], z_ref[1, :, cols])
-            blocks[4 * j : 4 * j + 4] = part.astype(BF16).reshape(4, deep, width)
-        scatter_blocks(sem2, own_place(), blocks, keep, send)
-
-    half = ((CUTS // 2, deep, width), BF16, "a")
-    scratch = [
-        pltpu.VMEM((2, slots, ff), BF16),
-        pltpu.VMEM((2, slots, width), BF16),
-        pltpu.VMEM((CUTS, deep, width), BF16),
-        pltpu.SemaphoreType.DMA((4,)),
-        pltpu.SemaphoreType.DMA((CUTS,)),
-    ]
-    ins = [(z, "a"), (dm, "a"), (recv, "a")]
-    return run(body, ins, [half, half, ((8, width), F32, "v")], scratch, us=4)
-
-
-def up_grads(lines, recv, weights, kept, dims):
+def mlp_grads(lines, recv, weights, kept, dims):
     slots, width, ff = dims
     deep = width // 4
     shapes = all_sizes(dims)
-    halves = (slice(0, slots), slice(slots, 2 * slots))
-    names = ("gp", "h", "du", "dp", "dh", "small", "dm")
-    given = ("gp", "h", "c", "du", "dp", "small")
+    names = ("gp", "h", "du", "dp", "dh", "small")
+    given = ("gp", "h", "c", "z", "dm", "du", "dp", "small")
     n_in = len(lines) + 3 + len(given)
 
     def body(*refs):
@@ -553,56 +518,112 @@
         rest = refs[n_in + 6 :]
         w = {"up": rest[0], "down": rest[1]}
         r = dict(zip(names, rest[2 : 2 + len(names)]))
-        c, d, blocks, sem, sem2 = rest[2 + len(names) :]
+        m, z, c, d, turned_ref, blocks, sem, sem2 = rest[2 + len(names) :]
         moves = Moves(sem)
+        inner = Moves(sem, 16)
         lead = lax.axis_index("section") == 0
-        for i, h in enumerate(halves):
-            moves.start("c%d" % i, hbm["c"].at[i], c.at[h])
-        moves.start("d0", hbm["du"].at[0], d.at[0])
-        own = moves.make("d1", hbm["du"].at[1], d.at[1])
-
-        @pl.when(jnp.logical_not(lead))
-        def _():
-            own.start()
-            own.wait()
+        other = jnp.logical_not(lead)
+        half = [slice(0, slots), slice(slots, 2 * slots)]
+        m1 = moves.make("m1", hbm["dm"].at[1], m.at[half[1]])
+        m1_recv = pltpu.make_async_copy(recv_hbm, m.at[half[1]], sem.at[0])
+        d1 = moves.make("d1", hbm["du"].at[1], d.at[half[1]])
+        moves.made.pop("d1")
+        early = [
+            inner.make("down", down_hbm.at[0], w["down"]),
+            inner.make("gp", hbm["gp"].at[1], r["gp"]),
+            inner.make("up", up_hbm.at[0], w["up"]),
+            inner.make("h", hbm["h"].at[1], r["h"]),
+        ]
+        late = {
+            "dp": inner.make("save dp", r["dp"], dp_hbm.at[1]),
+            "small": inner.make("save small", r["small"], small_hbm.at[1]),
+            "dh": inner.make("save dh", r["dh"], dh_hbm),
+        }
 
         @pl.when(lead)
         def _():
-            inner = Moves(sem.at[pl.ds(4, 12)])
-            inner.start("dm", recv_hbm, r["dm"])
-            inner.start("down", down_hbm.at[0], w["down"])
-            inner.start("gp", hbm["gp"].at[1], r["gp"])
-            inner.start("up", up_hbm.at[0], w["up"])
-            inner.start("h", hbm["h"].at[1], r["h"])
-            inner.wait("dm")
-            out = {"dp": dp_hbm.at[1]}
-
+            m1_recv.start()
+
+        @pl.when(other)
+        def _():
+            m1.start()
+
+        moves.start("m0", hbm["dm"].at[0], m.at[half[0]])
+        for i in (0, 1):
+            moves.start("z%d" % i, hbm["z"].at[i], z.at[half[i]])
+
+        @pl.when(other)
+        def _():
+            d1.start()
+
+        @pl.when(lead)
+        def _():
+            for copy in early:
+                copy.start()
+
+        for i in (0, 1):
+            moves.start("c%d" % i, hbm["c"].at[i], c.at[half[i]])
+        moves.start("d0", hbm["du"].at[0], d.at[half[0]])
+        scatter = Scatter(sem2, blocks, keep, send)
+        upper, lower = slice(0, deep), slice(deep, 2 * deep)
+        moves.wait("m1")
+        moves.wait("m0")
+        turned = m[...].T
+        sums[4] = dot(jnp.ones((16, 2 * slots), BF16), m[...])[:8]
+        turned_ref[:width] = turned
+        moves.wait("z0")
+        moves.wait("z1")
+
+        def down_part(j, carry):
+            cols = pl.ds(pl.multiple_of(j * width, width), width)
+            part = dot(turned_ref[:width], z[:, cols]).astype(BF16)
+            blocks[pl.ds(4 * j, 4), upper] = part.reshape(4, deep, width)
+            for i in range(4):
+                scatter.start(4 * j + i, upper)
+            return carry
+
+        lax.fori_loop(0, 4, down_part, 0)
+
+        @pl.when(other)
+        def _():
+            d1.wait()
+
+        @pl.when(lead)
+        def _():
             def done(n):
-                if n in out:
-                    inner.start("save " + n, r[n], out[n])
-
-            r["du"] = d.at[1]
-            backward_mlp(r["dm"], vec, w, r, inner.wait, done)
-            inner.start("save small", r["small"], small_hbm.at[1])
-            inner.start("save dh", r["dh"], dh_hbm)
-            inner.finish()
-
-        for n in ("c0", "c1", "d0"):
-            moves.wait(n)
-        ones = jnp.ones((16, slots), BF16)
-        turned = [c[h, :].T for h in halves]
-        for j in range(4):
-            cols = slice(j * width, (j + 1) * width)
-            parts = [d[i, :, cols] for i in (0, 1)]
-            sums[j] = (dot(ones, parts[0]) + dot(ones, parts[1]))[:8]
-            part = (dot(turned[0], parts[0]) + dot(turned[1], parts[1])).astype(BF16)
-            blocks[4 * j : 4 * j + 4] = part.reshape(4, deep, width)
-        scatter_blocks(sem2, own_place(), blocks, keep, send)
-
-    half = ((CUTS // 2, deep, width), BF16, "a")
+                if n == "dp":
+                    late[n].start()
+
+            r["du"] = d.at[half[1]]
+            backward_mlp(m.at[half[1]], vec, w, r, inner.wait, done)
+            late["small"].start()
+            late["dh"].start()
+
+        moves.finish()
+        turned_ref[...] = with_ones(c[...].T)
+
+        def up_part(j, carry):
+            cols = pl.ds(pl.multiple_of(j * width, width), width)
+            part = dot(turned_ref[...], d[:, cols])
+            sums[j] = part[width : width + 8]
+            blocks[pl.ds(4 * j, 4), lower] = part[:width].astype(BF16).reshape(4, deep, width)
+            for i in range(4):
+                scatter.start(4 * j + i, lower, CUTS)
+            return carry
+
+        lax.fori_loop(0, 4, up_part, 0)
+        scatter.finish(upper)
+        scatter.finish(lower, CUTS)
+
+        @pl.when(lead)
+        def _():
+            for copy in late.values():
+                copy.wait()
+
+    half = ((CUTS // 2, 2 * deep, width), BF16, "a")
     ins = [(v, "v") for v in lines] + [(recv, "a"), (weights[2], "a"), (weights[3], "a")]
     ins += [(kept[n], "a") for n in given]
-    outs = [half, half, ((4, 8, width), F32, "v")]
+    outs = [half, half, ((5, 8, width), F32, "v")]
     outs += [(kept[n].shape, kept[n].dtype, "a") for n in ("dp", "small")]
     outs += [((slots, width), F32, "a")]
     wshapes = weight_sizes(width, ff)
@@ -610,15 +631,18 @@
     scratch += [pltpu.VMEM(*shapes[n]) for n in names]
     scratch += [
         pltpu.VMEM((2 * slots, width), BF16),
-        pltpu.VMEM((2, slots, ff), BF16),
-        pltpu.VMEM((CUTS, deep, width), BF16),
-        pltpu.SemaphoreType.DMA((16,)),
-        pltpu.SemaphoreType.DMA((CUTS,)),
+        pltpu.VMEM((2 * slots, ff), BF16),
+        pltpu.VMEM((2 * slots, width), BF16),
+        pltpu.VMEM((2 * slots, ff), BF16),
+        pltpu.VMEM((width + 16, 2 * slots), BF16),
+        pltpu.VMEM((CUTS, 2 * deep, width), BF16),
+        pltpu.SemaphoreType.DMA((24,)),
+        pltpu.SemaphoreType.DMA((2 * CUTS,)),
     ]
-    return run(body, ins, outs, scratch, {n_in - 2: 3, n_in - 1: 4}, us=6)
-
-
-def attention_grads(lines, tokens, weights, kept, dh, grads, down_sums, up_sums, dims):
+    return run(body, ins, outs, scratch, {n_in - 2: 3, n_in - 1: 4}, us=12, limit=BIG)
+
+
+def attention_grads(lines, tokens, weights, kept, dh, grads, sums, dims):
     slots, width, ff = dims
     deep = width // 4
     tall = deep + 16
@@ -629,42 +653,61 @@
     )
     loads = ("inv", "v", "e", "kt", "qt")
     given = ("a", "ot", "dp", "dqkv", "small") + loads
-    n_in = len(lines) + 7 + len(given)
+    n_in = len(lines) + 6 + len(given)
 
     def body(*refs):
         vec = dict(zip(LINES, refs[: len(lines)]))
-        tokens_hbm, out_hbm, qkv_hbm, dh_hbm, grads_in, down_ref, up_ref = refs[
-            len(lines) : len(lines) + 7
+        tokens_hbm, out_hbm, qkv_hbm, dh_hbm, grads_in, sums_ref = refs[
+            len(lines) : len(lines) + 6
         ]
-        hbm = dict(zip(given, refs[len(lines) + 7 : n_in]))
+        hbm = dict(zip(given, refs[len(lines) + 6 : n_in]))
         keep, send, grads_hbm = refs[n_in : n_in + 3]
         rest = refs[n_in + 3 :]
         w = {"out": rest[0], "qkv": rest[1]}
         r = dict(zip(names, rest[2 : 2 + len(names)]))
-        x, a, d, o, p, s, blocks, sem, sem2 = rest[2 + len(names) :]
+        x, a, d, o, p, s, turned_ref, lines_ref, blocks, sem, sem2 = rest[2 + len(names) :]
         moves = Moves(sem)
+        inner = Moves(sem, 12)
         lead = lax.axis_index("section") == 0
-        moves.start("p1", hbm["dp"].at[1], p.at[1])
-        moves.start("o1", hbm["ot"].at[1], o.at[1])
-        moves.start("s1", hbm["small"].at[1], s.at[1])
-        own = moves.make("d1", hbm["dqkv"].at[1], d.at[1])
-
-        @pl.when(jnp.logical_not(lead))
+        other = jnp.logical_not(lead)
+        half = [slice(0, slots), slice(slots, 2 * slots)]
+        place = {
+            "dp": lambda i: p.at[half[i]],
+            "a": lambda i: a.at[half[i]],
+            "ot": lambda i: o.at[:, :, half[i]],
+            "dqkv": lambda i: d.at[:, :, :, half[i]],
+            "small": lambda i: s.at[i],
+        }
+        for n in ("dp", "ot", "small"):
+            moves.start(n + "1", hbm[n].at[1], place[n](1))
+        own = moves.make("dqkv1", hbm["dqkv"].at[1], place["dqkv"](1))
+        early = [inner.make("out", out_hbm.at[0], w["out"])]
+        early += [inner.make(n, hbm[n].at[1], r[n]) for n in loads]
+        early += [
+            inner.make("qkv", qkv_hbm.at[0], w["qkv"]),
+            inner.make("x", tokens_hbm.at[1, 0], x),
+            inner.make("dh", dh_hbm, r["dh"]),
+        ]
+        g_copy = inner.make("g", x, grads_hbm.at[1])
+
+        @pl.when(other)
         def _():
             own.start()
 
         @pl.when(lead)
         def _():
-            inner = Moves(sem.at[pl.ds(12, 12)])
-            inner.start("out", out_hbm.at[0], w["out"])
-            for n in loads:
-                inner.start(n, hbm[n].at[1], r[n])
-            inner.start("qkv", qkv_hbm.at[0], w["qkv"])
-            inner.start("x", tokens_hbm.at[1, 0], x)
-            inner.start("dh", dh_hbm, r["dh"])
-            for n in ("p1", "o1", "s1"):
-                moves.made[n].wait()
-            r.update(dp=p.at[1], ot=o.at[1], dqkv=d.at[1], small=s.at[1])
+            for copy in early:
+                copy.start()
+
+        for n in ("a", "dqkv", "ot", "dp", "small"):
+            moves.start(n + "0", hbm[n].at[0], place[n](0))
+        moves.start("a1", hbm["a"].at[1], place["a"](1))
+        for n in ("dp1", "ot1", "small1"):
+            moves.wait(n)
+
+        @pl.when(lead)
+        def _():
+            r.update({n: place[n](1) for n in ("dp", "ot", "dqkv", "small")})
 
             def wait(n):
                 if n == "qkv":
@@ -673,62 +716,70 @@
                 inner.wait(n)
 
             backward_attention(x, x, vec, w, r, wait, nothing)
-            inner.start("g", x, grads_hbm.at[1])
-            inner.finish()
-
-        @pl.when(jnp.logical_not(lead))
-        def _():
-            for n in ("p1", "o1", "s1", "d1"):
-                moves.made[n].wait()
-
-        for n in ("p1", "o1", "s1", "d1"):
-            moves.made.pop(n)
-        moves.start("p0", hbm["dp"].at[0], p.at[0])
-        moves.start("o0", hbm["ot"].at[0], o.at[0])
-        moves.start("s0", hbm["small"].at[0], s.at[0])
-        moves.start("d0", hbm["dqkv"].at[0], d.at[0])
-        moves.start("a0", hbm["a"].at[0], a.at[0])
-        moves.start("a1", hbm["a"].at[1], a.at[1])
+            g_copy.start()
+
+        @pl.when(other)
+        def _():
+            own.wait()
+
+        moves.made.pop("dqkv1")
         moves.finish()
-        ones = jnp.ones((16, slots), BF16)
-        turned = [a[i].T for i in (0, 1)]
+        scatter = Scatter(sem2, blocks, keep, send)
+        full, deep_rows = slice(0, tall), slice(0, deep)
+        turned_ref[...] = with_ones(a[...].T)
+
+        def qkv_part(j, carry):
+            part = dot_nt(turned_ref[...], d[j].reshape(width, 2 * slots))
+            lines_ref[j] = part[width : width + 8]
+            part = part[:width].astype(BF16).reshape(4, deep, width)
+            blocks[pl.ds(4 * j, 4), deep_rows] = part
+            return carry
+
+        lax.fori_loop(0, 3, qkv_part, 0)
+        part = dot(with_ones(o[...].reshape(width, 2 * slots).astype(BF16)), p[...])
+        blocks[12:16, deep_rows] = part[:width].astype(BF16).reshape(4, deep, width)
         both = s[0] + s[1]
         rows = [
-            both[A_GAIN_G : A_GAIN_G + 1], both[A_SHIFT_G : A_SHIFT_G + 1], None, None,
-            (dot(ones, p[0]) + dot(ones, p[1]))[:1],
+            both[A_GAIN_G : A_GAIN_G + 1], both[A_SHIFT_G : A_SHIFT_G + 1],
+            lines_ref[0, :1], lines_ref[2, :1],
+            part[width : width + 1],
             both[M_GAIN_G : M_GAIN_G + 1], both[M_SHIFT_G : M_SHIFT_G + 1],
-            down_ref[:1], up_ref[0, :1], up_ref[1, :1], up_ref[2, :1], up_ref[3, :1],
+            *[sums_ref[i, :1] for i in (4, 0, 1, 2, 3)],
         ]
-        for j in range(3):
-            parts = [d[i, j].reshape(width, slots) for i in (0, 1)]
-            if j != 1:
-                rows[2 + j // 2] = (dot_nt(ones, parts[0]) + dot_nt(ones, parts[1]))[:1]
-            part = (dot_nt(turned[0], parts[0]) + dot_nt(turned[1], parts[1])).astype(BF16)
-            blocks[4 * j : 4 * j + 4, :deep] = part.reshape(4, deep, width)
-        mixed = [o[i].reshape(width, slots).astype(BF16) for i in (0, 1)]
-        part = dot(mixed[0], p[0]) + dot(mixed[1], p[1])
-        blocks[12:16, :deep] = part.astype(BF16).reshape(4, deep, width)
         for i in range(CUTS):
             line = rows[i] if i < 12 else jnp.zeros((1, width), F32)
             blocks[i, deep:] = jnp.broadcast_to(line, (16, width)).astype(BF16)
-        scatter_blocks(sem2, own_place(), blocks, keep, send)
+            scatter.start(i, full)
+        scatter.finish(full)
+
+        @pl.when(lead)
+        def _():
+            g_copy.wait()
 
     ins = [(v, "v") for v in lines] + [(tokens, "a"), (weights[1], "a"), (weights[0], "a")]
-    ins += [(dh, "a"), (grads, "a"), (down_sums, "v"), (up_sums, "v")]
+    ins += [(dh, "a"), (grads, "a"), (sums, "v")]
     ins += [(kept[n], "a") for n in given]
     half = ((CUTS // 2, tall, width), BF16, "a")
     outs = [half, half, (grads.shape, grads.dtype, "a")]
     wshapes = weight_sizes(width, ff)
     scratch = [pltpu.VMEM(wshapes["out"], BF16), pltpu.VMEM(wshapes["qkv"], BF16)]
     scratch += [pltpu.VMEM(*shapes[n]) for n in names]
-    scratch += [pltpu.VMEM((slots, width), BF16)]
-    scratch += [pltpu.VMEM((2, *shapes[n][0]), shapes[n][1]) for n in ("a", "dqkv", "ot", "dp", "small")]
+    scratch += [
+        pltpu.VMEM((slots, width), BF16),
+        pltpu.VMEM((2 * slots, width), BF16),
+        pltpu.VMEM((3, HEADS, HEAD, 2 * slots), BF16),
+        pltpu.VMEM((HEADS, HEAD, 2 * slots), F32),
+        pltpu.VMEM((2 * slots, width), BF16),
+        pltpu.VMEM((2, 8, width), F32),
+        pltpu.VMEM((width + 16, 2 * slots), BF16),
+        pltpu.VMEM((3, 8, width), F32),
+    ]
     scratch += [
         pltpu.VMEM((CUTS, tall, width), BF16),
         pltpu.SemaphoreType.DMA((24,)),
         pltpu.SemaphoreType.DMA((CUTS,)),
     ]
-    return run(body, ins, outs, scratch, {len(lines) + 4: 2}, us=12)
+    return run(body, ins, outs, scratch, {len(lines) + 4: 2}, us=12, limit=BIG)
 
 
 def block(own, other, p):
@@ -739,29 +790,20 @@
     return jnp.where(odd == 1, theirs, mine).astype(F32)
 
 
-def down_out(own, other, dims):
+def mlp_out(own, other, dims):
     slots, width, ff = dims
-
-    def body(own_ref, other_ref, out):
+    deep = width // 4
+
+    def body(own_ref, other_ref, down, up):
         for j in range(4):
             part = [block(own_ref, other_ref, 4 * j + i) for i in range(4)]
-            out[0, j * width : (j + 1) * width, :] = jnp.concatenate(part, 0).T
-
-    return run(body, [(own, "v"), (other, "v")], [((1, ff, width), F32, "v")], [], us=3)[0]
-
-
-def up_out(own, other, dims):
-    slots, width, ff = dims
-    deep = width // 4
-
-    def body(own_ref, other_ref, out):
-        for p in range(CUTS):
-            j, i = p // 4, p % 4
-            out[0, i * deep : (i + 1) * deep, j * width : (j + 1) * width] = block(
-                own_ref, other_ref, p
-            )
-
-    return run(body, [(own, "v"), (other, "v")], [((1, width, ff), F32, "v")], [], us=3)[0]
+            down[0, j * width : (j + 1) * width, :] = jnp.concatenate(
+                [v[:deep] for v in part], 0
+            ).T
+            up[0, :, j * width : (j + 1) * width] = jnp.concatenate([v[deep:] for v in part], 0)
+
+    outs = [((1, ff, width), F32, "v"), ((1, width, ff), F32, "v")]
+    return run(body, [(own, "v"), (other, "v")], outs, [], us=4)
 
 
 def attention_out(own, other, dims):
@@ -797,17 +839,16 @@
     return total.astype(BF16)
 
 
-def all_reduced(keep, send):
-    if lax.axis_size("dp") != CUTS:
-        return lax.psum(keep, "dp"), lax.psum(send, "dp")
-    u = added(keep, swapped(send, 1))
-    u = u.reshape(4, 2, *u.shape[1:])
-    u = added(u[:, 0], swapped(u[:, 1], 2))
-    u = added(u[0], *[swapped(u[j], 4 * j) for j in (1, 2, 3)])
-    u = jnp.stack([u] + [swapped(u, 4 * j) for j in (1, 2, 3)])
-    u = jnp.stack([u, swapped(u, 2)], 1)
-    u = u.reshape(8, *u.shape[2:])
-    return u, swapped(u, 1)
+def tied(token, *xs):
+    return lax.optimization_barrier((token, *xs))[1:]
+
+
+def square_send(u):
+    return [swapped(u[:, j], 2 * j) for j in (1, 2, 3)]
+
+
+def square_gather(u):
+    return [swapped(u, 2 * j) for j in (1, 2, 3)]
 
 
 def shards(
@@ -830,17 +871,40 @@
     recv, bufs = lax.fori_loop(0, STEPS, advance, blank(dims))
     outs, grads = bufs[:2]
     kept = dict(zip(SAVED + TERMS, bufs[2:]))
-    keep, send, down_sums = down_grads(kept["z"], kept["dm"], recv, dims)
-    down_sum = all_reduced(keep, send)
-    keep, send, up_sums, kept["dp"], kept["small"], dh = up_grads(lines, recv, weights, kept, dims)
-    up_sum = all_reduced(keep, send)
-    keep, send, grads = attention_grads(
-        lines, tokens, weights, kept, dh, grads, down_sums, up_sums, dims
+    m_keep, m_send, sums, kept["dp"], kept["small"], dh = mlp_grads(
+        lines, recv, weights, kept, dims
     )
-    attention_sum = all_reduced(keep, send)
-    g_down = down_out(*down_sum, dims)
-    g_up = up_out(*up_sum, dims)
-    g_qkv, g_out, *rows = attention_out(*attention_sum, dims)
+    if lax.axis_size("dp") != CUTS:
+        a_keep, a_send, grads = attention_grads(lines, tokens, weights, kept, dh, grads, sums, dims)
+        m, m_other, a, a_other = lax.psum((m_keep, m_send, a_keep, a_send), "dp")
+    else:
+        m = added(m_keep, swapped(m_send, 1)).reshape(2, 4, *m_keep.shape[1:])
+        m1 = square_send(m)
+        (dh,) = tied(m, dh)
+        a_keep, a_send, grads = attention_grads(lines, tokens, weights, kept, dh, grads, sums, dims)
+        a_got = jnp.concatenate([swapped(v, 1) for v in jnp.split(a_send, 2)], 0)
+        m1 = tied(a_keep, *m1)
+        m = added(m[:, 0], *m1)
+        m2 = swapped(m, 8)
+        (a_got,) = tied(m, a_got)
+        a = added(a_keep, a_got).reshape(2, 4, *a_keep.shape[1:])
+        a1 = square_send(a)
+        m2, *a1 = lax.optimization_barrier((m2, *a1))
+        m = added(m, m2[::-1])
+        m1 = square_gather(m)
+        a = added(a[:, 0], *a1)
+        a2 = swapped(a, 8)
+        (a2,) = tied(m, a2)
+        a = added(a, a2[::-1])
+        a1 = square_gather(a)
+        m1 = tied(a, *m1)
+        m = jnp.stack([m, *m1], 1).reshape(8, *m.shape[1:])
+        m_other = swapped(m, 1)
+        a1 = tied(m, *a1)
+        a = jnp.stack([a, *a1], 1).reshape(8, *a.shape[1:])
+        a_other = swapped(a, 1)
+    g_down, g_up = mlp_out(m, m_other, dims)
+    g_qkv, g_out, *rows = attention_out(a, a_other, dims)
     g_ag, g_as, g_qb, g_vb, g_ob, g_mg, g_ms, g_db, g_ub = rows
     return (
         outs[None, :, None], grads[None, :, None], g_ag, g_as, g_qkv, g_qb, g_vb, g_out, g_ob,

time: 179 us -> 166 us (0.927)
  starting transfers between devices: 48.5 us -> 33.8 us
  Pallas kernels: 63.3 us -> 59.2 us
  waiting for transfers between devices: 62.8 us -> 65.4 us
    ppermute x30 -> x19, starting transfers between devices: 34.2 us -> 18.8 us  [swapped(): return lax.ppermute(x, 'dp', [(i, i ^ bits) for i in range(CUTS)])]
    pallas_call x10 -> x8, Pallas kernels: 63.3 us -> 59.2 us  [run(): pl.pallas_call(body, out_shape=[jax.ShapeDtypeStruct(s, t) for s, t, _ in...]
    ppermute x30 -> x19, waiting for transfers between devices: 33.5 us -> 35.5 us  [swapped(): return lax.ppermute(x, 'dp', [(i, i ^ bits) for i in range(CUTS)])]
  transfers between devices with their start and end apart: 33 -> 22, of which waited for: 15 -> 12; matrix products, arithmetic and copies ran while one was open for 1% -> 1% of each run, Pallas kernels for 14% -> 8%
where the time goes in v1:
time: 166 us; the launch traced here: 165 us
  waiting for transfers between devices  65.4 us (39%)
  Pallas kernels  59.2 us (36%)
  starting transfers between devices  33.8 us (20%)
  local copies, waits for them, and re-layouts  3.32 us (2%)
  other arithmetic  2.62 us (2%)
    pallas_call x8, Pallas kernels, run(): pl.pallas_call(body, out_shape=[jax.ShapeDtypeStruct(s, t) for s, t, _ in...  59.2 us
    ppermute x19, waiting for transfers between devices, swapped(): return lax.ppermute(x, 'dp', [(i, i ^ bits) for i in range(CUTS)])  35.5 us
    ppermute x3, waiting for transfers between devices, advance(): return (lax.ppermute(send, 'section', [(0, 1), (1, 0)]), bufs)  29.8 us
    ppermute x19, starting transfers between devices, swapped(): return lax.ppermute(x, 'dp', [(i, i ^ bits) for i in range(CUTS)])  18.8 us
    ppermute x3, starting transfers between devices, advance(): return (lax.ppermute(send, 'section', [(0, 1), (1, 0)]), bufs)  15 us
  transfers between devices with their start and end apart: 22, of which 12 were waited for; matrix products, arithmetic and copies ran while one was open for 1% of the time, Pallas kernels for 8%

profile of v1, /device:TPU:0, one launch (start us, length us, event | category | flops | bytes accessed | tf_op | source)
XLA Modules:
  0.0 165.4 jit_solution(10119320702947630086)
XLA Ops:
  0.7 1.4 copy.52
  2.7 75.6 %while.49 = (s32[]{:T(128)}, bf16[512,384]{1,0:T(8,128)(2,1)}, bf16[2,512,384]{2,1,0:T(8,128)(2,1)}, bf16[2,512,384]{2,1,0:T(8,128)(2,1)}, bf16[2,512,384]{2,1,0...) while((s32[]{:T(128)}, bf16[512,384]{1,0:T(8,128)(2,1)}, ...), condition=%wide.region_1.0_spmd, body=%wide.region_0.0_spmd.sunk | while | flops 15000000512 | bytes 31573220 | solution.py:871
  2.7 10.1 %eval_jaxpr.5 = (bf16[512,384]{1,0:T(8,128)(2,1)}, bf16[2,512,384]{2,1,0:T(8,128)(2,1)}, bf16[2,512,384]{2,1,0:T(8,128)(2,1)}, bf16[2,512,384]{2,1,0:T(8,128)(2,...) custom-call(s32[1]{0:T(128)} %bitcast.68.refs_0_, ...), custom_call_target="tpu_custom_call", output_to_operand_aliasing={{1}: (18, {}), {2}: (19, {}), {3}: (20, {}), {4}: (21, {}),... | custom-call | flops 15000000512 | bytes 30000000 | tf_op jit(solution)/shard_map/while/body/eval_jaxpr/pallas_call | solution.py:280
  12.8 11.8 %collective-permute-done = bf16[512,384]{1,0:T(8,128)(2,1)} collective-permute-done((bf16[512,384]{1,0:T(8,128)(2,1)}, bf16[512,384]{1,0:T(8,128)(2,1)}, u32[]{:S(2)}, u32[]{:S(2)}) %collective-permute-start) | collective-permute-done | bytes 393248 | tf_op jit(solution)/shard_map/while/body/eval_jaxpr/ppermute | solution.py:869
  24.6 10.1 %eval_jaxpr.5 = (bf16[512,384]{1,0:T(8,128)(2,1)}, bf16[2,512,384]{2,1,0:T(8,128)(2,1)}, bf16[2,512,384]{2,1,0:T(8,128)(2,1)}, bf16[2,512,384]{2,1,0:T(8,128)(2,...) custom-call(s32[1]{0:T(128)} %bitcast.68.refs_0_, ...), custom_call_target="tpu_custom_call", output_to_operand_aliasing={{1}: (18, {}), {2}: (19, {}), {3}: (20, {}), {4}: (21, {}),... | custom-call | flops 15000000512 | bytes 30000000 | tf_op jit(solution)/shard_map/while/body/eval_jaxpr/pallas_call | solution.py:280
  34.7 7.0 %collective-permute-start = (bf16[512,384]{1,0:T(8,128)(2,1)}, bf16[512,384]{1,0:T(8,128)(2,1)}, u32[]{:S(2)}, u32[]{:S(2)}) collective-permute-start(bf16[512,384]{1,0:T(8,128)(2,1)} %get-tuple-element.1058), channel_id=1, source_target_pairs={{0,16},{16,0},{1,17},{17,1},{2,18},{18,2},{3,19},{19,3},{4,20},{20... | collective-permute-start | bytes 1179656 | tf_op jit(solution)/shard_map/while/body/eval_jaxpr/ppermute | solution.py:869
  41.7 9.5 %collective-permute-done = bf16[512,384]{1,0:T(8,128)(2,1)} collective-permute-done((bf16[512,384]{1,0:T(8,128)(2,1)}, bf16[512,384]{1,0:T(8,128)(2,1)}, u32[]{:S(2)}, u32[]{:S(2)}) %collective-permute-start) | collective-permute-done | bytes 393248 | tf_op jit(solution)/shard_map/while/body/eval_jaxpr/ppermute | solution.py:869
  51.1 10.5 %eval_jaxpr.5 = (bf16[512,384]{1,0:T(8,128)(2,1)}, bf16[2,512,384]{2,1,0:T(8,128)(2,1)}, bf16[2,512,384]{2,1,0:T(8,128)(2,1)}, bf16[2,512,384]{2,1,0:T(8,128)(2,...) custom-call(s32[1]{0:T(128)} %bitcast.68.refs_0_, ...), custom_call_target="tpu_custom_call", output_to_operand_aliasing={{1}: (18, {}), {2}: (19, {}), {3}: (20, {}), {4}: (21, {}),... | custom-call | flops 15000000512 | bytes 30000000 | tf_op jit(solution)/shard_map/while/body/eval_jaxpr/pallas_call | solution.py:280
  61.7 8.0 %collective-permute-start = (bf16[512,384]{1,0:T(8,128)(2,1)}, bf16[512,384]{1,0:T(8,128)(2,1)}, u32[]{:S(2)}, u32[]{:S(2)}) collective-permute-start(bf16[512,384]{1,0:T(8,128)(2,1)} %get-tuple-element.1058), channel_id=1, source_target_pairs={{0,16},{16,0},{1,17},{17,1},{2,18},{18,2},{3,19},{19,3},{4,20},{20... | collective-permute-start | bytes 1179656 | tf_op jit(solution)/shard_map/while/body/eval_jaxpr/ppermute | solution.py:869
  69.7 8.6 %collective-permute-done = bf16[512,384]{1,0:T(8,128)(2,1)} collective-permute-done((bf16[512,384]{1,0:T(8,128)(2,1)}, bf16[512,384]{1,0:T(8,128)(2,1)}, u32[]{:S(2)}, u32[]{:S(2)}) %collective-permute-start) | collective-permute-done | bytes 393248 | tf_op jit(solution)/shard_map/while/body/eval_jaxpr/ppermute | solution.py:869
  78.3 12.4 %shard_map.272 = (bf16[8,192,384]{2,1,0:T(8,128)(2,1)}, bf16[8,192,384]{2,1,0:T(8,128)(2,1)}, f32[5,8,384]{2,1,0:T(8,128)}, bf16[2,512,384]{2,1,0:T(8,128)(2,1)}...) custom-call(bf16[1,384]{1,0:T(2,128)(2,1)S(1)} %get-tuple-element.1233, ...), custom_call_target="tpu_custom_call", output_to_operand_aliasing={{3}: (18, {}), {4}: (19, {})} | custom-call | flops 12000000000 | bytes 24000000 | tf_op jit(solution)/shard_map/pallas_call | solution.py:280
  90.7 3.0 %collective-permute-done.1 = bf16[8,192,384]{2,1,0:T(8,128)(2,1)S(1)} collective-permute-done((bf16[8,192,384]{2,1,0:T(8,128)(2,1)}, bf16[8,192,384]{2,1,0:T(8,128)(2,1)S(1)}, u32[]{:S(2)}, u32[]{:S(2)}) %collective-permute-start.1) | collective-permute-done | bytes 1179680 | tf_op jit(solution)/shard_map/ppermute | solution.py:832
  93.8 1.7 %add_convert_fusion = bf16[8,192,384]{2,1,0:T(8,128)(2,1)S(1)} fusion(bf16[8,192,384]{2,1,0:T(8,128)(2,1)S(1)} %collective-permute-done.1, bf16[8,192,384]{2,1,0:T(8,128)(2,1)} %get-tuple-element.644), kind=kLoop, calls=%fused_computation | loop fusion | flops 2359296 | bytes 3538944 | tf_op jit(solution)/shard_map/convert_element_type | solution.py:839
  95.7 2.2 %collective-permute-start.4 = (bf16[2,192,384]{2,1,0:T(8,128)(2,1)S(1)}, bf16[2,192,384]{2,1,0:T(8,128)(2,1)S(1)}, u32[]{:S(2)}, u32[]{:S(2)}) collective-permute-start(bf16[2,192,384]{2,1,0:T(8,128)(2,1)S(1)} %get-tuple-element.814), channel_id=1, source_target_pairs={{0,6},{1,7},{2,4},{3,5},{4,2},{5,3},{6,0},{7,1},{8,14},{9,15},{10,... | collective-permute-start | bytes 884744 | tf_op jit(solution)/shard_map/ppermute | solution.py:832
  99.3 11.9 %shard_map.273 = (bf16[8,112,384]{2,1,0:T(8,128)(2,1)}, bf16[8,112,384]{2,1,0:T(8,128)(2,1)}, bf16[2,512,384]{2,1,0:T(8,128)(2,1)}) custom-call(bf16[1,384]{1,0:T(2,128)(2,1)S(1)} %get-tuple-element.1233, bf16[1,384]{1,0:T(2,128)(2,1)S(1)} %get-tuple-element.1234, bf16[1,384]{1,0:T(2,128)(2,1)S(1)} %copy-done.9, ...), custom_call_target="tpu_custom_call", output_to_operand_aliasing={{2}: (13, {})} | custom-call | flops 12000000000 | bytes 24000000 | tf_op jit(solution)/shard_map/pallas_call | solution.py:280
  113.2 2.3 %collective-permute-start.7 = (bf16[2,192,384]{2,1,0:T(8,128)(2,1)S(1)}, bf16[2,192,384]{2,1,0:T(8,128)(2,1)S(1)}, u32[]{:S(2)}, u32[]{:S(2)}) collective-permute-start(bf16[2,192,384]{2,1,0:T(8,128)(2,1)S(1)} %fusion.2), channel_id=1, source_target_pairs={{0,8},{1,9},{2,10},{3,11},{4,12},{5,13},{6,14},{7,15},{8,0},{9,1},... | collective-permute-start | bytes 884744 | tf_op jit(solution)/shard_map/ppermute | solution.py:832
  115.8 2.6 %collective-permute-start.10 = (bf16[2,112,384]{2,1,0:T(8,128)(2,1)S(1)}, bf16[2,112,384]{2,1,0:T(8,128)(2,1)S(1)}, u32[]{:S(2)}, u32[]{:S(2)}) collective-permute-start(bf16[2,112,384]{2,1,0:T(8,128)(2,1)S(1)} %get-tuple-element.817), channel_id=1, source_target_pairs={{0,6},{1,7},{2,4},{3,5},{4,2},{5,3},{6,0},{7,1},{8,14},{9,15},{10,... | collective-permute-start | bytes 516104 | tf_op jit(solution)/shard_map/ppermute | solution.py:832
  119.3 7.3 %collective-permute-done.10 = bf16[2,112,384]{2,1,0:T(8,128)(2,1)S(1)} collective-permute-done((bf16[2,112,384]{2,1,0:T(8,128)(2,1)S(1)}, bf16[2,112,384]{2,1,0:T(8,128)(2,1)S(1)}, u32[]{:S(2)}, u32[]{:S(2)}) %collective-permute-start.10) | collective-permute-done | bytes 172064 | tf_op jit(solution)/shard_map/ppermute | solution.py:832
  126.6 5.6 %collective-permute-done.9 = bf16[2,112,384]{2,1,0:T(8,128)(2,1)S(1)} collective-permute-done((bf16[2,112,384]{2,1,0:T(8,128)(2,1)S(1)}, bf16[2,112,384]{2,1,0:T(8,128)(2,1)S(1)}, u32[]{:S(2)}, u32[]{:S(2)}) %collective-permute-start.9) | collective-permute-done | bytes 172064 | tf_op jit(solution)/shard_map/ppermute | solution.py:832
  132.3 1.5 collective-permute-start.11
  133.9 2.5 %collective-permute-start.14 = (bf16[2,192,384]{2,1,0:T(8,128)(2,1)S(1)}, bf16[2,192,384]{2,1,0:T(8,128)(2,1)S(1)}, u32[]{:S(2)}, u32[]{:S(2)}) collective-permute-start(bf16[2,192,384]{2,1,0:T(8,128)(2,1)S(1)} %add_convert_fusion.2), channel_id=1, source_target_pairs={{0,6},{1,7},{2,4},{3,5},{4,2},{5,3},{6,0},{7,1},{8,14},{9,15},{10,... | collective-permute-start | bytes 884744 | tf_op jit(solution)/shard_map/ppermute | solution.py:832
  136.5 1.4 collective-permute-start.12
  137.9 4.3 %collective-permute-done.11 = bf16[2,112,384]{2,1,0:T(8,128)(2,1)S(1)} collective-permute-done((bf16[2,112,384]{2,1,0:T(8,128)(2,1)S(1)}, bf16[2,112,384]{2,1,0:T(8,128)(2,1)S(1)}, u32[]{:S(2)}, u32[]{:S(2)}) %collective-permute-start.11) | collective-permute-done | bytes 172064 | tf_op jit(solution)/shard_map/ppermute | solution.py:832
  142.4 1.6 collective-permute-start.16
  144.0 2.9 %collective-permute-done.14 = bf16[2,192,384]{2,1,0:T(8,128)(2,1)S(1)} collective-permute-done((bf16[2,192,384]{2,1,0:T(8,128)(2,1)S(1)}, bf16[2,192,384]{2,1,0:T(8,128)(2,1)S(1)}, u32[]{:S(2)}, u32[]{:S(2)}) %collective-permute-start.14) | collective-permute-done | bytes 294944 | tf_op jit(solution)/shard_map/ppermute | solution.py:832
  146.9 1.4 collective-permute-start.15
  148.3 4.9 %collective-permute-done.13 = bf16[2,192,384]{2,1,0:T(8,128)(2,1)S(1)} collective-permute-done((bf16[2,192,384]{2,1,0:T(8,128)(2,1)S(1)}, bf16[2,192,384]{2,1,0:T(8,128)(2,1)S(1)}, u32[]{:S(2)}, u32[]{:S(2)}) %collective-permute-start.13) | collective-permute-done | bytes 294944 | tf_op jit(solution)/shard_map/ppermute | solution.py:832
  153.4 3.3 %collective-permute-done.17 = bf16[2,112,384]{2,1,0:T(8,128)(2,1)S(1)} collective-permute-done((bf16[2,112,384]{2,1,0:T(8,128)(2,1)S(1)}, bf16[2,112,384]{2,1,0:T(8,128)(2,1)S(1)}, u32[]{:S(2)}, u32[]{:S(2)}) %collective-permute-start.17) | collective-permute-done | bytes 172064 | tf_op jit(solution)/shard_map/ppermute | solution.py:832
  156.8 2.1 %collective-permute-done.16 = bf16[2,112,384]{2,1,0:T(8,128)(2,1)S(1)} collective-permute-done((bf16[2,112,384]{2,1,0:T(8,128)(2,1)S(1)}, bf16[2,112,384]{2,1,0:T(8,128)(2,1)S(1)}, u32[]{:S(2)}, u32[]{:S(2)}) %collective-permute-start.16) | collective-permute-done | bytes 172064 | tf_op jit(solution)/shard_map/ppermute | solution.py:832
  159.0 2.1 %collective-permute-done.18.other_ref = bf16[8,112,384]{2,1,0:T(8,128)(2,1)S(1)} collective-permute-done((bf16[8,112,384]{2,1,0:T(8,128)(2,1)S(1)}, bf16[8,112,384]{2,1,0:T(8,128)(2,1)S(1)}, u32[]{:S(2)}, u32[]{:S(2)}) %collective-permute-start.18) | collective-permute-done | bytes 688160 | tf_op jit(solution)/shard_map/ppermute | solution.py:832
  161.2 1.6 shard_map.274
  162.8 2.6 %shard_map.275 = (f32[1,1536,384]{2,1,0:T(8,128)}, f32[1,384,1536]{2,1,0:T(8,128)}) custom-call(bf16[8,192,384]{2,1,0:T(8,128)(2,1)S(1)} %bitcast.70, bf16[8,192,384]{2,1,0:T(8,128)(2,1)S(1)} %collective-permute-done.19.other_ref), custom_call_target="tpu_custom_call" | custom-call | flops 4000000000 | bytes 8000000 | tf_op jit(solution)/shard_map/pallas_call | solution.py:280
  (72 shorter events, 6.2 us)
Async XLA Ops:
  12.8 11.9 %collective-permute-start = (bf16[512,384]{1,0:T(8,128)(2,1)}, bf16[512,384]{1,0:T(8,128)(2,1)}, u32[]{:S(2)}, u32[]{:S(2)}) collective-permute-start(bf16[512,384]{1,0:T(8,128)(2,1)} %get-tuple-element.1058), channel_id=1, source_target_pairs={{0,16},{16,0},{1,17},{17,1},{2,18},{18,2},{3,19},{19,3},{4,20},{20... | collective-permute-start | bytes 1179656 | tf_op jit(solution)/shard_map/while/body/eval_jaxpr/ppermute | solution.py:869
  34.7 16.4 %collective-permute-start = (bf16[512,384]{1,0:T(8,128)(2,1)}, bf16[512,384]{1,0:T(8,128)(2,1)}, u32[]{:S(2)}, u32[]{:S(2)}) collective-permute-start(bf16[512,384]{1,0:T(8,128)(2,1)} %get-tuple-element.1058), channel_id=1, source_target_pairs={{0,16},{16,0},{1,17},{17,1},{2,18},{18,2},{3,19},{19,3},{4,20},{20... | collective-permute-start | bytes 1179656 | tf_op jit(solution)/shard_map/while/body/eval_jaxpr/ppermute | solution.py:869
  61.7 16.6 %collective-permute-start = (bf16[512,384]{1,0:T(8,128)(2,1)}, bf16[512,384]{1,0:T(8,128)(2,1)}, u32[]{:S(2)}, u32[]{:S(2)}) collective-permute-start(bf16[512,384]{1,0:T(8,128)(2,1)} %get-tuple-element.1058), channel_id=1, source_target_pairs={{0,16},{16,0},{1,17},{17,1},{2,18},{18,2},{3,19},{19,3},{4,20},{20... | collective-permute-start | bytes 1179656 | tf_op jit(solution)/shard_map/while/body/eval_jaxpr/ppermute | solution.py:869
  90.6 3.1 %collective-permute-start.1 = (bf16[8,192,384]{2,1,0:T(8,128)(2,1)}, bf16[8,192,384]{2,1,0:T(8,128)(2,1)S(1)}, u32[]{:S(2)}, u32[]{:S(2)}) collective-permute-start(bf16[8,192,384]{2,1,0:T(8,128)(2,1)} %get-tuple-element.645), channel_id=1, source_target_pairs={{0,1},{1,0},{2,3},{3,2},{4,5},{5,4},{6,7},{7,6},{8,9},{9,8},{10,11... | collective-permute-start | bytes 3538952 | tf_op jit(solution)/shard_map/ppermute | solution.py:832
  93.8 5.5 %copy-start.15 = (bf16[2,3,6,64,512]{4,3,2,1,0:T(8,128)(2,1)S(1)}, bf16[2,3,6,64,512]{4,3,2,1,0:T(8,128)(2,1)}, u32[]{:S(2)}) copy-start(bf16[2,3,6,64,512]{4,3,2,1,0:T(8,128)(2,1)} %get-tuple-element.653.refs_18_) | copy-start | bytes 7077892
  93.8 5.5 %copy-start.16 = (f32[2,6,64,512]{3,2,1,0:T(8,128)S(1)}, f32[2,6,64,512]{3,2,1,0:T(8,128)}, u32[]{:S(2)}) copy-start(f32[2,6,64,512]{3,2,1,0:T(8,128)} %get-tuple-element.651.refs_16_) | copy-start | bytes 4718596
  95.5 3.8 %copy-start.4 = (bf16[2,1,512,384]{3,2,1,0:T(8,128)(2,1)S(1)}, bf16[2,1,512,384]{3,2,1,0:T(8,128)(2,1)}, u32[]{:S(2)}) copy-start(bf16[2,1,512,384]{3,2,1,0:T(8,128)(2,1)} %get-tuple-element.1229) | copy-start | bytes 2359300
  95.5 3.8 %copy-start.9 = (bf16[1,384]{1,0:T(2,128)(2,1)S(1)}, bf16[1,384]{1,0:T(2,128)(2,1)}, u32[]{:S(2)}) copy-start(bf16[1,384]{1,0:T(2,128)(2,1)} %get-tuple-element.1235) | copy-start | bytes 2308
  95.5 3.8 %copy-start.10 = (bf16[1,384]{1,0:T(2,128)(2,1)S(1)}, bf16[1,384]{1,0:T(2,128)(2,1)}, u32[]{:S(2)}) copy-start(bf16[1,384]{1,0:T(2,128)(2,1)} %get-tuple-element.1236) | copy-start | bytes 2308
  95.5 3.8 %copy-start.11 = (bf16[1,384]{1,0:T(2,128)(2,1)S(1)}, bf16[1,384]{1,0:T(2,128)(2,1)}, u32[]{:S(2)}) copy-start(bf16[1,384]{1,0:T(2,128)(2,1)} %get-tuple-element.1237) | copy-start | bytes 2308
  95.5 3.7 %copy-start.12 = (bf16[1,384]{1,0:T(2,128)(2,1)S(1)}, bf16[1,384]{1,0:T(2,128)(2,1)}, u32[]{:S(2)}) copy-start(bf16[1,384]{1,0:T(2,128)(2,1)} %get-tuple-element.1238) | copy-start | bytes 2308
  95.5 3.7 %copy-start.13 = (bf16[1,384]{1,0:T(2,128)(2,1)S(1)}, bf16[1,384]{1,0:T(2,128)(2,1)}, u32[]{:S(2)}) copy-start(bf16[1,384]{1,0:T(2,128)(2,1)} %get-tuple-element.1239) | copy-start | bytes 2308
  95.6 3.7 %copy-start.14 = (bf16[1,384]{1,0:T(2,128)(2,1)S(1)}, bf16[1,384]{1,0:T(2,128)(2,1)}, u32[]{:S(2)}) copy-start(bf16[1,384]{1,0:T(2,128)(2,1)} %get-tuple-element.1240) | copy-start | bytes 2308
  95.6 3.7 %copy-start.17 = (f32[2,6,1,512]{3,2,1,0:T(1,128)S(1)}, f32[2,6,1,512]{3,2,1,0:T(1,128)}, u32[]{:S(2)}) copy-start(f32[2,6,1,512]{3,2,1,0:T(1,128)} %get-tuple-element.655.refs_20_) | copy-start | bytes 73732
  95.7 17.3 %collective-permute-start.4 = (bf16[2,192,384]{2,1,0:T(8,128)(2,1)S(1)}, bf16[2,192,384]{2,1,0:T(8,128)(2,1)S(1)}, u32[]{:S(2)}, u32[]{:S(2)}) collective-permute-start(bf16[2,192,384]{2,1,0:T(8,128)(2,1)S(1)} %get-tuple-element.814), channel_id=1, source_target_pairs={{0,6},{1,7},{2,4},{3,5},{4,2},{5,3},{6,0},{7,1},{8,14},{9,15},{10,... | collective-permute-start | bytes 884744 | tf_op jit(solution)/shard_map/ppermute | solution.py:832
  97.9 15.1 %collective-permute-start.3 = (bf16[2,192,384]{2,1,0:T(8,128)(2,1)S(1)}, bf16[2,192,384]{2,1,0:T(8,128)(2,1)S(1)}, u32[]{:S(2)}, u32[]{:S(2)}) collective-permute-start(bf16[2,192,384]{2,1,0:T(8,128)(2,1)S(1)} %get-tuple-element.815), channel_id=1, source_target_pairs={{0,4},{1,5},{2,6},{3,7},{4,0},{5,1},{6,2},{7,3},{8,12},{9,13},{10,... | collective-permute-start | bytes 884744 | tf_op jit(solution)/shard_map/ppermute | solution.py:832
  98.3 14.7 %collective-permute-start.2 = (bf16[2,192,384]{2,1,0:T(8,128)(2,1)S(1)}, bf16[2,192,384]{2,1,0:T(8,128)(2,1)S(1)}, u32[]{:S(2)}, u32[]{:S(2)}) collective-permute-start(bf16[2,192,384]{2,1,0:T(8,128)(2,1)S(1)} %get-tuple-element.816), channel_id=1, source_target_pairs={{0,2},{1,3},{2,0},{3,1},{4,6},{5,7},{6,4},{7,5},{8,10},{9,11},{10,... | collective-permute-start | bytes 884744 | tf_op jit(solution)/shard_map/ppermute | solution.py:832
  112.4 3.0 %collective-permute-start.5 = (bf16[4,112,384]{2,1,0:T(8,128)(2,1)S(1)}, bf16[4,112,384]{2,1,0:T(8,128)(2,1)S(1)}, u32[]{:S(2)}, u32[]{:S(2)}) collective-permute-start(bf16[4,112,384]{2,1,0:T(8,128)(2,1)S(1)} %get-tuple-element.820), channel_id=1, source_target_pairs={{0,1},{1,0},{2,3},{3,2},{4,5},{5,4},{6,7},{7,6},{8,9},{9,8},{10,11... | collective-permute-start | bytes 1032200 | tf_op jit(solution)/shard_map/ppermute | solution.py:832
  112.5 2.9 %collective-permute-start.6 = (bf16[4,112,384]{2,1,0:T(8,128)(2,1)S(1)}, bf16[4,112,384]{2,1,0:T(8,128)(2,1)S(1)}, u32[]{:S(2)}, u32[]{:S(2)}) collective-permute-start(bf16[4,112,384]{2,1,0:T(8,128)(2,1)S(1)} %get-tuple-element.821), channel_id=1, source_target_pairs={{0,1},{1,0},{2,3},{3,2},{4,5},{5,4},{6,7},{7,6},{8,9},{9,8},{10,11... | collective-permute-start | bytes 1032200 | tf_op jit(solution)/shard_map/ppermute | solution.py:832
  113.2 19.0 %collective-permute-start.7 = (bf16[2,192,384]{2,1,0:T(8,128)(2,1)S(1)}, bf16[2,192,384]{2,1,0:T(8,128)(2,1)S(1)}, u32[]{:S(2)}, u32[]{:S(2)}) collective-permute-start(bf16[2,192,384]{2,1,0:T(8,128)(2,1)S(1)} %fusion.2), channel_id=1, source_target_pairs={{0,8},{1,9},{2,10},{3,11},{4,12},{5,13},{6,14},{7,15},{8,0},{9,1},... | collective-permute-start | bytes 884744 | tf_op jit(solution)/shard_map/ppermute | solution.py:832
  115.8 10.8 %collective-permute-start.10 = (bf16[2,112,384]{2,1,0:T(8,128)(2,1)S(1)}, bf16[2,112,384]{2,1,0:T(8,128)(2,1)S(1)}, u32[]{:S(2)}, u32[]{:S(2)}) collective-permute-start(bf16[2,112,384]{2,1,0:T(8,128)(2,1)S(1)} %get-tuple-element.817), channel_id=1, source_target_pairs={{0,6},{1,7},{2,4},{3,5},{4,2},{5,3},{6,0},{7,1},{8,14},{9,15},{10,... | collective-permute-start | bytes 516104 | tf_op jit(solution)/shard_map/ppermute | solution.py:832
  118.4 13.8 %collective-permute-start.9 = (bf16[2,112,384]{2,1,0:T(8,128)(2,1)S(1)}, bf16[2,112,384]{2,1,0:T(8,128)(2,1)S(1)}, u32[]{:S(2)}, u32[]{:S(2)}) collective-permute-start(bf16[2,112,384]{2,1,0:T(8,128)(2,1)S(1)} %get-tuple-element.818), channel_id=1, source_target_pairs={{0,4},{1,5},{2,6},{3,7},{4,0},{5,1},{6,2},{7,3},{8,12},{9,13},{10,... | collective-permute-start | bytes 516104 | tf_op jit(solution)/shard_map/ppermute | solution.py:832
  118.8 13.4 %collective-permute-start.8 = (bf16[2,112,384]{2,1,0:T(8,128)(2,1)S(1)}, bf16[2,112,384]{2,1,0:T(8,128)(2,1)S(1)}, u32[]{:S(2)}, u32[]{:S(2)}) collective-permute-start(bf16[2,112,384]{2,1,0:T(8,128)(2,1)S(1)} %get-tuple-element.819), channel_id=1, source_target_pairs={{0,2},{1,3},{2,0},{3,1},{4,6},{5,7},{6,4},{7,5},{8,10},{9,11},{10,... | collective-permute-start | bytes 516104 | tf_op jit(solution)/shard_map/ppermute | solution.py:832
  132.3 10.0 %collective-permute-start.11 = (bf16[2,112,384]{2,1,0:T(8,128)(2,1)S(1)}, bf16[2,112,384]{2,1,0:T(8,128)(2,1)S(1)}, u32[]{:S(2)}, u32[]{:S(2)}) collective-permute-start(bf16[2,112,384]{2,1,0:T(8,128)(2,1)S(1)} %fusion.5), channel_id=1, source_target_pairs={{0,8},{1,9},{2,10},{3,11},{4,12},{5,13},{6,14},{7,15},{8,0},{9,1},... | collective-permute-start | bytes 516104 | tf_op jit(solution)/shard_map/ppermute | solution.py:832
  133.9 13.0 %collective-permute-start.14 = (bf16[2,192,384]{2,1,0:T(8,128)(2,1)S(1)}, bf16[2,192,384]{2,1,0:T(8,128)(2,1)S(1)}, u32[]{:S(2)}, u32[]{:S(2)}) collective-permute-start(bf16[2,192,384]{2,1,0:T(8,128)(2,1)S(1)} %add_convert_fusion.2), channel_id=1, source_target_pairs={{0,6},{1,7},{2,4},{3,5},{4,2},{5,3},{6,0},{7,1},{8,14},{9,15},{10,... | collective-permute-start | bytes 884744 | tf_op jit(solution)/shard_map/ppermute | solution.py:832
  136.4 16.8 %collective-permute-start.13 = (bf16[2,192,384]{2,1,0:T(8,128)(2,1)S(1)}, bf16[2,192,384]{2,1,0:T(8,128)(2,1)S(1)}, u32[]{:S(2)}, u32[]{:S(2)}) collective-permute-start(bf16[2,192,384]{2,1,0:T(8,128)(2,1)S(1)} %add_convert_fusion.2), channel_id=1, source_target_pairs={{0,4},{1,5},{2,6},{3,7},{4,0},{5,1},{6,2},{7,3},{8,12},{9,13},{10,... | collective-permute-start | bytes 884744 | tf_op jit(solution)/shard_map/ppermute | solution.py:832
  136.5 16.7 %collective-permute-start.12 = (bf16[2,192,384]{2,1,0:T(8,128)(2,1)S(1)}, bf16[2,192,384]{2,1,0:T(8,128)(2,1)S(1)}, u32[]{:S(2)}, u32[]{:S(2)}) collective-permute-start(bf16[2,192,384]{2,1,0:T(8,128)(2,1)S(1)} %add_convert_fusion.2), channel_id=1, source_target_pairs={{0,2},{1,3},{2,0},{3,1},{4,6},{5,7},{6,4},{7,5},{8,10},{9,11},{10,... | collective-permute-start | bytes 884744 | tf_op jit(solution)/shard_map/ppermute | solution.py:832
  142.3 14.5 %collective-permute-start.17 = (bf16[2,112,384]{2,1,0:T(8,128)(2,1)S(1)}, bf16[2,112,384]{2,1,0:T(8,128)(2,1)S(1)}, u32[]{:S(2)}, u32[]{:S(2)}) collective-permute-start(bf16[2,112,384]{2,1,0:T(8,128)(2,1)S(1)} %add_convert_fusion.3), channel_id=1, source_target_pairs={{0,6},{1,7},{2,4},{3,5},{4,2},{5,3},{6,0},{7,1},{8,14},{9,15},{10,... | collective-permute-start | bytes 516104 | tf_op jit(solution)/shard_map/ppermute | solution.py:832
  142.4 16.5 %collective-permute-start.16 = (bf16[2,112,384]{2,1,0:T(8,128)(2,1)S(1)}, bf16[2,112,384]{2,1,0:T(8,128)(2,1)S(1)}, u32[]{:S(2)}, u32[]{:S(2)}) collective-permute-start(bf16[2,112,384]{2,1,0:T(8,128)(2,1)S(1)} %add_convert_fusion.3), channel_id=1, source_target_pairs={{0,4},{1,5},{2,6},{3,7},{4,0},{5,1},{6,2},{7,3},{8,12},{9,13},{10,... | collective-permute-start | bytes 516104 | tf_op jit(solution)/shard_map/ppermute | solution.py:832
  146.9 12.0 %collective-permute-start.15 = (bf16[2,112,384]{2,1,0:T(8,128)(2,1)S(1)}, bf16[2,112,384]{2,1,0:T(8,128)(2,1)S(1)}, u32[]{:S(2)}, u32[]{:S(2)}) collective-permute-start(bf16[2,112,384]{2,1,0:T(8,128)(2,1)S(1)} %add_convert_fusion.3), channel_id=1, source_target_pairs={{0,2},{1,3},{2,0},{3,1},{4,6},{5,7},{6,4},{7,5},{8,10},{9,11},{10,... | collective-permute-start | bytes 516104 | tf_op jit(solution)/shard_map/ppermute | solution.py:832
  153.4 9.4 %collective-permute-start.19 = (bf16[8,192,384]{2,1,0:T(8,128)(2,1)S(1)}, bf16[8,192,384]{2,1,0:T(8,128)(2,1)S(1)}, u32[]{:S(2)}, u32[]{:S(2)}) collective-permute-start(bf16[8,192,384]{2,1,0:T(8,128)(2,1)S(1)} %bitcast.69), channel_id=1, source_target_pairs={{0,1},{1,0},{2,3},{3,2},{4,5},{5,4},{6,7},{7,6},{8,9},{9,8},{10,11... | collective-permute-start | bytes 3538952 | tf_op jit(solution)/shard_map/ppermute | solution.py:832
  158.9 2.2 %collective-permute-start.18 = (bf16[8,112,384]{2,1,0:T(8,128)(2,1)S(1)}, bf16[8,112,384]{2,1,0:T(8,128)(2,1)S(1)}, u32[]{:S(2)}, u32[]{:S(2)}) collective-permute-start(bf16[8,112,384]{2,1,0:T(8,128)(2,1)S(1)} %bitcast.71), channel_id=1, source_target_pairs={{0,1},{1,0},{2,3},{3,2},{4,5},{5,4},{6,7},{7,6},{8,9},{9,8},{10,11... | collective-permute-start | bytes 2064392 | tf_op jit(solution)/shard_map/ppermute | solution.py:832
  (9 other events, 18.3 us)

commit v2 on v1

--- a/solution.py
+++ b/solution.py
@@ -15,7 +15,8 @@
 F32 = jnp.float32
 BF16 = jnp.bfloat16
 VMEM_LIMIT = 16 * 2**20
-BIG = 55 * 2**20
+BIG = 52 * 2**20
+MID = 52 * 2**20
 
 
 def dot(a, b):
@@ -39,6 +40,7 @@
 
 LINES = ("ag", "as", "qb", "vb", "ob", "mg", "ms", "db", "ub")
 CHUNK = 256
+WIDE = 256
 
 
 def padded(rows, odd):
@@ -76,18 +78,20 @@
 
     def soften(h, odd):
         s_ref = r["s"].at[odd]
-        for c in range(slots // LANES):
-            cols = slice(c * LANES, (c + 1) * LANES)
-            peak = s_ref[0:PATCHES, cols]
-            for g in range(1, groups):
+        for c in range(slots // WIDE):
+            cols = slice(c * WIDE, (c + 1) * WIDE)
+            peak = None
+            for g in range(groups):
                 block = s_ref[g * PATCHES : (g + 1) * PATCHES, cols]
-                peak = jnp.maximum(peak, block if g < 2 else block + shift[g])
+                top = jnp.max(block.reshape(PATCHES // 8, 8, WIDE), 0)
+                top = top if g < 2 else top + shift[g]
+                peak = top if g == 0 else jnp.maximum(peak, top)
             peak = jnp.max(peak, 0, keepdims=True)
-            acc = jnp.zeros((PATCHES, LANES), F32)
+            acc = jnp.zeros((8, WIDE), F32)
             for g in range(groups):
                 block = s_ref[g * PATCHES : (g + 1) * PATCHES, cols]
                 e = jnp.exp(block - (peak - shift[g]))
-                acc = acc + e
+                acc = acc + jnp.sum(e.reshape(PATCHES // 8, 8, WIDE), 0)
                 r["e"][h, g * PATCHES : (g + 1) * PATCHES, cols] = e.astype(BF16)
             r["inv"][h, :, cols] = 1.0 / jnp.sum(acc, 0, keepdims=True)
 
@@ -210,8 +214,8 @@
 
     def weigh(h, odd):
         s_ref = r["s"].at[odd]
-        for c in range(slots // LANES):
-            cols = slice(c * LANES, (c + 1) * LANES)
+        for c in range(slots // WIDE):
+            cols = slice(c * WIDE, (c + 1) * WIDE)
             center = r["center"][odd, :, cols]
             for b in range(0, slots, PATCHES):
                 block = s_ref[b : b + PATCHES, cols] - center
@@ -346,7 +350,7 @@
 
     def body(*refs):
         step_ref, views_ref = refs[:2]
-        vec = dict(zip(LINES, refs[2 : 2 + len(lines)]))
+        line_hbm = refs[2 : 2 + len(lines)]
         tokens_hbm, cot_hbm, recv_hbm = refs[2 + len(lines) : 5 + len(lines)]
         w_hbm = dict(zip(WEIGHTS, refs[5 + len(lines) : n_in]))
         rest = refs[n_in + len(bufs) :]
@@ -355,7 +359,12 @@
         rest = rest[3 + len(SAVED + TERMS) :]
         w = dict(zip(WEIGHTS, rest[:4]))
         r = dict(zip(names, rest[4 : 4 + len(names)]))
-        x, dm, y, sem = rest[4 + len(names) :]
+        x, dm, y, sem, line_sem = rest[4 + len(names) : 9 + len(names)]
+        vec = dict(zip(LINES, rest[9 + len(names) :]))
+        line_copy = [
+            pltpu.make_async_copy(src, vec[n], line_sem.at[i])
+            for i, (n, src) in enumerate(zip(LINES, line_hbm))
+        ]
         moves = Moves(sem)
         t = step_ref[0]
         lead = lax.axis_index("section") == 0
@@ -388,7 +397,10 @@
             def _():
                 recv_copy.start()
 
-            for n in WEIGHTS:
+            w_copy["qkv"].start()
+            for copy in line_copy:
+                copy.start()
+            for n in WEIGHTS[1:]:
                 w_copy[n].start()
 
             @pl.when(not_lead)
@@ -396,8 +408,10 @@
                 cot_copy.start()
 
             token_copy.wait()
+            for copy in line_copy:
+                copy.wait()
             forward(
-                x, y, views_ref[slot, 0], vec, w, r,
+                x, y, views_ref[slot], vec, w, r,
                 lambda n: w_copy[n].wait(), lambda n: s_copy[n].start() if n in s_copy else None,
             )
             y_copy.start()
@@ -413,10 +427,14 @@
         @pl.when(only_b)
         def _():
             grad_copy.start()
+            for copy in line_copy:
+                copy.start()
             for n in ("down", "gp", "up", "h", "out", "inv", "ot", "v", "e", "kt", "qt", "qkv"):
                 (w_copy if n in w_copy else l_copy)[n].start()
             token_copy.start()
             grad_copy.wait()
+            for copy in line_copy:
+                copy.wait()
             for n in ("down", "gp", "up", "h"):
                 (w_copy if n in w_copy else l_copy)[n].wait()
 
@@ -458,12 +476,14 @@
             def _():
                 g_send.wait()
 
-    ins = [(step, "s"), (views, "s")] + [(v, "v") for v in lines]
+    ins = [(step, "s"), (views, "s")] + [(v, "a") for v in lines]
     ins += [(x, "a") for x in (tokens, cotangent, recv, *weights, *bufs)]
     outs = [((slots, width), BF16, "a")] + [(b.shape, b.dtype, "a") for b in bufs]
     scratch = [pltpu.VMEM(wshapes[n], BF16) for n in WEIGHTS]
     scratch += [pltpu.VMEM(*shapes[n]) for n in names]
     scratch += [pltpu.VMEM((slots, width), BF16)] * 3 + [pltpu.SemaphoreType.DMA((40,))]
+    scratch += [pltpu.SemaphoreType.DMA((len(lines),))]
+    scratch += [pltpu.VMEM(v.shape, v.dtype) for v in lines]
     got = run(body, ins, outs, scratch, {n_in + i: 1 + i for i in range(len(bufs))}, us=15, limit=BIG)
     return got[0], tuple(got[1:])
 
@@ -502,18 +522,18 @@
     return lax.axis_index("dp") if lax.axis_size("dp") == CUTS else 0
 
 
-def mlp_grads(lines, recv, weights, kept, dims):
+def mlp_grads(gain, recv, weights, kept, dims):
     slots, width, ff = dims
     deep = width // 4
     shapes = all_sizes(dims)
     names = ("gp", "h", "du", "dp", "dh", "small")
     given = ("gp", "h", "c", "z", "dm", "du", "dp", "small")
-    n_in = len(lines) + 3 + len(given)
+    n_in = 1 + 3 + len(given)
 
     def body(*refs):
-        vec = dict(zip(LINES, refs[: len(lines)]))
-        recv_hbm, up_hbm, down_hbm = refs[len(lines) : len(lines) + 3]
-        hbm = dict(zip(given, refs[len(lines) + 3 : n_in]))
+        vec = {"mg": refs[0]}
+        recv_hbm, up_hbm, down_hbm = refs[1:4]
+        hbm = dict(zip(given, refs[4:n_in]))
         keep, send, sums, dp_hbm, small_hbm, dh_hbm = refs[n_in : n_in + 6]
         rest = refs[n_in + 6 :]
         w = {"up": rest[0], "down": rest[1]}
@@ -543,30 +563,35 @@
         @pl.when(lead)
         def _():
             m1_recv.start()
+            for copy in early:
+                copy.start()
 
         @pl.when(other)
         def _():
             m1.start()
+            d1.start()
 
         moves.start("m0", hbm["dm"].at[0], m.at[half[0]])
         for i in (0, 1):
             moves.start("z%d" % i, hbm["z"].at[i], z.at[half[i]])
-
-        @pl.when(other)
-        def _():
-            d1.start()
-
-        @pl.when(lead)
-        def _():
-            for copy in early:
-                copy.start()
-
         for i in (0, 1):
             moves.start("c%d" % i, hbm["c"].at[i], c.at[half[i]])
         moves.start("d0", hbm["du"].at[0], d.at[half[0]])
         scatter = Scatter(sem2, blocks, keep, send)
         upper, lower = slice(0, deep), slice(deep, 2 * deep)
         moves.wait("m1")
+
+        @pl.when(lead)
+        def _():
+            def done(n):
+                if n == "dp":
+                    late[n].start()
+
+            r["du"] = d.at[half[1]]
+            backward_mlp(m.at[half[1]], vec, w, r, inner.wait, done)
+            late["small"].start()
+            late["dh"].start()
+
         moves.wait("m0")
         turned = m[...].T
         sums[4] = dot(jnp.ones((16, 2 * slots), BF16), m[...])[:8]
@@ -587,17 +612,6 @@
         @pl.when(other)
         def _():
             d1.wait()
-
-        @pl.when(lead)
-        def _():
-            def done(n):
-                if n == "dp":
-                    late[n].start()
-
-            r["du"] = d.at[half[1]]
-            backward_mlp(m.at[half[1]], vec, w, r, inner.wait, done)
-            late["small"].start()
-            late["dh"].start()
 
         moves.finish()
         turned_ref[...] = with_ones(c[...].T)
@@ -621,7 +635,7 @@
                 copy.wait()
 
     half = ((CUTS // 2, 2 * deep, width), BF16, "a")
-    ins = [(v, "v") for v in lines] + [(recv, "a"), (weights[2], "a"), (weights[3], "a")]
+    ins = [(gain, "v")] + [(recv, "a"), (weights[2], "a"), (weights[3], "a")]
     ins += [(kept[n], "a") for n in given]
     outs = [half, half, ((5, 8, width), F32, "v")]
     outs += [(kept[n].shape, kept[n].dtype, "a") for n in ("dp", "small")]
@@ -642,7 +656,7 @@
     return run(body, ins, outs, scratch, {n_in - 2: 3, n_in - 1: 4}, us=12, limit=BIG)
 
 
-def attention_grads(lines, tokens, weights, kept, dh, grads, sums, dims):
+def attention_grads(gain, tokens, weights, kept, dh, grads, sums, dims):
     slots, width, ff = dims
     deep = width // 4
     tall = deep + 16
@@ -653,14 +667,12 @@
     )
     loads = ("inv", "v", "e", "kt", "qt")
     given = ("a", "ot", "dp", "dqkv", "small") + loads
-    n_in = len(lines) + 6 + len(given)
+    n_in = 1 + 6 + len(given)
 
     def body(*refs):
-        vec = dict(zip(LINES, refs[: len(lines)]))
-        tokens_hbm, out_hbm, qkv_hbm, dh_hbm, grads_in, sums_ref = refs[
-            len(lines) : len(lines) + 6
-        ]
-        hbm = dict(zip(given, refs[len(lines) + 6 : n_in]))
+        vec = {"ag": refs[0]}
+        tokens_hbm, out_hbm, qkv_hbm, dh_hbm, grads_in, sums_ref = refs[1:7]
+        hbm = dict(zip(given, refs[7:n_in]))
         keep, send, grads_hbm = refs[n_in : n_in + 3]
         rest = refs[n_in + 3 :]
         w = {"out": rest[0], "qkv": rest[1]}
@@ -756,7 +768,7 @@
         def _():
             g_copy.wait()
 
-    ins = [(v, "v") for v in lines] + [(tokens, "a"), (weights[1], "a"), (weights[0], "a")]
+    ins = [(gain, "v")] + [(tokens, "a"), (weights[1], "a"), (weights[0], "a")]
     ins += [(dh, "a"), (grads, "a"), (sums, "v")]
     ins += [(kept[n], "a") for n in given]
     half = ((CUTS // 2, tall, width), BF16, "a")
@@ -779,7 +791,7 @@
         pltpu.SemaphoreType.DMA((24,)),
         pltpu.SemaphoreType.DMA((CUTS,)),
     ]
-    return run(body, ins, outs, scratch, {len(lines) + 4: 2}, us=12, limit=BIG)
+    return run(body, ins, outs, scratch, {1 + 4: 2}, us=12, limit=MID)
 
 
 def block(own, other, p):
@@ -794,7 +806,8 @@
     slots, width, ff = dims
     deep = width // 4
 
-    def body(own_ref, other_ref, down, up):
+    def body(own_ref, other_ref, down, up, token):
+        token[...] = jnp.zeros((8, LANES), F32)
         for j in range(4):
             part = [block(own_ref, other_ref, 4 * j + i) for i in range(4)]
             down[0, j * width : (j + 1) * width, :] = jnp.concatenate(
@@ -802,7 +815,7 @@
             ).T
             up[0, :, j * width : (j + 1) * width] = jnp.concatenate([v[deep:] for v in part], 0)
 
-    outs = [((1, ff, width), F32, "v"), ((1, width, ff), F32, "v")]
+    outs = [((1, ff, width), F32, "v"), ((1, width, ff), F32, "v"), ((8, LANES), F32, "v")]
     return run(body, [(own, "v"), (other, "v")], outs, [], us=4)
 
 
@@ -862,26 +875,29 @@
         up_bias,
     )
 
+    counts = views[:, 0]
+
     def advance(t, carry):
         recv, bufs = carry
         step = jnp.reshape(t, (1,))
-        send, bufs = cell(step, views, lines, tokens, cotangent, recv, weights, bufs, dims)
+        send, bufs = cell(step, counts, lines, tokens, cotangent, recv, weights, bufs, dims)
         return lax.ppermute(send, "section", [(0, 1), (1, 0)]), bufs
 
     recv, bufs = lax.fori_loop(0, STEPS, advance, blank(dims))
     outs, grads = bufs[:2]
     kept = dict(zip(SAVED + TERMS, bufs[2:]))
     m_keep, m_send, sums, kept["dp"], kept["small"], dh = mlp_grads(
-        lines, recv, weights, kept, dims
+        mlp_gain, recv, weights, kept, dims
     )
     if lax.axis_size("dp") != CUTS:
-        a_keep, a_send, grads = attention_grads(lines, tokens, weights, kept, dh, grads, sums, dims)
+        a_keep, a_send, grads = attention_grads(attn_gain, tokens, weights, kept, dh, grads, sums, dims)
         m, m_other, a, a_other = lax.psum((m_keep, m_send, a_keep, a_send), "dp")
+        g_down, g_up, _ = mlp_out(m, m_other, dims)
     else:
         m = added(m_keep, swapped(m_send, 1)).reshape(2, 4, *m_keep.shape[1:])
         m1 = square_send(m)
         (dh,) = tied(m, dh)
-        a_keep, a_send, grads = attention_grads(lines, tokens, weights, kept, dh, grads, sums, dims)
+        a_keep, a_send, grads = attention_grads(attn_gain, tokens, weights, kept, dh, grads, sums, dims)
         a_got = jnp.concatenate([swapped(v, 1) for v in jnp.split(a_send, 2)], 0)
         m1 = tied(a_keep, *m1)
         m = added(m[:, 0], *m1)
@@ -899,11 +915,10 @@
         a1 = square_gather(a)
         m1 = tied(a, *m1)
         m = jnp.stack([m, *m1], 1).reshape(8, *m.shape[1:])
-        m_other = swapped(m, 1)
-        a1 = tied(m, *a1)
+        g_down, g_up, token = mlp_out(m, swapped(m, 1), dims)
+        a1 = tied(token, *a1)
         a = jnp.stack([a, *a1], 1).reshape(8, *a.shape[1:])
         a_other = swapped(a, 1)
-    g_down, g_up = mlp_out(m, m_other, dims)
     g_qkv, g_out, *rows = attention_out(a, a_other, dims)
     g_ag, g_as, g_qb, g_vb, g_ob, g_mg, g_ms, g_db, g_ub = rows
     return (

time: 166 us -> 163 us (0.982)
  transfers between devices with their start and end apart: 22 -> 22, of which waited for: 12 -> 12; matrix products, arithmetic and copies ran while one was open for 1% -> 1% of each run, Pallas kernels for 8% -> 9%
where the time goes in v2:
time: 163 us
  waiting for transfers between devices  64.8 us (40%)
  Pallas kernels  60.6 us (37%)
  starting transfers between devices  33.5 us (21%)
  local copies, waits for them, and re-layouts  2.11 us (1%)
    pallas_call x8, Pallas kernels, run(): pl.pallas_call(body, out_shape=[jax.ShapeDtypeStruct(s, t) for s, t, _ in...  60.6 us
    ppermute x19, waiting for transfers between devices, swapped(): return lax.ppermute(x, 'dp', [(i, i ^ bits) for i in range(CUTS)])  35.6 us
    ppermute x3, waiting for transfers between devices, advance(): return (lax.ppermute(send, 'section', [(0, 1), (1, 0)]), bufs)  29.2 us
    ppermute x19, starting transfers between devices, swapped(): return lax.ppermute(x, 'dp', [(i, i ^ bits) for i in range(CUTS)])  18.8 us
    ppermute x3, starting transfers between devices, advance(): return (lax.ppermute(send, 'section', [(0, 1), (1, 0)]), bufs)  14.8 us
  transfers between devices with their start and end apart: 22, of which 12 were waited for; matrix products, arithmetic and copies ran while one was open for 1% of the time, Pallas kernels for 9%

profile of v2, /device:TPU:0, one launch (start us, length us, event | category | flops | bytes accessed | tf_op | source)
XLA Modules:
  0.0 163.2 jit_solution(1641729902626834303)
XLA Ops:
  0.7 1.2 copy-done.2
  2.5 74.6 %while.49 = (s32[]{:T(128)}, bf16[512,384]{1,0:T(8,128)(2,1)}, bf16[2,512,384]{2,1,0:T(8,128)(2,1)}, bf16[2,512,384]{2,1,0:T(8,128)(2,1)}, bf16[2,512,384]{2,1,0...) while((s32[]{:T(128)}, bf16[512,384]{1,0:T(8,128)(2,1)}, ...), condition=%wide.region_1.0_spmd, body=%wide.region_0.0_spmd.sunk | while | flops 15000000512 | bytes 31573220 | solution.py:886
  2.5 9.9 %eval_jaxpr.5 = (bf16[512,384]{1,0:T(8,128)(2,1)S(1)}, bf16[2,512,384]{2,1,0:T(8,128)(2,1)}, bf16[2,512,384]{2,1,0:T(8,128)(2,1)}, bf16[2,512,384]{2,1,0:T(8,128...) custom-call(s32[1]{0:T(128)} %bitcast.69.refs_0_, ...), custom_call_target="tpu_custom_call", output_to_operand_aliasing={{1}: (18, {}), {2}: (19, {}), {3}: (20, {}), {4}: (21, {}),... | custom-call | flops 15000000512 | bytes 30000000 | tf_op jit(solution)/shard_map/while/body/eval_jaxpr/pallas_call | solution.py:284
  12.5 11.6 %collective-permute-done = bf16[512,384]{1,0:T(8,128)(2,1)} collective-permute-done((bf16[512,384]{1,0:T(8,128)(2,1)S(1)}, bf16[512,384]{1,0:T(8,128)(2,1)}, u32[]{:S(2)}, u32[]{:S(2)}) %collective-permute-start) | collective-permute-done | bytes 393248 | tf_op jit(solution)/shard_map/while/body/eval_jaxpr/ppermute | solution.py:884
  24.1 9.9 %eval_jaxpr.5 = (bf16[512,384]{1,0:T(8,128)(2,1)S(1)}, bf16[2,512,384]{2,1,0:T(8,128)(2,1)}, bf16[2,512,384]{2,1,0:T(8,128)(2,1)}, bf16[2,512,384]{2,1,0:T(8,128...) custom-call(s32[1]{0:T(128)} %bitcast.69.refs_0_, ...), custom_call_target="tpu_custom_call", output_to_operand_aliasing={{1}: (18, {}), {2}: (19, {}), {3}: (20, {}), {4}: (21, {}),... | custom-call | flops 15000000512 | bytes 30000000 | tf_op jit(solution)/shard_map/while/body/eval_jaxpr/pallas_call | solution.py:284
  34.0 7.1 %collective-permute-start = (bf16[512,384]{1,0:T(8,128)(2,1)S(1)}, bf16[512,384]{1,0:T(8,128)(2,1)}, u32[]{:S(2)}, u32[]{:S(2)}) collective-permute-start(bf16[512,384]{1,0:T(8,128)(2,1)S(1)} %get-tuple-element.1022), channel_id=1, source_target_pairs={{0,16},{16,0},{1,17},{17,1},{2,18},{18,2},{3,19},{19,3},{4,20},{20... | collective-permute-start | bytes 1179656 | tf_op jit(solution)/shard_map/while/body/eval_jaxpr/ppermute | solution.py:884
  41.0 9.3 %collective-permute-done = bf16[512,384]{1,0:T(8,128)(2,1)} collective-permute-done((bf16[512,384]{1,0:T(8,128)(2,1)S(1)}, bf16[512,384]{1,0:T(8,128)(2,1)}, u32[]{:S(2)}, u32[]{:S(2)}) %collective-permute-start) | collective-permute-done | bytes 393248 | tf_op jit(solution)/shard_map/while/body/eval_jaxpr/ppermute | solution.py:884
  50.3 10.8 %eval_jaxpr.5 = (bf16[512,384]{1,0:T(8,128)(2,1)S(1)}, bf16[2,512,384]{2,1,0:T(8,128)(2,1)}, bf16[2,512,384]{2,1,0:T(8,128)(2,1)}, bf16[2,512,384]{2,1,0:T(8,128...) custom-call(s32[1]{0:T(128)} %bitcast.69.refs_0_, ...), custom_call_target="tpu_custom_call", output_to_operand_aliasing={{1}: (18, {}), {2}: (19, {}), {3}: (20, {}), {4}: (21, {}),... | custom-call | flops 15000000512 | bytes 30000000 | tf_op jit(solution)/shard_map/while/body/eval_jaxpr/pallas_call | solution.py:284
  61.1 7.6 %collective-permute-start = (bf16[512,384]{1,0:T(8,128)(2,1)S(1)}, bf16[512,384]{1,0:T(8,128)(2,1)}, u32[]{:S(2)}, u32[]{:S(2)}) collective-permute-start(bf16[512,384]{1,0:T(8,128)(2,1)S(1)} %get-tuple-element.1022), channel_id=1, source_target_pairs={{0,16},{16,0},{1,17},{17,1},{2,18},{18,2},{3,19},{19,3},{4,20},{20... | collective-permute-start | bytes 1179656 | tf_op jit(solution)/shard_map/while/body/eval_jaxpr/ppermute | solution.py:884
  68.7 8.4 %collective-permute-done = bf16[512,384]{1,0:T(8,128)(2,1)} collective-permute-done((bf16[512,384]{1,0:T(8,128)(2,1)S(1)}, bf16[512,384]{1,0:T(8,128)(2,1)}, u32[]{:S(2)}, u32[]{:S(2)}) %collective-permute-start) | collective-permute-done | bytes 393248 | tf_op jit(solution)/shard_map/while/body/eval_jaxpr/ppermute | solution.py:884
  77.1 13.5 %shard_map.272 = (bf16[8,192,384]{2,1,0:T(8,128)(2,1)S(1)}, bf16[8,192,384]{2,1,0:T(8,128)(2,1)}, f32[5,8,384]{2,1,0:T(8,128)S(1)}, bf16[2,512,384]{2,1,0:T(8,12...) custom-call(bf16[1,384]{1,0:T(2,128)(2,1)} %get-tuple-element.1196, ...), custom_call_target="tpu_custom_call", output_to_operand_aliasing={{3}: (10, {}), {4}: (11, {})} | custom-call | flops 12000000000 | bytes 24000000 | tf_op jit(solution)/shard_map/pallas_call | solution.py:284
  90.7 3.0 %collective-permute-done.1 = bf16[8,192,384]{2,1,0:T(8,128)(2,1)S(1)} collective-permute-done((bf16[8,192,384]{2,1,0:T(8,128)(2,1)}, bf16[8,192,384]{2,1,0:T(8,128)(2,1)S(1)}, u32[]{:S(2)}, u32[]{:S(2)}) %collective-permute-start.1) | collective-permute-done | bytes 1179680 | tf_op jit(solution)/shard_map/ppermute | solution.py:845
  94.2 2.1 %collective-permute-start.4 = (bf16[2,192,384]{2,1,0:T(8,128)(2,1)S(1)}, bf16[2,192,384]{2,1,0:T(8,128)(2,1)S(1)}, u32[]{:S(2)}, u32[]{:S(2)}) collective-permute-start(bf16[2,192,384]{2,1,0:T(8,128)(2,1)S(1)} %get-tuple-element.778), channel_id=1, source_target_pairs={{0,6},{1,7},{2,4},{3,5},{4,2},{5,3},{6,0},{7,1},{8,14},{9,15},{10,... | collective-permute-start | bytes 884744 | tf_op jit(solution)/shard_map/ppermute | solution.py:845
  96.8 1.0 collective-permute-start.2
  97.8 12.3 %shard_map.273 = (bf16[8,112,384]{2,1,0:T(8,128)(2,1)S(1)}, bf16[8,112,384]{2,1,0:T(8,128)(2,1)S(1)}, bf16[2,512,384]{2,1,0:T(8,128)(2,1)S(1)}) custom-call(bf16[1,384]{1,0:T(2,128)(2,1)S(1)} %copy-done.10, bf16[2,1,512,384]{3,2,1,0:T(8,128)(2,1)S(1)} %copy-done.5, bf16[1,384,384]{2,1,0:T(8,128)(2,1)S(1)} %copy-done.6, ...), custom_call_target="tpu_custom_call", output_to_operand_aliasing={{2}: (5, {})} | custom-call | flops 12000000000 | bytes 24000000 | tf_op jit(solution)/shard_map/pallas_call | solution.py:284
  111.0 2.2 %collective-permute-start.7 = (bf16[2,192,384]{2,1,0:T(8,128)(2,1)S(1)}, bf16[2,192,384]{2,1,0:T(8,128)(2,1)S(1)}, u32[]{:S(2)}, u32[]{:S(2)}) collective-permute-start(bf16[2,192,384]{2,1,0:T(8,128)(2,1)S(1)} %fusion.2), channel_id=1, source_target_pairs={{0,8},{1,9},{2,10},{3,11},{4,12},{5,13},{6,14},{7,15},{8,0},{9,1},... | collective-permute-start | bytes 884744 | tf_op jit(solution)/shard_map/ppermute | solution.py:845
  113.5 2.6 %collective-permute-start.10 = (bf16[2,112,384]{2,1,0:T(8,128)(2,1)S(1)}, bf16[2,112,384]{2,1,0:T(8,128)(2,1)S(1)}, u32[]{:S(2)}, u32[]{:S(2)}) collective-permute-start(bf16[2,112,384]{2,1,0:T(8,128)(2,1)S(1)} %get-tuple-element.781), channel_id=1, source_target_pairs={{0,6},{1,7},{2,4},{3,5},{4,2},{5,3},{6,0},{7,1},{8,14},{9,15},{10,... | collective-permute-start | bytes 516104 | tf_op jit(solution)/shard_map/ppermute | solution.py:845
  117.1 7.3 %collective-permute-done.10 = bf16[2,112,384]{2,1,0:T(8,128)(2,1)S(1)} collective-permute-done((bf16[2,112,384]{2,1,0:T(8,128)(2,1)S(1)}, bf16[2,112,384]{2,1,0:T(8,128)(2,1)S(1)}, u32[]{:S(2)}, u32[]{:S(2)}) %collective-permute-start.10) | collective-permute-done | bytes 172064 | tf_op jit(solution)/shard_map/ppermute | solution.py:845
  124.4 5.6 %collective-permute-done.9 = bf16[2,112,384]{2,1,0:T(8,128)(2,1)S(1)} collective-permute-done((bf16[2,112,384]{2,1,0:T(8,128)(2,1)S(1)}, bf16[2,112,384]{2,1,0:T(8,128)(2,1)S(1)}, u32[]{:S(2)}, u32[]{:S(2)}) %collective-permute-start.9) | collective-permute-done | bytes 172064 | tf_op jit(solution)/shard_map/ppermute | solution.py:845
  130.1 1.5 collective-permute-start.11
  131.7 2.5 %collective-permute-start.18 = (bf16[2,192,384]{2,1,0:T(8,128)(2,1)S(1)}, bf16[2,192,384]{2,1,0:T(8,128)(2,1)S(1)}, u32[]{:S(2)}, u32[]{:S(2)}) collective-permute-start(bf16[2,192,384]{2,1,0:T(8,128)(2,1)S(1)} %add_convert_fusion.2), channel_id=1, source_target_pairs={{0,6},{1,7},{2,4},{3,5},{4,2},{5,3},{6,0},{7,1},{8,14},{9,15},{10,... | collective-permute-start | bytes 884744 | tf_op jit(solution)/shard_map/ppermute | solution.py:845
  134.3 1.4 collective-permute-start.16
  135.7 4.3 %collective-permute-done.11 = bf16[2,112,384]{2,1,0:T(8,128)(2,1)S(1)} collective-permute-done((bf16[2,112,384]{2,1,0:T(8,128)(2,1)S(1)}, bf16[2,112,384]{2,1,0:T(8,128)(2,1)S(1)}, u32[]{:S(2)}, u32[]{:S(2)}) %collective-permute-start.11) | collective-permute-done | bytes 172064 | tf_op jit(solution)/shard_map/ppermute | solution.py:845
  140.1 1.5 collective-permute-start.13
  141.7 2.9 %collective-permute-done.18 = bf16[2,192,384]{2,1,0:T(8,128)(2,1)S(1)} collective-permute-done((bf16[2,192,384]{2,1,0:T(8,128)(2,1)S(1)}, bf16[2,192,384]{2,1,0:T(8,128)(2,1)S(1)}, u32[]{:S(2)}, u32[]{:S(2)}) %collective-permute-start.18) | collective-permute-done | bytes 294944 | tf_op jit(solution)/shard_map/ppermute | solution.py:845
  144.6 1.5 collective-permute-start.12
  146.1 4.9 %collective-permute-done.17 = bf16[2,192,384]{2,1,0:T(8,128)(2,1)S(1)} collective-permute-done((bf16[2,192,384]{2,1,0:T(8,128)(2,1)S(1)}, bf16[2,192,384]{2,1,0:T(8,128)(2,1)S(1)}, u32[]{:S(2)}, u32[]{:S(2)}) %collective-permute-start.17) | collective-permute-done | bytes 294944 | tf_op jit(solution)/shard_map/ppermute | solution.py:845
  151.2 3.3 %collective-permute-done.14 = bf16[2,112,384]{2,1,0:T(8,128)(2,1)S(1)} collective-permute-done((bf16[2,112,384]{2,1,0:T(8,128)(2,1)S(1)}, bf16[2,112,384]{2,1,0:T(8,128)(2,1)S(1)}, u32[]{:S(2)}, u32[]{:S(2)}) %collective-permute-start.14) | collective-permute-done | bytes 172064 | tf_op jit(solution)/shard_map/ppermute | solution.py:845
  154.5 2.1 %collective-permute-done.13 = bf16[2,112,384]{2,1,0:T(8,128)(2,1)S(1)} collective-permute-done((bf16[2,112,384]{2,1,0:T(8,128)(2,1)S(1)}, bf16[2,112,384]{2,1,0:T(8,128)(2,1)S(1)}, u32[]{:S(2)}, u32[]{:S(2)}) %collective-permute-start.13) | collective-permute-done | bytes 172064 | tf_op jit(solution)/shard_map/ppermute | solution.py:845
  156.8 2.1 %collective-permute-done.15.other_ref = bf16[8,112,384]{2,1,0:T(8,128)(2,1)S(1)} collective-permute-done((bf16[8,112,384]{2,1,0:T(8,128)(2,1)S(1)}, bf16[8,112,384]{2,1,0:T(8,128)(2,1)S(1)}, u32[]{:S(2)}, u32[]{:S(2)}) %collective-permute-start.15) | collective-permute-done | bytes 688160 | tf_op jit(solution)/shard_map/ppermute | solution.py:845
  158.9 1.6 shard_map.274
  160.5 2.7 %shard_map.275 = (f32[1,1536,384]{2,1,0:T(8,128)}, f32[1,384,1536]{2,1,0:T(8,128)}, f32[8,128]{1,0:T(8,128)}) custom-call(bf16[8,192,384]{2,1,0:T(8,128)(2,1)S(1)} %bitcast.71, bf16[8,192,384]{2,1,0:T(8,128)(2,1)S(1)} %collective-permute-done.19.other_ref), custom_call_target="tpu_custom_call" | custom-call | flops 4000000000 | bytes 8000000 | tf_op jit(solution)/shard_map/pallas_call | solution.py:284
  (69 shorter events, 4.7 us)
Async XLA Ops:
  12.4 11.7 %collective-permute-start = (bf16[512,384]{1,0:T(8,128)(2,1)S(1)}, bf16[512,384]{1,0:T(8,128)(2,1)}, u32[]{:S(2)}, u32[]{:S(2)}) collective-permute-start(bf16[512,384]{1,0:T(8,128)(2,1)S(1)} %get-tuple-element.1022), channel_id=1, source_target_pairs={{0,16},{16,0},{1,17},{17,1},{2,18},{18,2},{3,19},{19,3},{4,20},{20... | collective-permute-start | bytes 1179656 | tf_op jit(solution)/shard_map/while/body/eval_jaxpr/ppermute | solution.py:884
  34.0 16.3 %collective-permute-start = (bf16[512,384]{1,0:T(8,128)(2,1)S(1)}, bf16[512,384]{1,0:T(8,128)(2,1)}, u32[]{:S(2)}, u32[]{:S(2)}) collective-permute-start(bf16[512,384]{1,0:T(8,128)(2,1)S(1)} %get-tuple-element.1022), channel_id=1, source_target_pairs={{0,16},{16,0},{1,17},{17,1},{2,18},{18,2},{3,19},{19,3},{4,20},{20... | collective-permute-start | bytes 1179656 | tf_op jit(solution)/shard_map/while/body/eval_jaxpr/ppermute | solution.py:884
  61.1 16.0 %collective-permute-start = (bf16[512,384]{1,0:T(8,128)(2,1)S(1)}, bf16[512,384]{1,0:T(8,128)(2,1)}, u32[]{:S(2)}, u32[]{:S(2)}) collective-permute-start(bf16[512,384]{1,0:T(8,128)(2,1)S(1)} %get-tuple-element.1022), channel_id=1, source_target_pairs={{0,16},{16,0},{1,17},{17,1},{2,18},{18,2},{3,19},{19,3},{4,20},{20... | collective-permute-start | bytes 1179656 | tf_op jit(solution)/shard_map/while/body/eval_jaxpr/ppermute | solution.py:884
  77.1 20.6 %copy-start.12 = (f32[2,6,64,512]{3,2,1,0:T(8,128)S(1)}, f32[2,6,64,512]{3,2,1,0:T(8,128)}, u32[]{:S(2)}) copy-start(f32[2,6,64,512]{3,2,1,0:T(8,128)} %get-tuple-element.651.refs_8_) | copy-start | bytes 4718596
  77.1 20.6 %copy-start.15 = (bf16[2,512,384]{2,1,0:T(8,128)(2,1)S(1)}, bf16[2,512,384]{2,1,0:T(8,128)(2,1)}, u32[]{:S(2)}) copy-start(bf16[2,512,384]{2,1,0:T(8,128)(2,1)} %get-tuple-element.650.refs_7_) | copy-start | bytes 2359300
  90.6 3.1 %collective-permute-start.1 = (bf16[8,192,384]{2,1,0:T(8,128)(2,1)}, bf16[8,192,384]{2,1,0:T(8,128)(2,1)S(1)}, u32[]{:S(2)}, u32[]{:S(2)}) collective-permute-start(bf16[8,192,384]{2,1,0:T(8,128)(2,1)} %get-tuple-element.645), channel_id=1, source_target_pairs={{0,1},{1,0},{2,3},{3,2},{4,5},{5,4},{6,7},{7,6},{8,9},{9,8},{10,11... | collective-permute-start | bytes 3538952 | tf_op jit(solution)/shard_map/ppermute | solution.py:845
  93.7 4.0 %copy-start.6 = (bf16[1,384,384]{2,1,0:T(8,128)(2,1)S(1)}, bf16[1,384,384]{2,1,0:T(8,128)(2,1)}, u32[]{:S(2)}) copy-start(bf16[1,384,384]{2,1,0:T(8,128)(2,1)} %get-tuple-element.1195) | copy-start | bytes 884740
  93.7 4.0 %copy-start.11 = (bf16[2,3,6,64,512]{4,3,2,1,0:T(8,128)(2,1)S(1)}, bf16[2,3,6,64,512]{4,3,2,1,0:T(8,128)(2,1)}, u32[]{:S(2)}) copy-start(bf16[2,3,6,64,512]{4,3,2,1,0:T(8,128)(2,1)} %get-tuple-element.653.refs_10_) | copy-start | bytes 7077892
  93.7 4.0 %copy-start.13 = (bf16[2,512,384]{2,1,0:T(8,128)(2,1)S(1)}, bf16[2,512,384]{2,1,0:T(8,128)(2,1)}, u32[]{:S(2)}) copy-start(bf16[2,512,384]{2,1,0:T(8,128)(2,1)} %get-tuple-element.648.refs_5_) | copy-start | bytes 2359300
  94.0 3.7 %copy-start.3 = (bf16[1,384,1152]{2,1,0:T(8,128)(2,1)S(1)}, bf16[1,384,1152]{2,1,0:T(8,128)(2,1)}, u32[]{:S(2)}) copy-start(bf16[1,384,1152]{2,1,0:T(8,128)(2,1)} %get-tuple-element.1193) | copy-start | bytes 2654212
  94.0 3.7 %copy-start.5 = (bf16[2,1,512,384]{3,2,1,0:T(8,128)(2,1)S(1)}, bf16[2,1,512,384]{3,2,1,0:T(8,128)(2,1)}, u32[]{:S(2)}) copy-start(bf16[2,1,512,384]{3,2,1,0:T(8,128)(2,1)} %get-tuple-element.1194) | copy-start | bytes 2359300
  94.1 3.7 %copy-start.10 = (bf16[1,384]{1,0:T(2,128)(2,1)S(1)}, bf16[1,384]{1,0:T(2,128)(2,1)}, u32[]{:S(2)}) copy-start(bf16[1,384]{1,0:T(2,128)(2,1)} %get-tuple-element.1197) | copy-start | bytes 2308
  94.1 3.7 %copy-start.16 = (f32[2,6,1,512]{3,2,1,0:T(1,128)S(1)}, f32[2,6,1,512]{3,2,1,0:T(1,128)}, u32[]{:S(2)}) copy-start(f32[2,6,1,512]{3,2,1,0:T(1,128)} %get-tuple-element.655.refs_12_) | copy-start | bytes 73732
  94.1 3.7 %copy-start.17 = (f32[2,8,384]{2,1,0:T(8,128)S(1)}, f32[2,8,384]{2,1,0:T(8,128)}, u32[]{:S(2)}) copy-start(f32[2,8,384]{2,1,0:T(8,128)} %get-tuple-element.654.refs_11_) | copy-start | bytes 73732
  94.2 16.6 %collective-permute-start.4 = (bf16[2,192,384]{2,1,0:T(8,128)(2,1)S(1)}, bf16[2,192,384]{2,1,0:T(8,128)(2,1)S(1)}, u32[]{:S(2)}, u32[]{:S(2)}) collective-permute-start(bf16[2,192,384]{2,1,0:T(8,128)(2,1)S(1)} %get-tuple-element.778), channel_id=1, source_target_pairs={{0,6},{1,7},{2,4},{3,5},{4,2},{5,3},{6,0},{7,1},{8,14},{9,15},{10,... | collective-permute-start | bytes 884744 | tf_op jit(solution)/shard_map/ppermute | solution.py:845
  96.3 14.5 %collective-permute-start.3 = (bf16[2,192,384]{2,1,0:T(8,128)(2,1)S(1)}, bf16[2,192,384]{2,1,0:T(8,128)(2,1)S(1)}, u32[]{:S(2)}, u32[]{:S(2)}) collective-permute-start(bf16[2,192,384]{2,1,0:T(8,128)(2,1)S(1)} %get-tuple-element.779), channel_id=1, source_target_pairs={{0,4},{1,5},{2,6},{3,7},{4,0},{5,1},{6,2},{7,3},{8,12},{9,13},{10,... | collective-permute-start | bytes 884744 | tf_op jit(solution)/shard_map/ppermute | solution.py:845
  96.8 14.0 %collective-permute-start.2 = (bf16[2,192,384]{2,1,0:T(8,128)(2,1)S(1)}, bf16[2,192,384]{2,1,0:T(8,128)(2,1)S(1)}, u32[]{:S(2)}, u32[]{:S(2)}) collective-permute-start(bf16[2,192,384]{2,1,0:T(8,128)(2,1)S(1)} %get-tuple-element.780), channel_id=1, source_target_pairs={{0,2},{1,3},{2,0},{3,1},{4,6},{5,7},{6,4},{7,5},{8,10},{9,11},{10,... | collective-permute-start | bytes 884744 | tf_op jit(solution)/shard_map/ppermute | solution.py:845
  110.2 3.0 %collective-permute-start.5 = (bf16[4,112,384]{2,1,0:T(8,128)(2,1)S(1)}, bf16[4,112,384]{2,1,0:T(8,128)(2,1)S(1)}, u32[]{:S(2)}, u32[]{:S(2)}) collective-permute-start(bf16[4,112,384]{2,1,0:T(8,128)(2,1)S(1)} %get-tuple-element.784), channel_id=1, source_target_pairs={{0,1},{1,0},{2,3},{3,2},{4,5},{5,4},{6,7},{7,6},{8,9},{9,8},{10,11... | collective-permute-start | bytes 1032200 | tf_op jit(solution)/shard_map/ppermute | solution.py:845
  110.3 2.9 %collective-permute-start.6 = (bf16[4,112,384]{2,1,0:T(8,128)(2,1)S(1)}, bf16[4,112,384]{2,1,0:T(8,128)(2,1)S(1)}, u32[]{:S(2)}, u32[]{:S(2)}) collective-permute-start(bf16[4,112,384]{2,1,0:T(8,128)(2,1)S(1)} %get-tuple-element.785), channel_id=1, source_target_pairs={{0,1},{1,0},{2,3},{3,2},{4,5},{5,4},{6,7},{7,6},{8,9},{9,8},{10,11... | collective-permute-start | bytes 1032200 | tf_op jit(solution)/shard_map/ppermute | solution.py:845
  111.0 19.0 %collective-permute-start.7 = (bf16[2,192,384]{2,1,0:T(8,128)(2,1)S(1)}, bf16[2,192,384]{2,1,0:T(8,128)(2,1)S(1)}, u32[]{:S(2)}, u32[]{:S(2)}) collective-permute-start(bf16[2,192,384]{2,1,0:T(8,128)(2,1)S(1)} %fusion.2), channel_id=1, source_target_pairs={{0,8},{1,9},{2,10},{3,11},{4,12},{5,13},{6,14},{7,15},{8,0},{9,1},... | collective-permute-start | bytes 884744 | tf_op jit(solution)/shard_map/ppermute | solution.py:845
  113.5 10.8 %collective-permute-start.10 = (bf16[2,112,384]{2,1,0:T(8,128)(2,1)S(1)}, bf16[2,112,384]{2,1,0:T(8,128)(2,1)S(1)}, u32[]{:S(2)}, u32[]{:S(2)}) collective-permute-start(bf16[2,112,384]{2,1,0:T(8,128)(2,1)S(1)} %get-tuple-element.781), channel_id=1, source_target_pairs={{0,6},{1,7},{2,4},{3,5},{4,2},{5,3},{6,0},{7,1},{8,14},{9,15},{10,... | collective-permute-start | bytes 516104 | tf_op jit(solution)/shard_map/ppermute | solution.py:845
  116.1 13.8 %collective-permute-start.9 = (bf16[2,112,384]{2,1,0:T(8,128)(2,1)S(1)}, bf16[2,112,384]{2,1,0:T(8,128)(2,1)S(1)}, u32[]{:S(2)}, u32[]{:S(2)}) collective-permute-start(bf16[2,112,384]{2,1,0:T(8,128)(2,1)S(1)} %get-tuple-element.782), channel_id=1, source_target_pairs={{0,4},{1,5},{2,6},{3,7},{4,0},{5,1},{6,2},{7,3},{8,12},{9,13},{10,... | collective-permute-start | bytes 516104 | tf_op jit(solution)/shard_map/ppermute | solution.py:845
  116.6 13.4 %collective-permute-start.8 = (bf16[2,112,384]{2,1,0:T(8,128)(2,1)S(1)}, bf16[2,112,384]{2,1,0:T(8,128)(2,1)S(1)}, u32[]{:S(2)}, u32[]{:S(2)}) collective-permute-start(bf16[2,112,384]{2,1,0:T(8,128)(2,1)S(1)} %get-tuple-element.783), channel_id=1, source_target_pairs={{0,2},{1,3},{2,0},{3,1},{4,6},{5,7},{6,4},{7,5},{8,10},{9,11},{10,... | collective-permute-start | bytes 516104 | tf_op jit(solution)/shard_map/ppermute | solution.py:845
  130.1 9.9 %collective-permute-start.11 = (bf16[2,112,384]{2,1,0:T(8,128)(2,1)S(1)}, bf16[2,112,384]{2,1,0:T(8,128)(2,1)S(1)}, u32[]{:S(2)}, u32[]{:S(2)}) collective-permute-start(bf16[2,112,384]{2,1,0:T(8,128)(2,1)S(1)} %fusion.5), channel_id=1, source_target_pairs={{0,8},{1,9},{2,10},{3,11},{4,12},{5,13},{6,14},{7,15},{8,0},{9,1},... | collective-permute-start | bytes 516104 | tf_op jit(solution)/shard_map/ppermute | solution.py:845
  131.7 13.0 %collective-permute-start.18 = (bf16[2,192,384]{2,1,0:T(8,128)(2,1)S(1)}, bf16[2,192,384]{2,1,0:T(8,128)(2,1)S(1)}, u32[]{:S(2)}, u32[]{:S(2)}) collective-permute-start(bf16[2,192,384]{2,1,0:T(8,128)(2,1)S(1)} %add_convert_fusion.2), channel_id=1, source_target_pairs={{0,6},{1,7},{2,4},{3,5},{4,2},{5,3},{6,0},{7,1},{8,14},{9,15},{10,... | collective-permute-start | bytes 884744 | tf_op jit(solution)/shard_map/ppermute | solution.py:845
  134.1 16.8 %collective-permute-start.17 = (bf16[2,192,384]{2,1,0:T(8,128)(2,1)S(1)}, bf16[2,192,384]{2,1,0:T(8,128)(2,1)S(1)}, u32[]{:S(2)}, u32[]{:S(2)}) collective-permute-start(bf16[2,192,384]{2,1,0:T(8,128)(2,1)S(1)} %add_convert_fusion.2), channel_id=1, source_target_pairs={{0,4},{1,5},{2,6},{3,7},{4,0},{5,1},{6,2},{7,3},{8,12},{9,13},{10,... | collective-permute-start | bytes 884744 | tf_op jit(solution)/shard_map/ppermute | solution.py:845
  134.3 16.7 %collective-permute-start.16 = (bf16[2,192,384]{2,1,0:T(8,128)(2,1)S(1)}, bf16[2,192,384]{2,1,0:T(8,128)(2,1)S(1)}, u32[]{:S(2)}, u32[]{:S(2)}) collective-permute-start(bf16[2,192,384]{2,1,0:T(8,128)(2,1)S(1)} %add_convert_fusion.2), channel_id=1, source_target_pairs={{0,2},{1,3},{2,0},{3,1},{4,6},{5,7},{6,4},{7,5},{8,10},{9,11},{10,... | collective-permute-start | bytes 884744 | tf_op jit(solution)/shard_map/ppermute | solution.py:845
  140.1 14.5 %collective-permute-start.14 = (bf16[2,112,384]{2,1,0:T(8,128)(2,1)S(1)}, bf16[2,112,384]{2,1,0:T(8,128)(2,1)S(1)}, u32[]{:S(2)}, u32[]{:S(2)}) collective-permute-start(bf16[2,112,384]{2,1,0:T(8,128)(2,1)S(1)} %add_convert_fusion.3), channel_id=1, source_target_pairs={{0,6},{1,7},{2,4},{3,5},{4,2},{5,3},{6,0},{7,1},{8,14},{9,15},{10,... | collective-permute-start | bytes 516104 | tf_op jit(solution)/shard_map/ppermute | solution.py:845
  140.1 16.5 %collective-permute-start.13 = (bf16[2,112,384]{2,1,0:T(8,128)(2,1)S(1)}, bf16[2,112,384]{2,1,0:T(8,128)(2,1)S(1)}, u32[]{:S(2)}, u32[]{:S(2)}) collective-permute-start(bf16[2,112,384]{2,1,0:T(8,128)(2,1)S(1)} %add_convert_fusion.3), channel_id=1, source_target_pairs={{0,4},{1,5},{2,6},{3,7},{4,0},{5,1},{6,2},{7,3},{8,12},{9,13},{10,... | collective-permute-start | bytes 516104 | tf_op jit(solution)/shard_map/ppermute | solution.py:845
  144.6 12.0 %collective-permute-start.12 = (bf16[2,112,384]{2,1,0:T(8,128)(2,1)S(1)}, bf16[2,112,384]{2,1,0:T(8,128)(2,1)S(1)}, u32[]{:S(2)}, u32[]{:S(2)}) collective-permute-start(bf16[2,112,384]{2,1,0:T(8,128)(2,1)S(1)} %add_convert_fusion.3), channel_id=1, source_target_pairs={{0,2},{1,3},{2,0},{3,1},{4,6},{5,7},{6,4},{7,5},{8,10},{9,11},{10,... | collective-permute-start | bytes 516104 | tf_op jit(solution)/shard_map/ppermute | solution.py:845
  151.1 9.4 %collective-permute-start.19 = (bf16[8,192,384]{2,1,0:T(8,128)(2,1)S(1)}, bf16[8,192,384]{2,1,0:T(8,128)(2,1)S(1)}, u32[]{:S(2)}, u32[]{:S(2)}) collective-permute-start(bf16[8,192,384]{2,1,0:T(8,128)(2,1)S(1)} %bitcast.70), channel_id=1, source_target_pairs={{0,1},{1,0},{2,3},{3,2},{4,5},{5,4},{6,7},{7,6},{8,9},{9,8},{10,11... | collective-permute-start | bytes 3538952 | tf_op jit(solution)/shard_map/ppermute | solution.py:845
  156.7 2.2 %collective-permute-start.15 = (bf16[8,112,384]{2,1,0:T(8,128)(2,1)S(1)}, bf16[8,112,384]{2,1,0:T(8,128)(2,1)S(1)}, u32[]{:S(2)}, u32[]{:S(2)}) collective-permute-start(bf16[8,112,384]{2,1,0:T(8,128)(2,1)S(1)} %bitcast.72), channel_id=1, source_target_pairs={{0,1},{1,0},{2,3},{3,2},{4,5},{5,4},{6,7},{7,6},{8,9},{9,8},{10,11... | collective-permute-start | bytes 2064392 | tf_op jit(solution)/shard_map/ppermute | solution.py:845
  (8 other events, 16.2 us)

commit v3 on v2

--- a/solution.py
+++ b/solution.py
@@ -40,6 +40,7 @@
 
 LINES = ("ag", "as", "qb", "vb", "ob", "mg", "ms", "db", "ub")
 CHUNK = 256
+LOG2E = 1.4426950408889634
 WIDE = 256
 
 
@@ -128,10 +129,11 @@
     for f in range(0, ff, CHUNK):
         cols = slice(f, f + CHUNK)
         u = dot(c, w["up"][:, cols]) + ub[:, cols]
-        phi = 0.5 + 0.5 * lax.erf(u * 0.5**0.5)
-        density = jnp.exp(-0.5 * u * u) * 0.3989422804014327
+        t = u * 0.5**0.5
+        phi = 0.5 + 0.5 * lax.erf(t)
+        bell = jnp.exp2(t * t * -LOG2E)
         r["z"][:, cols] = (u * phi).astype(BF16)
-        r["gp"][:, cols] = (phi + u * density).astype(BF16)
+        r["gp"][:, cols] = (phi + u * 0.3989422804014327 * bell).astype(BF16)
     done("z")
     done("gp")
     wait("down")

time: 163 us -> 163 us (level)
  no operation moved by 1% of the time
where the time goes in v3:
time: 163 us
  waiting for transfers between devices  64.8 us (40%)
  Pallas kernels  60.3 us (37%)
  starting transfers between devices  33.5 us (21%)
  local copies, waits for them, and re-layouts  2.11 us (1%)
    pallas_call x8, Pallas kernels, run(): pl.pallas_call(body, out_shape=[jax.ShapeDtypeStruct(s, t) for s, t, _ in...  60.3 us
    ppermute x19, waiting for transfers between devices, swapped(): return lax.ppermute(x, 'dp', [(i, i ^ bits) for i in range(CUTS)])  35.4 us
    ppermute x3, waiting for transfers between devices, advance(): return (lax.ppermute(send, 'section', [(0, 1), (1, 0)]), bufs)  29.4 us
    ppermute x19, starting transfers between devices, swapped(): return lax.ppermute(x, 'dp', [(i, i ^ bits) for i in range(CUTS)])  18.8 us
    ppermute x3, starting transfers between devices, advance(): return (lax.ppermute(send, 'section', [(0, 1), (1, 0)]), bufs)  14.7 us
  transfers between devices with their start and end apart: 22, of which 12 were waited for; matrix products, arithmetic and copies ran while one was open for 1% of the time, Pallas kernels for 9%

profile of v3, /device:TPU:0, one launch (start us, length us, event | category | flops | bytes accessed | tf_op | source)
XLA Modules:
  0.0 162.9 jit_solution(15318670893575144327)
XLA Ops:
  0.7 1.2 copy-done.2
  2.5 74.4 %while.49 = (s32[]{:T(128)}, bf16[512,384]{1,0:T(8,128)(2,1)}, bf16[2,512,384]{2,1,0:T(8,128)(2,1)}, bf16[2,512,384]{2,1,0:T(8,128)(2,1)}, bf16[2,512,384]{2,1,0...) while((s32[]{:T(128)}, bf16[512,384]{1,0:T(8,128)(2,1)}, ...), condition=%wide.region_1.0_spmd, body=%wide.region_0.0_spmd.sunk | while | flops 15000000512 | bytes 31573220 | solution.py:888
  2.5 9.7 %eval_jaxpr.5 = (bf16[512,384]{1,0:T(8,128)(2,1)S(1)}, bf16[2,512,384]{2,1,0:T(8,128)(2,1)}, bf16[2,512,384]{2,1,0:T(8,128)(2,1)}, bf16[2,512,384]{2,1,0:T(8,128...) custom-call(s32[1]{0:T(128)} %bitcast.69.refs_0_, ...), custom_call_target="tpu_custom_call", output_to_operand_aliasing={{1}: (18, {}), {2}: (19, {}), {3}: (20, {}), {4}: (21, {}),... | custom-call | flops 15000000512 | bytes 30000000 | tf_op jit(solution)/shard_map/while/body/eval_jaxpr/pallas_call | solution.py:286
  12.4 11.6 %collective-permute-done = bf16[512,384]{1,0:T(8,128)(2,1)} collective-permute-done((bf16[512,384]{1,0:T(8,128)(2,1)S(1)}, bf16[512,384]{1,0:T(8,128)(2,1)}, u32[]{:S(2)}, u32[]{:S(2)}) %collective-permute-start) | collective-permute-done | bytes 393248 | tf_op jit(solution)/shard_map/while/body/eval_jaxpr/ppermute | solution.py:886
  24.0 9.8 %eval_jaxpr.5 = (bf16[512,384]{1,0:T(8,128)(2,1)S(1)}, bf16[2,512,384]{2,1,0:T(8,128)(2,1)}, bf16[2,512,384]{2,1,0:T(8,128)(2,1)}, bf16[2,512,384]{2,1,0:T(8,128...) custom-call(s32[1]{0:T(128)} %bitcast.69.refs_0_, ...), custom_call_target="tpu_custom_call", output_to_operand_aliasing={{1}: (18, {}), {2}: (19, {}), {3}: (20, {}), {4}: (21, {}),... | custom-call | flops 15000000512 | bytes 30000000 | tf_op jit(solution)/shard_map/while/body/eval_jaxpr/pallas_call | solution.py:286
  33.7 7.1 %collective-permute-start = (bf16[512,384]{1,0:T(8,128)(2,1)S(1)}, bf16[512,384]{1,0:T(8,128)(2,1)}, u32[]{:S(2)}, u32[]{:S(2)}) collective-permute-start(bf16[512,384]{1,0:T(8,128)(2,1)S(1)} %get-tuple-element.1022), channel_id=1, source_target_pairs={{0,16},{16,0},{1,17},{17,1},{2,18},{18,2},{3,19},{19,3},{4,20},{20... | collective-permute-start | bytes 1179656 | tf_op jit(solution)/shard_map/while/body/eval_jaxpr/ppermute | solution.py:886
  40.8 9.3 %collective-permute-done = bf16[512,384]{1,0:T(8,128)(2,1)} collective-permute-done((bf16[512,384]{1,0:T(8,128)(2,1)S(1)}, bf16[512,384]{1,0:T(8,128)(2,1)}, u32[]{:S(2)}, u32[]{:S(2)}) %collective-permute-start) | collective-permute-done | bytes 393248 | tf_op jit(solution)/shard_map/while/body/eval_jaxpr/ppermute | solution.py:886
  50.2 10.8 %eval_jaxpr.5 = (bf16[512,384]{1,0:T(8,128)(2,1)S(1)}, bf16[2,512,384]{2,1,0:T(8,128)(2,1)}, bf16[2,512,384]{2,1,0:T(8,128)(2,1)}, bf16[2,512,384]{2,1,0:T(8,128...) custom-call(s32[1]{0:T(128)} %bitcast.69.refs_0_, ...), custom_call_target="tpu_custom_call", output_to_operand_aliasing={{1}: (18, {}), {2}: (19, {}), {3}: (20, {}), {4}: (21, {}),... | custom-call | flops 15000000512 | bytes 30000000 | tf_op jit(solution)/shard_map/while/body/eval_jaxpr/pallas_call | solution.py:286
  60.9 7.5 %collective-permute-start = (bf16[512,384]{1,0:T(8,128)(2,1)S(1)}, bf16[512,384]{1,0:T(8,128)(2,1)}, u32[]{:S(2)}, u32[]{:S(2)}) collective-permute-start(bf16[512,384]{1,0:T(8,128)(2,1)S(1)} %get-tuple-element.1022), channel_id=1, source_target_pairs={{0,16},{16,0},{1,17},{17,1},{2,18},{18,2},{3,19},{19,3},{4,20},{20... | collective-permute-start | bytes 1179656 | tf_op jit(solution)/shard_map/while/body/eval_jaxpr/ppermute | solution.py:886
  68.5 8.4 %collective-permute-done = bf16[512,384]{1,0:T(8,128)(2,1)} collective-permute-done((bf16[512,384]{1,0:T(8,128)(2,1)S(1)}, bf16[512,384]{1,0:T(8,128)(2,1)}, u32[]{:S(2)}, u32[]{:S(2)}) %collective-permute-start) | collective-permute-done | bytes 393248 | tf_op jit(solution)/shard_map/while/body/eval_jaxpr/ppermute | solution.py:886
  76.9 13.5 %shard_map.272 = (bf16[8,192,384]{2,1,0:T(8,128)(2,1)S(1)}, bf16[8,192,384]{2,1,0:T(8,128)(2,1)}, f32[5,8,384]{2,1,0:T(8,128)S(1)}, bf16[2,512,384]{2,1,0:T(8,12...) custom-call(bf16[1,384]{1,0:T(2,128)(2,1)} %get-tuple-element.1196, ...), custom_call_target="tpu_custom_call", output_to_operand_aliasing={{3}: (10, {}), {4}: (11, {})} | custom-call | flops 12000000000 | bytes 24000000 | tf_op jit(solution)/shard_map/pallas_call | solution.py:286
  90.5 3.0 %collective-permute-done.1 = bf16[8,192,384]{2,1,0:T(8,128)(2,1)S(1)} collective-permute-done((bf16[8,192,384]{2,1,0:T(8,128)(2,1)}, bf16[8,192,384]{2,1,0:T(8,128)(2,1)S(1)}, u32[]{:S(2)}, u32[]{:S(2)}) %collective-permute-start.1) | collective-permute-done | bytes 1179680 | tf_op jit(solution)/shard_map/ppermute | solution.py:847
  94.0 2.0 %collective-permute-start.4 = (bf16[2,192,384]{2,1,0:T(8,128)(2,1)S(1)}, bf16[2,192,384]{2,1,0:T(8,128)(2,1)S(1)}, u32[]{:S(2)}, u32[]{:S(2)}) collective-permute-start(bf16[2,192,384]{2,1,0:T(8,128)(2,1)S(1)} %get-tuple-element.778), channel_id=1, source_target_pairs={{0,6},{1,7},{2,4},{3,5},{4,2},{5,3},{6,0},{7,1},{8,14},{9,15},{10,... | collective-permute-start | bytes 884744 | tf_op jit(solution)/shard_map/ppermute | solution.py:847
  96.3 1.2 collective-permute-start.2
  97.6 12.3 %shard_map.273 = (bf16[8,112,384]{2,1,0:T(8,128)(2,1)S(1)}, bf16[8,112,384]{2,1,0:T(8,128)(2,1)S(1)}, bf16[2,512,384]{2,1,0:T(8,128)(2,1)S(1)}) custom-call(bf16[1,384]{1,0:T(2,128)(2,1)S(1)} %copy-done.10, bf16[2,1,512,384]{3,2,1,0:T(8,128)(2,1)S(1)} %copy-done.5, bf16[1,384,384]{2,1,0:T(8,128)(2,1)S(1)} %copy-done.6, ...), custom_call_target="tpu_custom_call", output_to_operand_aliasing={{2}: (5, {})} | custom-call | flops 12000000000 | bytes 24000000 | tf_op jit(solution)/shard_map/pallas_call | solution.py:286
  110.8 2.2 %collective-permute-start.7 = (bf16[2,192,384]{2,1,0:T(8,128)(2,1)S(1)}, bf16[2,192,384]{2,1,0:T(8,128)(2,1)S(1)}, u32[]{:S(2)}, u32[]{:S(2)}) collective-permute-start(bf16[2,192,384]{2,1,0:T(8,128)(2,1)S(1)} %fusion.2), channel_id=1, source_target_pairs={{0,8},{1,9},{2,10},{3,11},{4,12},{5,13},{6,14},{7,15},{8,0},{9,1},... | collective-permute-start | bytes 884744 | tf_op jit(solution)/shard_map/ppermute | solution.py:847
  113.4 2.6 %collective-permute-start.10 = (bf16[2,112,384]{2,1,0:T(8,128)(2,1)S(1)}, bf16[2,112,384]{2,1,0:T(8,128)(2,1)S(1)}, u32[]{:S(2)}, u32[]{:S(2)}) collective-permute-start(bf16[2,112,384]{2,1,0:T(8,128)(2,1)S(1)} %get-tuple-element.781), channel_id=1, source_target_pairs={{0,6},{1,7},{2,4},{3,5},{4,2},{5,3},{6,0},{7,1},{8,14},{9,15},{10,... | collective-permute-start | bytes 516104 | tf_op jit(solution)/shard_map/ppermute | solution.py:847
  116.9 7.3 %collective-permute-done.10 = bf16[2,112,384]{2,1,0:T(8,128)(2,1)S(1)} collective-permute-done((bf16[2,112,384]{2,1,0:T(8,128)(2,1)S(1)}, bf16[2,112,384]{2,1,0:T(8,128)(2,1)S(1)}, u32[]{:S(2)}, u32[]{:S(2)}) %collective-permute-start.10) | collective-permute-done | bytes 172064 | tf_op jit(solution)/shard_map/ppermute | solution.py:847
  124.2 5.5 %collective-permute-done.9 = bf16[2,112,384]{2,1,0:T(8,128)(2,1)S(1)} collective-permute-done((bf16[2,112,384]{2,1,0:T(8,128)(2,1)S(1)}, bf16[2,112,384]{2,1,0:T(8,128)(2,1)S(1)}, u32[]{:S(2)}, u32[]{:S(2)}) %collective-permute-start.9) | collective-permute-done | bytes 172064 | tf_op jit(solution)/shard_map/ppermute | solution.py:847
  129.8 1.6 collective-permute-start.11
  131.4 2.4 %collective-permute-start.18 = (bf16[2,192,384]{2,1,0:T(8,128)(2,1)S(1)}, bf16[2,192,384]{2,1,0:T(8,128)(2,1)S(1)}, u32[]{:S(2)}, u32[]{:S(2)}) collective-permute-start(bf16[2,192,384]{2,1,0:T(8,128)(2,1)S(1)} %add_convert_fusion.2), channel_id=1, source_target_pairs={{0,6},{1,7},{2,4},{3,5},{4,2},{5,3},{6,0},{7,1},{8,14},{9,15},{10,... | collective-permute-start | bytes 884744 | tf_op jit(solution)/shard_map/ppermute | solution.py:847
  134.1 1.4 collective-permute-start.16
  135.5 4.2 %collective-permute-done.11 = bf16[2,112,384]{2,1,0:T(8,128)(2,1)S(1)} collective-permute-done((bf16[2,112,384]{2,1,0:T(8,128)(2,1)S(1)}, bf16[2,112,384]{2,1,0:T(8,128)(2,1)S(1)}, u32[]{:S(2)}, u32[]{:S(2)}) %collective-permute-start.11) | collective-permute-done | bytes 172064 | tf_op jit(solution)/shard_map/ppermute | solution.py:847
  139.8 1.5 collective-permute-start.13
  141.4 3.0 %collective-permute-done.18 = bf16[2,192,384]{2,1,0:T(8,128)(2,1)S(1)} collective-permute-done((bf16[2,192,384]{2,1,0:T(8,128)(2,1)S(1)}, bf16[2,192,384]{2,1,0:T(8,128)(2,1)S(1)}, u32[]{:S(2)}, u32[]{:S(2)}) %collective-permute-start.18) | collective-permute-done | bytes 294944 | tf_op jit(solution)/shard_map/ppermute | solution.py:847
  144.3 1.5 collective-permute-start.12
  145.8 4.9 %collective-permute-done.17 = bf16[2,192,384]{2,1,0:T(8,128)(2,1)S(1)} collective-permute-done((bf16[2,192,384]{2,1,0:T(8,128)(2,1)S(1)}, bf16[2,192,384]{2,1,0:T(8,128)(2,1)S(1)}, u32[]{:S(2)}, u32[]{:S(2)}) %collective-permute-start.17) | collective-permute-done | bytes 294944 | tf_op jit(solution)/shard_map/ppermute | solution.py:847
  150.9 3.4 %collective-permute-done.14 = bf16[2,112,384]{2,1,0:T(8,128)(2,1)S(1)} collective-permute-done((bf16[2,112,384]{2,1,0:T(8,128)(2,1)S(1)}, bf16[2,112,384]{2,1,0:T(8,128)(2,1)S(1)}, u32[]{:S(2)}, u32[]{:S(2)}) %collective-permute-start.14) | collective-permute-done | bytes 172064 | tf_op jit(solution)/shard_map/ppermute | solution.py:847
  154.3 2.0 %collective-permute-done.13 = bf16[2,112,384]{2,1,0:T(8,128)(2,1)S(1)} collective-permute-done((bf16[2,112,384]{2,1,0:T(8,128)(2,1)S(1)}, bf16[2,112,384]{2,1,0:T(8,128)(2,1)S(1)}, u32[]{:S(2)}, u32[]{:S(2)}) %collective-permute-start.13) | collective-permute-done | bytes 172064 | tf_op jit(solution)/shard_map/ppermute | solution.py:847
  156.5 2.1 %collective-permute-done.15.other_ref = bf16[8,112,384]{2,1,0:T(8,128)(2,1)S(1)} collective-permute-done((bf16[8,112,384]{2,1,0:T(8,128)(2,1)S(1)}, bf16[8,112,384]{2,1,0:T(8,128)(2,1)S(1)}, u32[]{:S(2)}, u32[]{:S(2)}) %collective-permute-start.15) | collective-permute-done | bytes 688160 | tf_op jit(solution)/shard_map/ppermute | solution.py:847
  158.6 1.6 shard_map.274
  160.2 2.7 %shard_map.275 = (f32[1,1536,384]{2,1,0:T(8,128)}, f32[1,384,1536]{2,1,0:T(8,128)}, f32[8,128]{1,0:T(8,128)}) custom-call(bf16[8,192,384]{2,1,0:T(8,128)(2,1)S(1)} %bitcast.71, bf16[8,192,384]{2,1,0:T(8,128)(2,1)S(1)} %collective-permute-done.19.other_ref), custom_call_target="tpu_custom_call" | custom-call | flops 4000000000 | bytes 8000000 | tf_op jit(solution)/shard_map/pallas_call | solution.py:286
  (69 shorter events, 4.6 us)
Async XLA Ops:
  12.3 11.7 %collective-permute-start = (bf16[512,384]{1,0:T(8,128)(2,1)S(1)}, bf16[512,384]{1,0:T(8,128)(2,1)}, u32[]{:S(2)}, u32[]{:S(2)}) collective-permute-start(bf16[512,384]{1,0:T(8,128)(2,1)S(1)} %get-tuple-element.1022), channel_id=1, source_target_pairs={{0,16},{16,0},{1,17},{17,1},{2,18},{18,2},{3,19},{19,3},{4,20},{20... | collective-permute-start | bytes 1179656 | tf_op jit(solution)/shard_map/while/body/eval_jaxpr/ppermute | solution.py:886
  33.7 16.4 %collective-permute-start = (bf16[512,384]{1,0:T(8,128)(2,1)S(1)}, bf16[512,384]{1,0:T(8,128)(2,1)}, u32[]{:S(2)}, u32[]{:S(2)}) collective-permute-start(bf16[512,384]{1,0:T(8,128)(2,1)S(1)} %get-tuple-element.1022), channel_id=1, source_target_pairs={{0,16},{16,0},{1,17},{17,1},{2,18},{18,2},{3,19},{19,3},{4,20},{20... | collective-permute-start | bytes 1179656 | tf_op jit(solution)/shard_map/while/body/eval_jaxpr/ppermute | solution.py:886
  60.9 16.0 %collective-permute-start = (bf16[512,384]{1,0:T(8,128)(2,1)S(1)}, bf16[512,384]{1,0:T(8,128)(2,1)}, u32[]{:S(2)}, u32[]{:S(2)}) collective-permute-start(bf16[512,384]{1,0:T(8,128)(2,1)S(1)} %get-tuple-element.1022), channel_id=1, source_target_pairs={{0,16},{16,0},{1,17},{17,1},{2,18},{18,2},{3,19},{19,3},{4,20},{20... | collective-permute-start | bytes 1179656 | tf_op jit(solution)/shard_map/while/body/eval_jaxpr/ppermute | solution.py:886
  76.9 20.6 %copy-start.12 = (f32[2,6,64,512]{3,2,1,0:T(8,128)S(1)}, f32[2,6,64,512]{3,2,1,0:T(8,128)}, u32[]{:S(2)}) copy-start(f32[2,6,64,512]{3,2,1,0:T(8,128)} %get-tuple-element.651.refs_8_) | copy-start | bytes 4718596
  76.9 20.6 %copy-start.15 = (bf16[2,512,384]{2,1,0:T(8,128)(2,1)S(1)}, bf16[2,512,384]{2,1,0:T(8,128)(2,1)}, u32[]{:S(2)}) copy-start(bf16[2,512,384]{2,1,0:T(8,128)(2,1)} %get-tuple-element.650.refs_7_) | copy-start | bytes 2359300
  90.4 3.1 %collective-permute-start.1 = (bf16[8,192,384]{2,1,0:T(8,128)(2,1)}, bf16[8,192,384]{2,1,0:T(8,128)(2,1)S(1)}, u32[]{:S(2)}, u32[]{:S(2)}) collective-permute-start(bf16[8,192,384]{2,1,0:T(8,128)(2,1)} %get-tuple-element.645), channel_id=1, source_target_pairs={{0,1},{1,0},{2,3},{3,2},{4,5},{5,4},{6,7},{7,6},{8,9},{9,8},{10,11... | collective-permute-start | bytes 3538952 | tf_op jit(solution)/shard_map/ppermute | solution.py:847
  93.5 4.0 %copy-start.6 = (bf16[1,384,384]{2,1,0:T(8,128)(2,1)S(1)}, bf16[1,384,384]{2,1,0:T(8,128)(2,1)}, u32[]{:S(2)}) copy-start(bf16[1,384,384]{2,1,0:T(8,128)(2,1)} %get-tuple-element.1195) | copy-start | bytes 884740
  93.5 4.0 %copy-start.11 = (bf16[2,3,6,64,512]{4,3,2,1,0:T(8,128)(2,1)S(1)}, bf16[2,3,6,64,512]{4,3,2,1,0:T(8,128)(2,1)}, u32[]{:S(2)}) copy-start(bf16[2,3,6,64,512]{4,3,2,1,0:T(8,128)(2,1)} %get-tuple-element.653.refs_10_) | copy-start | bytes 7077892
  93.5 4.0 %copy-start.13 = (bf16[2,512,384]{2,1,0:T(8,128)(2,1)S(1)}, bf16[2,512,384]{2,1,0:T(8,128)(2,1)}, u32[]{:S(2)}) copy-start(bf16[2,512,384]{2,1,0:T(8,128)(2,1)} %get-tuple-element.648.refs_5_) | copy-start | bytes 2359300
  93.8 3.7 %copy-start.3 = (bf16[1,384,1152]{2,1,0:T(8,128)(2,1)S(1)}, bf16[1,384,1152]{2,1,0:T(8,128)(2,1)}, u32[]{:S(2)}) copy-start(bf16[1,384,1152]{2,1,0:T(8,128)(2,1)} %get-tuple-element.1193) | copy-start | bytes 2654212
  93.9 3.7 %copy-start.5 = (bf16[2,1,512,384]{3,2,1,0:T(8,128)(2,1)S(1)}, bf16[2,1,512,384]{3,2,1,0:T(8,128)(2,1)}, u32[]{:S(2)}) copy-start(bf16[2,1,512,384]{3,2,1,0:T(8,128)(2,1)} %get-tuple-element.1194) | copy-start | bytes 2359300
  93.9 3.7 %copy-start.10 = (bf16[1,384]{1,0:T(2,128)(2,1)S(1)}, bf16[1,384]{1,0:T(2,128)(2,1)}, u32[]{:S(2)}) copy-start(bf16[1,384]{1,0:T(2,128)(2,1)} %get-tuple-element.1197) | copy-start | bytes 2308
  93.9 3.7 %copy-start.16 = (f32[2,6,1,512]{3,2,1,0:T(1,128)S(1)}, f32[2,6,1,512]{3,2,1,0:T(1,128)}, u32[]{:S(2)}) copy-start(f32[2,6,1,512]{3,2,1,0:T(1,128)} %get-tuple-element.655.refs_12_) | copy-start | bytes 73732
  93.9 3.7 %copy-start.17 = (f32[2,8,384]{2,1,0:T(8,128)S(1)}, f32[2,8,384]{2,1,0:T(8,128)}, u32[]{:S(2)}) copy-start(f32[2,8,384]{2,1,0:T(8,128)} %get-tuple-element.654.refs_11_) | copy-start | bytes 73732
  94.0 16.6 %collective-permute-start.4 = (bf16[2,192,384]{2,1,0:T(8,128)(2,1)S(1)}, bf16[2,192,384]{2,1,0:T(8,128)(2,1)S(1)}, u32[]{:S(2)}, u32[]{:S(2)}) collective-permute-start(bf16[2,192,384]{2,1,0:T(8,128)(2,1)S(1)} %get-tuple-element.778), channel_id=1, source_target_pairs={{0,6},{1,7},{2,4},{3,5},{4,2},{5,3},{6,0},{7,1},{8,14},{9,15},{10,... | collective-permute-start | bytes 884744 | tf_op jit(solution)/shard_map/ppermute | solution.py:847
  96.0 14.6 %collective-permute-start.3 = (bf16[2,192,384]{2,1,0:T(8,128)(2,1)S(1)}, bf16[2,192,384]{2,1,0:T(8,128)(2,1)S(1)}, u32[]{:S(2)}, u32[]{:S(2)}) collective-permute-start(bf16[2,192,384]{2,1,0:T(8,128)(2,1)S(1)} %get-tuple-element.779), channel_id=1, source_target_pairs={{0,4},{1,5},{2,6},{3,7},{4,0},{5,1},{6,2},{7,3},{8,12},{9,13},{10,... | collective-permute-start | bytes 884744 | tf_op jit(solution)/shard_map/ppermute | solution.py:847
  96.3 14.3 %collective-permute-start.2 = (bf16[2,192,384]{2,1,0:T(8,128)(2,1)S(1)}, bf16[2,192,384]{2,1,0:T(8,128)(2,1)S(1)}, u32[]{:S(2)}, u32[]{:S(2)}) collective-permute-start(bf16[2,192,384]{2,1,0:T(8,128)(2,1)S(1)} %get-tuple-element.780), channel_id=1, source_target_pairs={{0,2},{1,3},{2,0},{3,1},{4,6},{5,7},{6,4},{7,5},{8,10},{9,11},{10,... | collective-permute-start | bytes 884744 | tf_op jit(solution)/shard_map/ppermute | solution.py:847
  110.0 3.0 %collective-permute-start.5 = (bf16[4,112,384]{2,1,0:T(8,128)(2,1)S(1)}, bf16[4,112,384]{2,1,0:T(8,128)(2,1)S(1)}, u32[]{:S(2)}, u32[]{:S(2)}) collective-permute-start(bf16[4,112,384]{2,1,0:T(8,128)(2,1)S(1)} %get-tuple-element.784), channel_id=1, source_target_pairs={{0,1},{1,0},{2,3},{3,2},{4,5},{5,4},{6,7},{7,6},{8,9},{9,8},{10,11... | collective-permute-start | bytes 1032200 | tf_op jit(solution)/shard_map/ppermute | solution.py:847
  110.1 2.9 %collective-permute-start.6 = (bf16[4,112,384]{2,1,0:T(8,128)(2,1)S(1)}, bf16[4,112,384]{2,1,0:T(8,128)(2,1)S(1)}, u32[]{:S(2)}, u32[]{:S(2)}) collective-permute-start(bf16[4,112,384]{2,1,0:T(8,128)(2,1)S(1)} %get-tuple-element.785), channel_id=1, source_target_pairs={{0,1},{1,0},{2,3},{3,2},{4,5},{5,4},{6,7},{7,6},{8,9},{9,8},{10,11... | collective-permute-start | bytes 1032200 | tf_op jit(solution)/shard_map/ppermute | solution.py:847
  110.8 18.9 %collective-permute-start.7 = (bf16[2,192,384]{2,1,0:T(8,128)(2,1)S(1)}, bf16[2,192,384]{2,1,0:T(8,128)(2,1)S(1)}, u32[]{:S(2)}, u32[]{:S(2)}) collective-permute-start(bf16[2,192,384]{2,1,0:T(8,128)(2,1)S(1)} %fusion.2), channel_id=1, source_target_pairs={{0,8},{1,9},{2,10},{3,11},{4,12},{5,13},{6,14},{7,15},{8,0},{9,1},... | collective-permute-start | bytes 884744 | tf_op jit(solution)/shard_map/ppermute | solution.py:847
  113.4 10.8 %collective-permute-start.10 = (bf16[2,112,384]{2,1,0:T(8,128)(2,1)S(1)}, bf16[2,112,384]{2,1,0:T(8,128)(2,1)S(1)}, u32[]{:S(2)}, u32[]{:S(2)}) collective-permute-start(bf16[2,112,384]{2,1,0:T(8,128)(2,1)S(1)} %get-tuple-element.781), channel_id=1, source_target_pairs={{0,6},{1,7},{2,4},{3,5},{4,2},{5,3},{6,0},{7,1},{8,14},{9,15},{10,... | collective-permute-start | bytes 516104 | tf_op jit(solution)/shard_map/ppermute | solution.py:847
  115.9 13.7 %collective-permute-start.9 = (bf16[2,112,384]{2,1,0:T(8,128)(2,1)S(1)}, bf16[2,112,384]{2,1,0:T(8,128)(2,1)S(1)}, u32[]{:S(2)}, u32[]{:S(2)}) collective-permute-start(bf16[2,112,384]{2,1,0:T(8,128)(2,1)S(1)} %get-tuple-element.782), channel_id=1, source_target_pairs={{0,4},{1,5},{2,6},{3,7},{4,0},{5,1},{6,2},{7,3},{8,12},{9,13},{10,... | collective-permute-start | bytes 516104 | tf_op jit(solution)/shard_map/ppermute | solution.py:847
  116.3 13.4 %collective-permute-start.8 = (bf16[2,112,384]{2,1,0:T(8,128)(2,1)S(1)}, bf16[2,112,384]{2,1,0:T(8,128)(2,1)S(1)}, u32[]{:S(2)}, u32[]{:S(2)}) collective-permute-start(bf16[2,112,384]{2,1,0:T(8,128)(2,1)S(1)} %get-tuple-element.783), channel_id=1, source_target_pairs={{0,2},{1,3},{2,0},{3,1},{4,6},{5,7},{6,4},{7,5},{8,10},{9,11},{10,... | collective-permute-start | bytes 516104 | tf_op jit(solution)/shard_map/ppermute | solution.py:847
  129.8 10.0 %collective-permute-start.11 = (bf16[2,112,384]{2,1,0:T(8,128)(2,1)S(1)}, bf16[2,112,384]{2,1,0:T(8,128)(2,1)S(1)}, u32[]{:S(2)}, u32[]{:S(2)}) collective-permute-start(bf16[2,112,384]{2,1,0:T(8,128)(2,1)S(1)} %fusion.5), channel_id=1, source_target_pairs={{0,8},{1,9},{2,10},{3,11},{4,12},{5,13},{6,14},{7,15},{8,0},{9,1},... | collective-permute-start | bytes 516104 | tf_op jit(solution)/shard_map/ppermute | solution.py:847
  131.4 12.9 %collective-permute-start.18 = (bf16[2,192,384]{2,1,0:T(8,128)(2,1)S(1)}, bf16[2,192,384]{2,1,0:T(8,128)(2,1)S(1)}, u32[]{:S(2)}, u32[]{:S(2)}) collective-permute-start(bf16[2,192,384]{2,1,0:T(8,128)(2,1)S(1)} %add_convert_fusion.2), channel_id=1, source_target_pairs={{0,6},{1,7},{2,4},{3,5},{4,2},{5,3},{6,0},{7,1},{8,14},{9,15},{10,... | collective-permute-start | bytes 884744 | tf_op jit(solution)/shard_map/ppermute | solution.py:847
  133.8 16.8 %collective-permute-start.17 = (bf16[2,192,384]{2,1,0:T(8,128)(2,1)S(1)}, bf16[2,192,384]{2,1,0:T(8,128)(2,1)S(1)}, u32[]{:S(2)}, u32[]{:S(2)}) collective-permute-start(bf16[2,192,384]{2,1,0:T(8,128)(2,1)S(1)} %add_convert_fusion.2), channel_id=1, source_target_pairs={{0,4},{1,5},{2,6},{3,7},{4,0},{5,1},{6,2},{7,3},{8,12},{9,13},{10,... | collective-permute-start | bytes 884744 | tf_op jit(solution)/shard_map/ppermute | solution.py:847
  134.1 16.6 %collective-permute-start.16 = (bf16[2,192,384]{2,1,0:T(8,128)(2,1)S(1)}, bf16[2,192,384]{2,1,0:T(8,128)(2,1)S(1)}, u32[]{:S(2)}, u32[]{:S(2)}) collective-permute-start(bf16[2,192,384]{2,1,0:T(8,128)(2,1)S(1)} %add_convert_fusion.2), channel_id=1, source_target_pairs={{0,2},{1,3},{2,0},{3,1},{4,6},{5,7},{6,4},{7,5},{8,10},{9,11},{10,... | collective-permute-start | bytes 884744 | tf_op jit(solution)/shard_map/ppermute | solution.py:847
  139.8 14.5 %collective-permute-start.14 = (bf16[2,112,384]{2,1,0:T(8,128)(2,1)S(1)}, bf16[2,112,384]{2,1,0:T(8,128)(2,1)S(1)}, u32[]{:S(2)}, u32[]{:S(2)}) collective-permute-start(bf16[2,112,384]{2,1,0:T(8,128)(2,1)S(1)} %add_convert_fusion.3), channel_id=1, source_target_pairs={{0,6},{1,7},{2,4},{3,5},{4,2},{5,3},{6,0},{7,1},{8,14},{9,15},{10,... | collective-permute-start | bytes 516104 | tf_op jit(solution)/shard_map/ppermute | solution.py:847
  139.8 16.5 %collective-permute-start.13 = (bf16[2,112,384]{2,1,0:T(8,128)(2,1)S(1)}, bf16[2,112,384]{2,1,0:T(8,128)(2,1)S(1)}, u32[]{:S(2)}, u32[]{:S(2)}) collective-permute-start(bf16[2,112,384]{2,1,0:T(8,128)(2,1)S(1)} %add_convert_fusion.3), channel_id=1, source_target_pairs={{0,4},{1,5},{2,6},{3,7},{4,0},{5,1},{6,2},{7,3},{8,12},{9,13},{10,... | collective-permute-start | bytes 516104 | tf_op jit(solution)/shard_map/ppermute | solution.py:847
  144.3 12.0 %collective-permute-start.12 = (bf16[2,112,384]{2,1,0:T(8,128)(2,1)S(1)}, bf16[2,112,384]{2,1,0:T(8,128)(2,1)S(1)}, u32[]{:S(2)}, u32[]{:S(2)}) collective-permute-start(bf16[2,112,384]{2,1,0:T(8,128)(2,1)S(1)} %add_convert_fusion.3), channel_id=1, source_target_pairs={{0,2},{1,3},{2,0},{3,1},{4,6},{5,7},{6,4},{7,5},{8,10},{9,11},{10,... | collective-permute-start | bytes 516104 | tf_op jit(solution)/shard_map/ppermute | solution.py:847
  150.8 9.4 %collective-permute-start.19 = (bf16[8,192,384]{2,1,0:T(8,128)(2,1)S(1)}, bf16[8,192,384]{2,1,0:T(8,128)(2,1)S(1)}, u32[]{:S(2)}, u32[]{:S(2)}) collective-permute-start(bf16[8,192,384]{2,1,0:T(8,128)(2,1)S(1)} %bitcast.70), channel_id=1, source_target_pairs={{0,1},{1,0},{2,3},{3,2},{4,5},{5,4},{6,7},{7,6},{8,9},{9,8},{10,11... | collective-permute-start | bytes 3538952 | tf_op jit(solution)/shard_map/ppermute | solution.py:847
  156.4 2.2 %collective-permute-start.15 = (bf16[8,112,384]{2,1,0:T(8,128)(2,1)S(1)}, bf16[8,112,384]{2,1,0:T(8,128)(2,1)S(1)}, u32[]{:S(2)}, u32[]{:S(2)}) collective-permute-start(bf16[8,112,384]{2,1,0:T(8,128)(2,1)S(1)} %bitcast.72), channel_id=1, source_target_pairs={{0,1},{1,0},{2,3},{3,2},{4,5},{5,4},{6,7},{7,6},{8,9},{9,8},{10,11... | collective-permute-start | bytes 2064392 | tf_op jit(solution)/shard_map/ppermute | solution.py:847
  (8 other events, 16.2 us)
